TPU v7x, 32 devices: a whole 2x2x4 slice. The times are simulated.
32 devices in a mesh: dp: 2 (over y), fsdp: 16 (over z, x, core).
Axes of the slice: x: 2, y: 2, z: 4, core: 2. Of those that a mesh axis runs over, the one named last changes fastest.
Arguments:
- frames: bfloat16 [16, 2048, 1024], P('fsdp', 'dp'), may hold values from -6 to 6
- skip_in: bfloat16 [16, 2048, 1024], P('fsdp', 'dp'), may hold values from -6 to 6
- cond_in: bfloat16 [16, 2048, 1024], P('fsdp', 'dp'), may hold values from -6 to 6
- lengths: int32 [16, 8], P('fsdp'), may hold values from 1 to 1536, 2048 in all within a row
- drop_mask: int32 [16, 8], P('fsdp'), may hold values 0 or 1
- time_index: int32 [16, 8], P('fsdp'), may hold values from 0 to 999
- w_skip: bfloat16 [2048, 1024], P('dp', 'fsdp'), may hold values from -0.125 to 0.125
- w_qkv: bfloat16 [1024, 3072], P('dp', 'fsdp'), may hold values from -0.1875 to 0.1875
- w_out: bfloat16 [1024, 1024], P('dp', 'fsdp'), may hold values from -0.75 to 0.75
- w_up: bfloat16 [1024, 4096], P('dp', 'fsdp'), may hold values from -0.1875 to 0.1875
- w_down: bfloat16 [4096, 1024], P('dp', 'fsdp'), may hold values from -0.09375 to 0.09375
- w_mod: bfloat16 [1024, 4096], P('dp', 'fsdp'), may hold values from -0.1875 to 0.1875
- d_out: bfloat16 [16, 2048, 1024], P('fsdp', 'dp'), may hold values from -6 to 6
Outputs:
- output: bfloat16 [16, 2048, 1024], P('fsdp', 'dp')
- grad_frames: float32 [16, 2048, 1024], P('fsdp', 'dp')
- grad_skip: float32 [16, 2048, 1024], P('fsdp', 'dp')
- grad_w_skip: float32 [2048, 1024], P('dp', 'fsdp')
- grad_w_qkv: float32 [1024, 3072], P('dp', 'fsdp')
- grad_w_out: float32 [1024, 1024], P('dp', 'fsdp')
- grad_w_up: float32 [1024, 4096], P('dp', 'fsdp')
- grad_w_down: float32 [4096, 1024], P('dp', 'fsdp')
- grad_w_mod: float32 [1024, 4096], P('dp', 'fsdp')
Inputs may be any that keep to these rules, and one draw needn't show every extreme that they name: `lengths`: each row sums to 2048; the largest length of every row is 1536.
All inputs are finite; a program needn't handle non-finite values. No bound on the sum of `drop_mask` on one device may be relied on, other than what follows from the above.
Results may differ from a plain program's by a relative error of at most 0.02.
Values may be sent and summed in bfloat16 or wider, within the bound.
No kernel may reach another device: no remote copies, remote signals or barrier semaphores. Data moves between devices by JAX's collectives and lax.ppermute only.
A program may use at most 384 MiB of HBM per device.

v0:
```python
from functools import partial
import math

import jax
import jax.numpy as jnp
from jax import lax
from jax.experimental import pallas as pl
from jax.experimental.pallas import tpu as pltpu
from jax.sharding import PartitionSpec as P

HD = 64
LANES = 128
STEPS = 1000
LONG_PART = 0.75
NEG = -1e30
GELU_C = math.sqrt(2.0 / math.pi)
VMEM_MIB = 60

bf16 = jnp.bfloat16
f32 = jnp.float32
highest = lax.Precision.HIGHEST
epsilon = 1e-06


def dot(a, b, ca, cb):
    return lax.dot_general(a, b, (((ca,), (cb,)), ((), ())), preferred_element_type=f32)


def params(mib=VMEM_MIB):
    return pltpu.CompilerParams(vmem_limit_bytes=mib * 2**20)


def cost(flops, nbytes, trans=0):
    return pl.CostEstimate(flops=int(flops), bytes_accessed=int(nbytes), transcendentals=int(trans))


def shape(dims, dtype):
    return jax.ShapeDtypeStruct(dims, dtype)


class Net:
    def __init__(self, mesh):
        self.nd = mesh.shape["dp"]
        self.nf = mesh.shape["fsdp"]
        self.fb = self.nf.bit_length() - 1
        self.db = self.nd.bit_length() - 1
        common = [("fsdp", 1 << b) for b in range(self.fb - 1, 1, -1)]
        common += [("dp", 1 << b) for b in range(self.db - 1, 0, -1)]
        x, y, core = ("fsdp", 2), ("dp", 1), ("fsdp", 1)
        self.orders = (common + [x, y, core], common + [y, x, core])
        self.regroup = self.nd == 2
        self.attn_axis = "core" if self.regroup else "dp"
        self.na = 2 if self.regroup else self.nd

    def swap(self, x, bit):
        axis, mask = bit
        size = self.nf if axis == "fsdp" else self.nd
        return lax.ppermute(x, axis, [(i, i ^ mask) for i in range(size)])

    def attn_swap(self, x, r):
        return self.swap(x, ("fsdp", r) if self.regroup else ("dp", r))

    def attn_index(self):
        return lax.axis_index("fsdp") & 1 if self.regroup else lax.axis_index("dp")

    def group_of(self, f, y):
        return (f & ~1) | y if self.regroup else f

    def trade(self, x):
        if not self.regroup:
            return x
        perm = []
        for y in range(self.nd):
            for f in range(self.nf):
                c = f & 1
                if c != y:
                    perm.append((y * self.nf + f, c * self.nf + (f & ~1 | y)))
        return lax.ppermute(x, ("dp", "fsdp"), perm)

    def traded(self, x, got):
        if not self.regroup:
            return x
        return jnp.where(lax.axis_index("fsdp") & 1 != lax.axis_index("dp"), got, x)

    def offsets(self, order):
        out = []
        for s in range(self.nd * self.nf):
            d = f = 0
            for j, (axis, mask) in enumerate(order):
                if s >> j & 1:
                    if axis == "dp":
                        d ^= mask
                    else:
                        f ^= mask
            out.append((d, f))
        return out

    def halves(self, x, bit, axes):
        axis, mask = bit
        b = jnp.where(lax.axis_index(axis) & mask != 0, 1, 0)
        if axis == "fsdp":
            at = axes.index(mask)
            keep = lax.dynamic_index_in_dim(x, b, at, keepdims=False)
            send = lax.dynamic_index_in_dim(x, 1 - b, at, keepdims=False)
            return keep, send, axes[:at] + axes[at + 1 :]
        half = x.shape[-1] // 2
        keep = lax.dynamic_slice_in_dim(x, b * half, half, x.ndim - 1)
        send = lax.dynamic_slice_in_dim(x, (1 - b) * half, half, x.ndim - 1)
        return keep, send, axes


def plus(*xs):
    total = xs[0].astype(f32)
    for x in xs[1:]:
        total = total + x.astype(f32)
    return total.astype(bf16)


def tie(*groups):
    flat = lax.optimization_barrier(tuple(x for g in groups for x in g))
    out, at = [], 0
    for g in groups:
        out.append(list(flat[at : at + len(g)]))
        at += len(g)
    return out


class Gather:
    def __init__(self, net, block, split):
        self.net = net
        rows = block.shape[0]
        cuts = [(0, split, net.orders[0]), (split, rows, net.orders[1])]
        cuts = [c for c in cuts if c[0] < c[1]]
        self.bounds = [c[:2] for c in cuts]
        self.orders = [c[2] for c in cuts]
        self.x = [block[None]]
        self.done = 0
        self.common = len(net.orders[0]) - 3

    def send(self):
        if self.done == self.common:
            self.x = [self.x[0][:, a:b] for a, b in self.bounds]
        self.raw = [self.net.swap(x, o[self.done]) for x, o in zip(self.x, self.orders)]

    def join(self):
        if self.done == self.common + 1:
            self.far = self.raw
        else:
            self.x = [jnp.concatenate([x, r], axis=0) for x, r in zip(self.x, self.raw)]
        self.done += 1

    def finish_common(self):
        while self.done < self.common:
            self.send()
            self.join()

    def core(self, which):
        return [self.net.swap(x, self.orders[0][-1]) for x in which]


class Sum:
    def __init__(self, net, x):
        self.net = net
        n = x.shape[1]
        x = x.reshape((2,) * (net.fb - 1) + x.shape[1:])
        axes = [1 << b for b in range(net.fb - 1, 0, -1)]
        dps = [("dp", 1 << b) for b in range(net.db - 1, -1, -1)]
        fs = [("fsdp", 1 << b) for b in range(1, net.fb)]
        half = n // 2
        self.parts = [
            [lax.slice_in_dim(x, p * half, p * half + half, axis=x.ndim - 2), axes, order]
            for p, order in enumerate((dps + fs[:1], fs[:1] + dps))
        ]
        self.tail = fs[1:]

    @property
    def left(self):
        return max(len(p[2]) for p in self.parts) + len(self.tail)

    def send(self):
        if not self.parts[0][2] and len(self.parts) > 1:
            self.parts = [[jnp.concatenate([p[0] for p in self.parts], axis=-2), self.parts[0][1], self.tail]]
            self.tail = []
        self.keeps, self.raw = [], []
        for p in self.parts:
            keep, send, p[1] = self.net.halves(p[0], p[2][0], p[1])
            self.keeps.append(keep)
            self.raw.append(self.net.swap(send, p[2][0]))

    def join(self):
        for p, keep, got in zip(self.parts, self.keeps, self.raw):
            p[0] = plus(keep, got)
            p[2] = p[2][1:]

    def finish(self):
        while self.left:
            self.send()
            self.join()
        return self.parts[0][0]


def place_kernel(idx, *refs, plans, count):
    srcs, outs, sems = refs[:count], refs[count:-1], refs[-1]
    copies = []
    for ref, plan in zip(srcs, plans):
        kd = ref.shape[2]
        for slot, ((d, f), moves) in enumerate(plan):
            for first, rows, which, n, start in moves:
                row = pl.multiple_of((idx[1] ^ f) * n + start, 16)
                col = pl.multiple_of((idx[0] ^ d) * kd, LANES)
                copies.append(
                    pltpu.make_async_copy(
                        ref.at[slot, pl.ds(first, rows), :],
                        outs[which].at[pl.ds(row, rows), pl.ds(col, kd)],
                        sems.at[len(copies)],
                    )
                )
    for c in copies:
        c.start()
    for c in copies:
        c.wait()


def place(net, idx, gather, theirs, sizes):
    pieces = gather.x + gather.far + theirs
    lanes = pieces[0].shape[-1]
    plans = []
    total = 0
    count = len(gather.bounds)
    for i in range(len(pieces)):
        quarter, part = divmod(i, count)
        offs = net.offsets(gather.orders[part])
        some = offs[quarter * len(offs) // 4 : (quarter + 1) * len(offs) // 4]
        lo, hi = gather.bounds[part]
        moves, at = [], 0
        for which, n in enumerate(sizes):
            a, b = max(lo, at), min(hi, at + n)
            if a < b:
                moves.append((a - lo, b - a, which, n, a - at))
            at += n
        plans.append([(o, moves) for o in some])
        total += len(some) * len(moves)
    shapes = [shape((n * net.nf, lanes * net.nd), bf16) for n in sizes]
    return pl.pallas_call(
        partial(place_kernel, plans=plans, count=len(pieces)),
        grid_spec=pltpu.PrefetchScalarGridSpec(
            num_scalar_prefetch=1,
            grid=(1,),
            in_specs=[pl.BlockSpec(memory_space=pl.ANY)] * len(pieces),
            out_specs=[pl.BlockSpec(memory_space=pl.ANY)] * len(sizes),
            scratch_shapes=[pltpu.SemaphoreType.DMA((total,))],
        ),
        out_shape=shapes,
        compiler_params=params(16),
        cost_estimate=cost(0, 4 * sum(sizes) * net.nf * lanes * net.nd),
        name="place",
    )(idx, *pieces)


def norm_stats(x):
    mean = jnp.mean(x, axis=-1, keepdims=True)
    centered = x - mean
    var = jnp.mean(centered * centered, axis=-1, keepdims=True)
    rstd = lax.rsqrt(var + epsilon)
    return centered * rstd, rstd


def seg_sums(pick, x):
    top = x.astype(bf16)
    low = (x - top.astype(f32)).astype(bf16)
    return (dot(pick, top, 0, 0) + dot(pick, low, 0, 0))[:8]


def flip_kernel(*refs):
    n = len(refs) // 2
    for src, dst in zip(refs[:n], refs[n:]):
        dst[...] = jnp.transpose(src[...].astype(f32)).astype(bf16)


def flip(*xs):
    return pl.pallas_call(
        flip_kernel,
        out_shape=[shape(x.shape[::-1], bf16) for x in xs],
        compiler_params=params(32),
        cost_estimate=cost(0, 4 * sum(x.size for x in xs)),
        name="flip",
    )(*xs)


def skip_fwd_kernel(idx, lens, frames, skip, cond, w, hidden, mixed):
    rb, d = frames.shape
    pos = idx[0] * (rb * pl.num_programs(0)) + pl.program_id(0) * rb + lax.broadcasted_iota(jnp.int32, (rb, 1), 0)
    keep = jnp.zeros((rb, 1), f32)
    end = 0
    for u in range(lens.shape[1]):
        start, end = end, end + lens[0, u]
        keep = jnp.where((pos >= start) & (pos < end), (1 - lens[1, u]).astype(f32), keep)
    m = (frames[...].astype(f32) + keep * cond[...].astype(f32)).astype(bf16)
    mixed[...] = m
    hidden[...] = (dot(m, w[:, :d], 1, 1) + dot(skip[...], w[:, d:], 1, 1)).astype(bf16)


def skip_fwd(idx, lens, frames, skip, cond, w):
    r, d = frames.shape
    rb = min(256, r)
    row = pl.BlockSpec((rb, d), lambda i, s, t: (i, 0))
    return pl.pallas_call(
        skip_fwd_kernel,
        grid_spec=pltpu.PrefetchScalarGridSpec(
            num_scalar_prefetch=2,
            grid=(r // rb,),
            in_specs=[row, row, row, pl.BlockSpec(w.shape, lambda i, s, t: (0, 0))],
            out_specs=[row, row],
        ),
        out_shape=[shape((r, d), bf16)] * 2,
        compiler_params=params(),
        cost_estimate=cost(4 * r * d * d, 10 * r * d + 4 * d * d),
        name="skip_fwd",
    )(idx, lens, frames, skip, cond, w)


def turn(x, cos, sin, sign):
    width = x.shape[1]
    reps = width // LANES
    if reps > 1:
        cos = jnp.concatenate([cos] * reps, axis=1)
        sin = jnp.concatenate([sin] * reps, axis=1)
    lane = lax.broadcasted_iota(jnp.int32, (1, width), 1)
    other = jnp.where(lane % HD < HD // 2, pltpu.roll(x, width - HD // 2, 1), pltpu.roll(x, HD // 2, 1))
    return x * cos + other * sin if sign > 0 else x * cos - other * sin


def chosen(idx, own, got):
    half = pl.program_id(0) * 2 < pl.num_programs(0)
    new = jnp.where(half, got[0][...], got[1][...]) if len(got) > 1 else got[0][...]
    return jnp.where(idx[2] > 0, new, own[...])


def chosen_specs(rb, d, steps, halves=2):
    row = pl.BlockSpec((rb, d), lambda i, s: (i, 0))
    if halves == 1:
        return [row, row]
    return [
        row,
        pl.BlockSpec((rb, d), lambda i, s: (jnp.minimum(i, steps // 2 - 1), 0)),
        pl.BlockSpec((rb, d), lambda i, s: (jnp.maximum(i - steps // 2, 0), 0)),
    ]


def qkv_fwd_kernel(idx, hidden0, got, pick, mod, w, cos, sin, hidden, normed, *pieces):
    d = hidden.shape[1]
    na = len(pieces)
    hw = d // na
    h = chosen(idx, hidden0, (got,))
    hidden[...] = h
    xh, _ = norm_stats(h.astype(f32))
    pk = pick[...]
    y = (xh * (1.0 + dot(pk, mod[:, d:], 1, 0)) + dot(pk, mod[:, :d], 1, 0)).astype(bf16)
    normed[...] = y
    for part in range(3):
        for r in range(na):
            at = pl.multiple_of(part * d + (idx[0] ^ r) * hw, hw)
            z = dot(y, w[pl.ds(at, hw), :], 1, 1)
            if part < 2:
                z = turn(z, cos[...], sin[...], 1)
            if part == 0:
                z = z * (1.0 / math.sqrt(HD))
            pieces[r][part] = z.astype(bf16)


def qkv_fwd(net, idx, hidden0, got, pick, mod, w, cos, sin):
    r, d = hidden0.shape
    rb = min(256, r // 2)
    hw = d // net.na
    row = pl.BlockSpec((rb, d), lambda i, s: (i, 0))
    narrow = pl.BlockSpec((rb, LANES), lambda i, s: (i, 0))
    out = pl.BlockSpec((3, rb, hw), lambda i, s: (0, i, 0))
    res = pl.pallas_call(
        qkv_fwd_kernel,
        grid_spec=pltpu.PrefetchScalarGridSpec(
            num_scalar_prefetch=1,
            grid=(r // rb,),
            in_specs=chosen_specs(rb, d, r // rb, 1)
            + [
                narrow,
                pl.BlockSpec(mod.shape, lambda i, s: (0, 0)),
                pl.BlockSpec(w.shape, lambda i, s: (0, 0)),
                narrow,
                narrow,
            ],
            out_specs=[row, row] + [out] * net.na,
        ),
        out_shape=[shape((r, d), bf16)] * 2 + [shape((3, r, hw), bf16)] * net.na,
        compiler_params=params(),
        cost_estimate=cost(6 * r * d * d, 14 * r * d + 6 * d * d),
        name="qkv_fwd",
    )(idx, hidden0, got, pick, mod, w, cos, sin)
    return res[0], res[1], res[2:]


def out_fwd_kernel(idx, *refs, na):
    pieces = refs[:na]
    hidden, pick, mod, w, d_f0, got0, got1, attn, hidden2, normed, d_f = refs[na:]
    d = hidden.shape[1]
    d_f[...] = chosen(idx, d_f0, (got0, got1))
    hw = d // na
    for r in range(na):
        attn[:, pl.ds(pl.multiple_of((idx[0] ^ r) * hw, hw), hw)] = pieces[r][...]
    h2 = hidden[...].astype(f32) + dot(attn[...], w[...], 1, 1)
    hidden2[...] = h2
    xh, _ = norm_stats(h2)
    pk = pick[...]
    normed[...] = (xh * (1.0 + dot(pk, mod[:, d:], 1, 0)) + dot(pk, mod[:, :d], 1, 0)).astype(bf16)


def out_fwd(net, idx, pieces, hidden, pick, mod, w, d_f0, d_f_got):
    r, d = hidden.shape
    rb = min(256, r // 2)
    hw = d // net.na
    row = pl.BlockSpec((rb, d), lambda i, s: (i, 0))
    narrow = pl.BlockSpec((rb, LANES), lambda i, s: (i, 0))
    return pl.pallas_call(
        partial(out_fwd_kernel, na=net.na),
        grid_spec=pltpu.PrefetchScalarGridSpec(
            num_scalar_prefetch=1,
            grid=(r // rb,),
            in_specs=[pl.BlockSpec((rb, hw), lambda i, s: (i, 0))] * net.na
            + [
                row,
                narrow,
                pl.BlockSpec(mod.shape, lambda i, s: (0, 0)),
                pl.BlockSpec(w.shape, lambda i, s: (0, 0)),
            ]
            + chosen_specs(rb, d, r // rb),
            out_specs=[row, row, row, row],
        ),
        out_shape=[shape((r, d), bf16), shape((r, d), f32)] + [shape((r, d), bf16)] * 2,
        compiler_params=params(),
        cost_estimate=cost(2 * r * d * d, 12 * r * d + 2 * d * d),
        name="out_fwd",
    )(idx, *pieces, hidden, pick, mod, w, d_f0, *d_f_got)


def norm_back(x, grad, pick, scale):
    xh, rstd = norm_stats(x)
    g = grad * (1.0 + dot(pick, scale, 1, 0))
    dx = rstd * (
        g
        - jnp.mean(g, axis=-1, keepdims=True)
        - xh * jnp.mean(g * xh, axis=-1, keepdims=True)
    )
    return dx, seg_sums(pick, grad * xh), seg_sums(pick, grad)


def out_bwd_kernel(idx, grad, hidden2, d_f, pick, scale, w, d_h2, d_att, sums, *outs):
    refs, hold = outs[:-1], outs[-1]
    i = pl.program_id(0)
    na = len(refs)
    d = grad.shape[1]
    hw = d // na
    dx, d_scale, d_shift = norm_back(hidden2[...], grad[...], pick[...], scale[...])
    dh = d_f[...].astype(f32) + dx
    d_h2[...] = dh
    low = dh.astype(bf16)
    d_att[...] = low
    hold[...] = dot(low, w[...], 1, 0).astype(bf16)
    for r in range(na):
        refs[r][...] = hold[:, pl.ds(pl.multiple_of((idx[0] ^ r) * hw, hw), hw)]
    both = jnp.concatenate([d_shift, d_scale], axis=1)

    @pl.when(i == 0)
    def _():
        sums[...] = both

    @pl.when(i > 0)
    def _():
        sums[...] += both


def out_bwd(net, idx, grad, hidden2, d_f, pick, scale, w):
    r, d = grad.shape
    rb = min(256, r)
    hw = d // net.na
    row = pl.BlockSpec((rb, d), lambda i, s: (i, 0))
    narrow = pl.BlockSpec((rb, LANES), lambda i, s: (i, 0))
    whole = lambda a: pl.BlockSpec(a.shape, lambda i, s: (0, 0))
    res = pl.pallas_call(
        out_bwd_kernel,
        grid_spec=pltpu.PrefetchScalarGridSpec(
            num_scalar_prefetch=1,
            grid=(r // rb,),
            in_specs=[row, row, row, narrow, whole(scale), whole(w)],
            out_specs=[row, row, pl.BlockSpec((8, 2 * d), lambda i, s: (0, 0))]
            + [pl.BlockSpec((rb, hw), lambda i, s: (i, 0))] * net.na,
            scratch_shapes=[pltpu.VMEM((rb, d), bf16)],
        ),
        out_shape=[shape((r, d), f32), shape((r, d), bf16), shape((8, 2 * d), f32)]
        + [shape((r, hw), bf16)] * net.na,
        compiler_params=params(),
        cost_estimate=cost(2 * r * d * d, 20 * r * d + 2 * d * d),
        name="out_bwd",
    )(idx, grad, hidden2, d_f, pick, scale, w)
    return res[0], res[1], res[2], res[3:]


def turn_back_kernel(idx, *refs, na):
    pieces = refs[:-3]
    cos, sin, d_qkv = refs[-3:]
    d = d_qkv.shape[1] // 3
    hw = d // na
    for part in range(3):
        first = 0
        for k, piece in enumerate(pieces):
            r = k % na
            wide = piece.shape[2]
            z = piece[part]
            if part < 2:
                z = turn(z.astype(f32), cos[...], sin[...], -1).astype(bf16)
            d_qkv[:, pl.ds(pl.multiple_of(part * d + (idx[0] ^ r) * hw + first, LANES), wide)] = z
            first += wide if r == na - 1 else 0


def turn_back(net, idx, pieces, cos, sin, d):
    r = cos.shape[0]
    rb = min(256, r)
    narrow = pl.BlockSpec((rb, LANES), lambda i, s: (i, 0))
    return pl.pallas_call(
        partial(turn_back_kernel, na=net.na),
        grid_spec=pltpu.PrefetchScalarGridSpec(
            num_scalar_prefetch=1,
            grid=(r // rb,),
            in_specs=[pl.BlockSpec((3, rb, p.shape[2]), lambda i, s: (0, i, 0)) for p in pieces] + [narrow, narrow],
            out_specs=pl.BlockSpec((rb, 3 * d), lambda i, s: (i, 0)),
        ),
        out_shape=shape((r, 3 * d), bf16),
        compiler_params=params(),
        cost_estimate=cost(12 * r * d, 12 * r * d),
        name="turn_back",
    )(idx, *pieces, cos, sin)


def qkv_bwd_kernel(d_qkv, hidden, d_h2, pick, scale, w, d_h, sums):
    i = pl.program_id(0)
    grad = dot(d_qkv[...], w[...], 1, 0)
    dx, d_scale, d_shift = norm_back(hidden[...].astype(f32), grad, pick[...], scale[...])
    d_h[...] = (d_h2[...] + dx).astype(bf16)
    both = jnp.concatenate([d_shift, d_scale], axis=1)

    @pl.when(i == 0)
    def _():
        sums[...] = both

    @pl.when(i > 0)
    def _():
        sums[...] += both


def qkv_bwd(d_qkv, hidden, d_h2, pick, scale, w):
    r, d = hidden.shape
    rb = min(256, r)
    row = pl.BlockSpec((rb, d), lambda i: (i, 0))
    narrow = pl.BlockSpec((rb, LANES), lambda i: (i, 0))
    whole = lambda a: pl.BlockSpec(a.shape, lambda i: (0, 0))
    return pl.pallas_call(
        qkv_bwd_kernel,
        grid=(r // rb,),
        in_specs=[pl.BlockSpec((rb, 3 * d), lambda i: (i, 0)), row, row, narrow, whole(scale), whole(w)],
        out_specs=[row, pl.BlockSpec((8, 2 * d), lambda i: (0, 0))],
        out_shape=[shape((r, d), bf16), shape((8, 2 * d), f32)],
        compiler_params=params(),
        cost_estimate=cost(6 * r * d * d, 16 * r * d + 6 * d * d),
        name="qkv_bwd",
    )(d_qkv, hidden, d_h2, pick, scale, w)


def skip_bwd_kernel(idx, d_h, d_h_got, w, d_frames, d_skip):
    d = d_h.shape[1]
    g = jnp.where(idx[2] > 0, d_h_got[...], d_h[...])
    d_frames[...] = dot(g, w[:, :d], 1, 0)
    d_skip[...] = dot(g, w[:, d:], 1, 0)


def skip_bwd(idx, d_h, d_h_got, w):
    r, d = d_h.shape
    rb = min(256, r)
    row = pl.BlockSpec((rb, d), lambda i, s: (i, 0))
    return pl.pallas_call(
        skip_bwd_kernel,
        grid_spec=pltpu.PrefetchScalarGridSpec(
            num_scalar_prefetch=1,
            grid=(r // rb,),
            in_specs=[row, row, pl.BlockSpec(w.shape, lambda i, s: (0, 0))],
            out_specs=[row, row],
        ),
        out_shape=[shape((r, d), f32)] * 2,
        compiler_params=params(),
        cost_estimate=cost(4 * r * d * d, 12 * r * d + 4 * d * d),
        name="skip_bwd",
    )(idx, d_h, d_h_got, w)


def outer_kernel(idx, g, *refs, n, own, choose):
    xs = refs[:own]
    keep, send = refs[-2:]
    pairs = keep.shape[0]
    at = 0
    low = idx[1] & 1 == 0
    for k in range(0, own, 2 if choose else 1):
        x = jnp.where(idx[2] > 0, xs[k + 1][...], xs[k][...]) if choose else xs[k][...]
        width = x.shape[1]
        z = dot(g[...], x, 0, 0).astype(bf16).reshape(pairs, 2, n, width)
        keep[:, :, at : at + width] = jnp.where(low, z[:, 0], z[:, 1])
        send[:, :, at : at + width] = jnp.where(low, z[:, 1], z[:, 0])
        at += width


def outer(net, idx, g, xs, n, rows, first, into=None, choose=False):
    r, wide = g.shape
    per = max(1, 512 // (2 * n))
    while net.nf // 2 % per:
        per -= 1
    k = sum(x.shape[1] for x in xs) // (2 if choose else 1)
    out = pl.BlockSpec((per, n, k), lambda i, s: (i, first // n, 0))
    big = shape((net.nf // 2, rows, k), bf16)
    extra = list(into) if into is not None else []
    return pl.pallas_call(
        partial(outer_kernel, n=n, own=len(xs), choose=choose),
        grid_spec=pltpu.PrefetchScalarGridSpec(
            num_scalar_prefetch=1,
            grid=(wide // (2 * n * per),),
            in_specs=[pl.BlockSpec((r, 2 * n * per), lambda i, s: (0, i))]
            + [pl.BlockSpec(x.shape, lambda i, s: (0, 0)) for x in xs]
            + [pl.BlockSpec(memory_space=pl.ANY)] * len(extra),
            out_specs=[out, out],
        ),
        out_shape=[big, big],
        input_output_aliases={2 + len(xs) + i: i for i in range(len(extra))},
        compiler_params=params(),
        cost_estimate=cost(2 * r * wide * k, 2 * (r * wide + r * k + wide * k)),
        name="outer",
    )(idx, g, *xs, *extra)


def gelu_both(u):
    u2 = u * u
    t = jnp.tanh(GELU_C * u * (1.0 + 0.044715 * u2))
    half = 0.5 * (1.0 + t)
    return u * half, half + 0.5 * u * (1.0 - t * t) * (GELU_C * (1.0 + 3 * 0.044715 * u2))


def ffn_kernel(*refs, steps, second):
    x_ref, df_ref, o_in = refs[:3]
    at = 4 if second else 3
    ws = refs[at : at + steps]
    o_ref, dx_ref = refs[at + steps : at + steps + 2]
    gs = refs[at + steps + 2 : at + 2 * steps + 2]
    o_acc, dx_acc, o_low, wbuf, gbuf, sem_w, sem_g, sem_a = refs[at + 2 * steps + 2 :]
    s = pl.program_id(0)
    slot = lax.rem(s, 2)
    w_in = [pltpu.make_async_copy(ws[k], wbuf.at[k % 2], sem_w.at[k]) for k in range(steps)]
    g_out = [pltpu.make_async_copy(gbuf.at[k % 2], gs[k], sem_g.at[k]) for k in range(steps)]
    sums = [pltpu.make_async_copy(o_in, o_acc, sem_a.at[0])]
    if second:
        sums.append(pltpu.make_async_copy(refs[3], dx_acc, sem_a.at[1]))
    ends = [
        pltpu.make_async_copy(o_low if second else o_acc, o_ref, sem_a.at[2]),
        pltpu.make_async_copy(dx_acc, dx_ref, sem_a.at[3]),
    ]

    @pl.when(s == 0)
    def _():
        w_in[0].start()
        for c in sums:
            c.start()
        if not second:
            dx_acc[...] = jnp.zeros_like(dx_acc)

    for k in range(steps):

        @pl.when(s == k)
        def _():
            if k + 1 < steps:
                w_in[k + 1].start()
            w_in[k].wait()

    d = x_ref.shape[1]
    wu = wbuf[slot, :, 0].reshape(-1, d)
    wd = wbuf[slot, :, 1].reshape(-1, d)
    x, df = x_ref[...], df_ref[...]
    g, dg = gelu_both(dot(x, wu, 1, 1))
    act = g.astype(bf16)
    du = (dot(df, wd, 1, 1) * dg).astype(bf16)

    @pl.when(s == 0)
    def _():
        for c in sums:
            c.wait()

    o_acc[...] += dot(act, wd, 1, 0)
    dx_acc[...] += dot(du, wu, 1, 0)
    for k in range(2, steps):

        @pl.when(s == k)
        def _():
            g_out[k - 2].wait()

    part = gbuf.shape[1:2] + gbuf.shape[3:]
    gbuf[slot, :, 1] = dot(act, df, 0, 0).astype(bf16).reshape(part)
    gbuf[slot, :, 0] = dot(du, x, 0, 0).astype(bf16).reshape(part)
    for k in range(steps):

        @pl.when(s == k)
        def _():
            g_out[k].start()

    @pl.when(s == steps - 1)
    def _():
        if second:
            o_low[...] = o_acc[...].astype(bf16)
        for c in ends:
            c.start()
        for k in range(max(0, steps - 2), steps):
            g_out[k].wait()
        for c in ends:
            c.wait()


def ffn(x, df, o_in, pieces, dx_in=None):
    second = dx_in is not None
    r, d = x.shape
    steps = len(pieces)
    full = pl.BlockSpec((r, d), lambda s: (0, 0), pipeline_mode=pl.Buffered(1))
    far = pl.BlockSpec(memory_space=pl.ANY)
    args = [x, df, o_in] + ([dx_in] if second else []) + list(pieces)
    piece = shape(pieces[0].shape, bf16)
    units = piece.shape[0] * piece.shape[2]
    return pl.pallas_call(
        partial(ffn_kernel, steps=steps, second=second),
        grid=(steps,),
        in_specs=[full, full] + [far] * (len(args) - 2),
        out_specs=[far] * (steps + 2),
        out_shape=[shape((r, d), bf16 if second else f32), shape((r, d), f32)] + [piece] * steps,
        scratch_shapes=[
            pltpu.VMEM((r, d), f32),
            pltpu.VMEM((r, d), f32),
            pltpu.VMEM((r, d) if second else (16, LANES), bf16),
            pltpu.VMEM((2, *piece.shape), bf16),
            pltpu.VMEM((2, *piece.shape), bf16),
            pltpu.SemaphoreType.DMA((steps,)),
            pltpu.SemaphoreType.DMA((steps,)),
            pltpu.SemaphoreType.DMA((4,)),
        ],
        compiler_params=params(),
        cost_estimate=cost(12 * r * d * steps * units, 16 * r * d + 8 * steps * units * d, steps * units * r),
        name="ffn",
    )(*args)


def head_sel(h):
    lane = lax.broadcasted_iota(jnp.int32, (1, LANES), 1)
    return lane < HD if h == 0 else lane >= HD


def load_rolled(idx, hold, refs, part, rest):
    rows = refs[0].shape[-2]
    t = rows * len(refs)
    for r, ref in enumerate(refs):
        x = ref[part] if part is not None else ref[...]
        hold[pl.ds(pl.multiple_of((idx[0] ^ r) * rows, rows), rows), :] = x.astype(f32)
    hold[t : t + rest, :] = hold[0:rest, :]
    return hold[pl.ds(idx[1], t), :]


def store_unrolled(idx, hold, t, rest):
    row = lax.broadcasted_iota(jnp.int32, (rest, 1), 0)
    hold[0:rest, :] = jnp.where(row < idx[1], hold[t : t + rest, :], hold[0:rest, :])


def attn_fwd_kernel(idx, *refs, na, long):
    pieces = refs[:na]
    segr, segc = refs[na : na + 2]
    outs = refs[na + 2 : 2 * na + 2]
    lse_ref, hold, ql, kl, vt = refs[2 * na + 2 :]
    rows = outs[0].shape[0]
    t = rows * na
    rest = t - long
    ql[...] = load_rolled(idx, hold, pieces, 0, rest).astype(bf16)
    kl[...] = load_rolled(idx, hold, pieces, 1, rest).astype(bf16)
    vt[...] = jnp.transpose(load_rolled(idx, hold, pieces, 2, rest)).astype(bf16)

    def pair(r0, n, c0, cn, mask):
        q = ql[pl.ds(r0, n), :]
        k = kl[c0 : c0 + cn, :]
        got, lses = [], []
        for h in range(2):
            qh = jnp.where(head_sel(h), q, jnp.zeros_like(q))
            s = dot(k, qh, 1, 1)
            if mask is not None:
                s = jnp.where(mask, s, NEG)
            top = jnp.max(s, axis=0, keepdims=True)
            p = jnp.exp(s - top)
            total = jnp.sum(p, axis=0, keepdims=True)
            got.append(dot(vt[HD * h : HD * h + HD, c0 : c0 + cn], p.astype(bf16), 1, 0) / total)
            lses.append(top + jnp.log(total))
        lse_ref[0, :, pl.ds(r0, n)] = jnp.concatenate(lses, axis=0)
        hold[pl.ds(idx[1] + r0, n), :] = jnp.transpose(jnp.concatenate(got, axis=0))

    step = long // 2
    for i in range(2):
        pair(i * step, step, 0, long, None)
    pair(long, rest, long, rest, segc[:, :1] == segr[:1, :])
    store_unrolled(idx, hold, t, rest)
    for r in range(na):
        outs[r][...] = hold[pl.ds(pl.multiple_of((idx[0] ^ r) * rows, rows), rows), :].astype(bf16)


def attn_fwd(net, idx, pieces, segr, segc, long):
    na = net.na
    _, rows, hw = pieces[0].shape
    t = rows * na
    rest = t - long
    pairs = hw // LANES
    const = lambda a: pl.BlockSpec(a.shape, lambda j, s: (0, 0))
    work = pairs * 2 * (long * long + rest * rest)
    res = pl.pallas_call(
        partial(attn_fwd_kernel, na=na, long=long),
        grid_spec=pltpu.PrefetchScalarGridSpec(
            num_scalar_prefetch=1,
            grid=(pairs,),
            in_specs=[pl.BlockSpec((3, rows, LANES), lambda j, s: (0, 0, j))] * na + [const(segr), const(segc)],
            out_specs=[pl.BlockSpec((rows, LANES), lambda j, s: (0, j))] * na
            + [pl.BlockSpec((1, 2, t), lambda j, s: (j, 0, 0))],
            scratch_shapes=[
                pltpu.VMEM((t + rest, LANES), f32),
                pltpu.VMEM((t, LANES), bf16),
                pltpu.VMEM((t, LANES), bf16),
                pltpu.VMEM((LANES, t), bf16),
            ],
        ),
        out_shape=[shape((rows, hw), bf16)] * na + [shape((pairs, 2, t), f32)],
        compiler_params=params(),
        cost_estimate=cost(16 * HD * work, 8 * t * hw, work),
        name="attn_fwd",
    )(idx, *pieces, segr, segc)
    return res[:na], res[na]


def attn_bwd_kernel(idx, *refs, na, long):
    pieces, d_pieces = refs[:na], refs[na : 2 * na]
    lse_ref, segr, segc = refs[2 * na : 2 * na + 3]
    outs = refs[2 * na + 3 : 3 * na + 3]
    hold, ql, kl, vl, dl, kt, dqt, dka, dva = refs[3 * na + 3 :]
    rows = outs[0].shape[1]
    t = rows * na
    rest = t - long
    ql[...] = load_rolled(idx, hold, pieces, 0, rest).astype(bf16)
    kf = load_rolled(idx, hold, pieces, 1, rest)
    kl[...] = kf.astype(bf16)
    kt[...] = jnp.transpose(kf).astype(bf16)
    vl[...] = load_rolled(idx, hold, pieces, 2, rest).astype(bf16)
    dl[...] = load_rolled(idx, hold, d_pieces, None, rest).astype(bf16)
    dka[...] = jnp.zeros_like(dka)
    dva[...] = jnp.zeros_like(dva)

    def pair(r0, n, c0, cn, mask):
        q, do = ql[pl.ds(r0, n), :], dl[pl.ds(r0, n), :]
        k, v = kl[c0 : c0 + cn, :], vl[c0 : c0 + cn, :]
        dqs = []
        for h in range(2):
            qh = jnp.where(head_sel(h), q, jnp.zeros_like(q))
            dh = jnp.where(head_sel(h), do, jnp.zeros_like(do))
            s = dot(k, qh, 1, 1)
            if mask is not None:
                s = jnp.where(mask, s, NEG)
            p = jnp.exp(s - lse_ref[0, h : h + 1, pl.ds(r0, n)])
            dp = dot(v, dh, 1, 1)
            delta = jnp.sum(p * dp, axis=0, keepdims=True)
            ds = (p * (dp - delta)).astype(bf16)
            dqs.append(dot(kt[HD * h : HD * h + HD, c0 : c0 + cn], ds, 1, 0))
            dva[c0 : c0 + cn, :] += dot(p.astype(bf16), dh, 1, 0)
            dka[c0 : c0 + cn, :] += dot(ds, qh, 1, 0)
        dqt[pl.ds(r0, n), :] = jnp.transpose(jnp.concatenate(dqs, axis=0))

    step = long // 2

    def body(i, carry):
        pair(pl.multiple_of(i * step, step), step, 0, long, None)
        return carry

    lax.fori_loop(0, 2, body, 0)
    pair(long, rest, long, rest, segc[:, :1] == segr[:1, :])
    for part, src in enumerate((dqt, dka, dva)):
        x = src[...]
        if part == 0:
            x = x * (1.0 / math.sqrt(HD))
        hold[pl.ds(idx[1], t), :] = x
        store_unrolled(idx, hold, t, rest)
        for r in range(na):
            at = pl.multiple_of((idx[0] ^ r) * rows, rows)
            outs[r][part] = hold[pl.ds(at, rows), :].astype(bf16)


def attn_bwd(net, idx, pieces, d_pieces, lse, segr, segc, long, start, pairs):
    na = net.na
    rows = pieces[0].shape[1]
    t = rows * na
    rest = t - long
    hw = pairs * LANES
    const = lambda a: pl.BlockSpec(a.shape, lambda j, s: (0, 0))
    three = pl.BlockSpec((3, rows, LANES), lambda j, s: (0, 0, j + start))
    out = pl.BlockSpec((3, rows, LANES), lambda j, s: (0, 0, j))
    work = pairs * 2 * (long * long + rest * rest)
    return pl.pallas_call(
        partial(attn_bwd_kernel, na=na, long=long),
        grid_spec=pltpu.PrefetchScalarGridSpec(
            num_scalar_prefetch=1,
            grid=(pairs,),
            in_specs=[three] * na
            + [pl.BlockSpec((rows, LANES), lambda j, s: (0, j + start))] * na
            + [pl.BlockSpec((1, 2, t), lambda j, s: (j + start, 0, 0)), const(segr), const(segc)],
            out_specs=[out] * na,
            scratch_shapes=[pltpu.VMEM((t + rest, LANES), f32)]
            + [pltpu.VMEM((t, LANES), bf16)] * 4
            + [pltpu.VMEM((LANES, t), bf16)]
            + [pltpu.VMEM((t, LANES), f32)] * 3,
        ),
        out_shape=[shape((3, rows, hw), bf16)] * na,
        compiler_params=params(),
        cost_estimate=cost(40 * HD * work, 16 * t * hw, work),
        name="attn_bwd",
    )(idx, *pieces, *d_pieces, lse, segr, segc)


def prep_kernel(ints, me, w_mod, cos, sin, pick, segr, segc, smooth, part, idx, gs, *, nd, utt, long, regroup):
    nf = ints.shape[0]
    rows, rest = cos.shape[0], segr.shape[1]
    total = rows * (2 if regroup else nd)
    y, f, block = me[0], me[1], me[3]
    mine = ((f & ~1) | y) ^ f if regroup else 0
    starts, ends, at, first = [], [], 0, 0
    for u in range(utt):
        size = ints[mine, u]
        starts.append(at)
        first = jnp.where(size == long, at, first)
        at = at + size
        ends.append(at)
    idx[0], idx[1], idx[2] = block, first, me[2]
    kept = 0
    for g in range(nf):
        for u in range(utt):
            kept = kept + (1 - ints[g, utt + u])
    gs[0] = (nf * utt) / jnp.maximum(kept.astype(f32), 1.0)

    pos = block * rows + lax.broadcasted_iota(jnp.int32, (rows, LANES), 0)
    lane = lax.broadcasted_iota(jnp.int32, (rows, LANES), 1)
    offset = jnp.zeros((rows, LANES), jnp.int32)
    number = jnp.zeros((rows, LANES), jnp.int32)
    for u in range(1, utt):
        past = pos >= starts[u]
        offset = jnp.where(past, starts[u], offset)
        number = jnp.where(past, u, number)
    pick[...] = jnp.where((lane % utt == number) & (lane < 3 * utt), 1.0, 0.0).astype(bf16)
    half = HD // 2
    frequency = jnp.exp((lane[:1] % half).astype(f32) * (-math.log(10000.0) / half))
    angles = (pos - offset).astype(f32) * frequency
    cos[...] = jnp.cos(angles)
    sin[...] = jnp.where(lane[:1] % HD < half, -1.0, 1.0) * jnp.sin(angles)

    for ref, axis in ((segr, 1), (segc, 0)):
        p = first + long + lax.broadcasted_iota(jnp.int32, ref.shape, axis)
        p = jnp.where(p >= total, p - total, p)
        number = jnp.zeros(ref.shape, jnp.int32)
        for u in range(1, utt):
            number = jnp.where(p >= starts[u], u, number)
        ref[...] = number

    n, wide = smooth.shape
    d = wide * nd
    row = lax.broadcasted_iota(jnp.int32, (n, LANES), 0)
    when = jnp.zeros((n, LANES), jnp.int32)
    for j in range(n):
        k, u = divmod(j, utt)
        g = 2 * (k % (nf // 2)) + k // (nf // 2) if regroup else k
        when = jnp.where(row == j, ints[g ^ f, 2 * utt + u], when)
    flow = 1000.0 * (when[:, :1].astype(f32) / STEPS)
    col = y * wide + lax.broadcasted_iota(jnp.int32, (1, wide), 1)
    low = col < d // 2
    at = jnp.where(low, col, col - d // 2).astype(f32)
    angles = flow * jnp.exp(at * (-math.log(10000.0) / (d // 2)))
    e = jnp.where(low, jnp.sin(angles), jnp.cos(angles))
    e = (e / (1.0 + jnp.exp(-e))).astype(bf16)
    smooth[...] = e
    part[...] = dot(e, w_mod[...], 1, 0)


def prep(net, ints, me, w_mod, rows, long, rest):
    utt = ints.shape[1] // 3
    n = net.nf * utt
    smem = pl.BlockSpec(memory_space=pltpu.SMEM)
    vmem = pl.BlockSpec(memory_space=pltpu.VMEM)
    return pl.pallas_call(
        partial(prep_kernel, nd=net.nd, utt=utt, long=long, regroup=net.regroup),
        in_specs=[smem, smem, vmem],
        out_specs=[vmem] * 7 + [smem, smem],
        out_shape=[
            shape((rows, LANES), f32),
            shape((rows, LANES), f32),
            shape((rows, LANES), bf16),
            shape((8, rest), jnp.int32),
            shape((rest, LANES), jnp.int32),
            shape((n, w_mod.shape[0]), bf16),
            shape((n, w_mod.shape[1]), f32),
            shape((3,), jnp.int32),
            shape((1,), f32),
        ],
        compiler_params=params(32),
        cost_estimate=cost(2 * n * w_mod.size, 16 * rows * LANES, 4 * n * w_mod.shape[0]),
        name="prep",
    )(ints, me, w_mod)


def terms_kernel(*refs):
    out = refs[-1]
    x = refs[0][...]
    for ref in refs[1:-1]:
        x = x + ref[...]
    a = x.astype(bf16)
    b = (x - a.astype(f32)).astype(bf16)
    c = (x - a.astype(f32) - b.astype(f32)).astype(bf16)
    n = x.shape[0]
    out[...] = jnp.zeros_like(out)
    out[0 : 3 * n, :] = jnp.concatenate([a.astype(f32), b.astype(f32), c.astype(f32)], axis=0).astype(bf16)


def three_terms(*xs):
    return pl.pallas_call(
        terms_kernel,
        out_shape=shape((LANES, xs[0].shape[1]), bf16),
        compiler_params=params(16),
        cost_estimate=cost(0, 300 * xs[0].shape[1]),
        name="three_terms",
    )(*xs)


def scale_kernel(gs, x, out):
    out[...] = (x[...].astype(f32) * gs[0]).astype(bf16)


def scaled(x, gs):
    r, d = x.shape
    rb = min(512, r)
    row = pl.BlockSpec((rb, d), lambda i, s: (i, 0))
    return pl.pallas_call(
        scale_kernel,
        grid_spec=pltpu.PrefetchScalarGridSpec(num_scalar_prefetch=1, grid=(r // rb,), in_specs=[row], out_specs=row),
        out_shape=shape((r, d), bf16),
        compiler_params=params(16),
        cost_estimate=cost(r * d, 4 * r * d),
        name="scaled",
    )(gs, x)


def to_units(net, turned, w_down, y, f):
    nd, nf = net.nd, net.nf
    units = w_down.shape[0] // nf
    down = lax.all_to_all(w_down, "fsdp", split_axis=0, concat_axis=1, tiled=True)
    got = []
    for j in range(nd):
        perm = [(a * nf + b, nd * b + (a + j) % nd) for a in range(nd) for b in range(nf)]
        send = lax.dynamic_slice_in_dim(turned, (y + j) % nd * units, units, 0)
        got.append(move(net, send, perm, y, f))
    return got, down


def mix_kernel(idx, *refs, half, nd):
    ups, down, out = refs[:nd], refs[nd], refs[nd + 1]
    units, width = ups[0].shape
    own = lax.rem(idx[0], nd)
    for j, up in enumerate(ups):
        col = pl.multiple_of(lax.rem(own + nd - j, nd) * width, width)
        for at in range(0, units, half):
            out[2 * at : 2 * at + half, pl.ds(col, width)] = up[at : at + half, :]
    for at in range(0, units, half):
        out[2 * at + half : 2 * at + 2 * half, :] = down[at : at + half, :]


def own_units(net, ups, down, half, y, f):
    whole = pl.BlockSpec(memory_space=pltpu.VMEM)
    return pl.pallas_call(
        partial(mix_kernel, half=half, nd=net.nd),
        in_specs=[pl.BlockSpec(memory_space=pltpu.SMEM)] + [whole] * (net.nd + 1),
        out_specs=whole,
        out_shape=shape((2 * down.shape[0], down.shape[1]), bf16),
        compiler_params=params(16),
        cost_estimate=cost(0, 8 * down.size),
        name="own_units",
    )(jnp.stack([y * net.nf + f]).astype(jnp.int32), *ups, down)


def from_units(net, g_up, g_down, y, f):
    nd, nf = net.nd, net.nf
    grad_down = lax.all_to_all(g_down, "fsdp", split_axis=1, concat_axis=0, tiled=True)
    width = g_up.shape[1] // nd
    own = (y * nf + f) % nd
    got = []
    for j in range(nd):
        perm = [(nd * b + (a + j) % nd, a * nf + b) for a in range(nd) for b in range(nf)]
        send = lax.dynamic_slice_in_dim(g_up, (own - j) % nd * width, width, 1)
        got.append(move(net, send, perm, y, f))
    got = jnp.stack(got)
    rows = [lax.dynamic_index_in_dim(got, (h - y) % nd, 0, keepdims=False) for h in range(nd)]
    return jnp.concatenate(rows, axis=0).T.astype(f32), grad_down.astype(f32)


def move(net, x, perm, y, f):
    fixed = [a for a, b in perm if a == b]
    got = lax.ppermute(x, ("dp", "fsdp"), [(a, b) for a, b in perm if a != b])
    me = y * net.nf + f
    stays = False
    for a in fixed:
        stays = stays | (me == a)
    return jnp.where(stays, x, got) if fixed else got


def local(net, frames, skip_in, cond_in, lengths, drop_mask, time_index, w_skip, w_qkv, w_out, w_up, w_down, w_mod, d_out):
    frames, skip_in, cond_in, d_out = frames[0], skip_in[0], cond_in[0], d_out[0]
    rows, d = frames.shape
    nd, nf, na = net.nd, net.nf, net.na
    y, f = lax.axis_index("dp"), lax.axis_index("fsdp")
    utt = lengths.shape[1]
    group_len = rows * nd
    long = int(group_len * LONG_PART)
    rest = group_len - long
    core_bit = ("fsdp", 1)
    n_skip, n_qkv, n_out = w_skip.shape[1], w_qkv.shape[1], w_out.shape[1]
    part_of = lambda n, share: int(n * share) // 16 * 16
    block = net.attn_index()
    moved = ((f & 1) != y if net.regroup else y < 0).astype(jnp.int32)
    me = jnp.stack([y, f, moved, block]).astype(jnp.int32)
    cut = rows // 2
    cols = w_mod.shape[1]

    skip_turned, qkv_turned, out_turned, up_turned = flip(w_skip, w_qkv, w_out, w_up)
    g1 = Gather(net, skip_turned, part_of(n_skip, 0.5))
    g2 = Gather(net, jnp.concatenate([qkv_turned, out_turned], axis=0), part_of(n_qkv + n_out, 0.33))
    lens = jnp.concatenate([lengths, drop_mask], axis=0)
    ints = jnp.concatenate([lengths, drop_mask, time_index], axis=1)
    bits = list(range(net.fb))

    def more_ints():
        nonlocal ints
        if bits:
            ints = jnp.concatenate([ints, net.swap(ints, ("fsdp", 1 << bits.pop(0)))], axis=0)

    def step(g):
        if g.done < g.common:
            g.join()

    def start(g):
        if g.done < g.common:
            g.send()
        else:
            g.raw = []

    while g1.done < g1.common:
        g1.send()
        more_ints()
        g1.raw, (ints, lens), g2.x = tie(g1.raw, [ints, lens], g2.x)
        g1.join()
    g1.send()
    start(g2)
    while bits:
        more_ints()
    g1.raw, g2.raw, (ints, up_turned, w_down) = tie(g1.raw, g2.raw, [ints, up_turned, w_down])
    g1.join()
    step(g2)
    g1.send()
    start(g2)
    up_parts, down = to_units(net, up_turned, w_down, y, f)
    cos, sin, pick, segr, segc, smooth, part, idx, gs = prep(net, ints, me, w_mod, rows, long, rest)
    if net.regroup:
        part = part.reshape(2, nf // 2, utt, cols)
        mod_got = net.swap(lax.dynamic_index_in_dim(part, 1 - y, 0, keepdims=False), ("dp", 1))
        part = lax.dynamic_index_in_dim(part, y, 0, keepdims=False)
    else:
        for b in range(net.db):
            part = part + net.swap(part, ("dp", 1 << b))
        mod_got = part
    g1.raw, g2.raw, (ints, down, part, mod_got), up_parts = tie(
        g1.raw, g2.raw, [ints, down, part, mod_got], up_parts
    )
    g1.join()
    theirs = g1.core(g1.x + g1.far)
    step(g2)
    g2.finish_common()
    g2.send()
    if net.regroup:
        part = jnp.broadcast_to((part + mod_got)[:, None], (nf // 2, 2, utt, cols))
    part = part.reshape(nf, utt, cols)
    mod = lax.all_to_all(part, "fsdp", split_axis=0, concat_axis=2, tiled=True)
    skip_t, = place(net, me, g1, theirs, [n_skip])
    (skip_t, lens), = tie([skip_t, lens])
    hidden0, mixed = skip_fwd(me, lens, frames, skip_in, cond_in, skip_t)
    (hidden0, mixed, mod, down), g2.raw, up_parts = tie([hidden0, mixed, mod, down], g2.raw, up_parts)

    hidden_got = [net.trade(hidden0)]
    g2.join()
    g2.send()
    units = down.shape[0]
    half = units // 2 if units // 2 % 16 == 0 else units
    g3 = Gather(net, own_units(net, up_parts, down, half, y, f), units * 2 if half == units else units)
    start(g3)
    mods = three_terms(mod.reshape(utt, nf * cols))
    mod_a, mod_f = mods[:, : 2 * d], mods[:, 2 * d :]
    (hidden0, mod_a, mod_f, d_out), g2.raw, g3.raw = tie([hidden0, mod_a, mod_f, d_out], g2.raw, g3.raw)
    g2.join()
    theirs = g2.core(g2.x + g2.far)
    qkv_t, out_t = place(net, me, g2, theirs, [n_qkv, n_out])
    step(g3)
    (hidden0, qkv_t, out_t, d_out), hidden_got, g3.x = tie([hidden0, qkv_t, out_t, d_out], hidden_got, g3.x)

    start(g3)
    d_f0 = scaled(d_out, gs)
    d_f_got = [net.trade(d_f0[:cut])]
    hidden, normed_a, sent = qkv_fwd(net, idx, hidden0, hidden_got[0], pick, mod_a, qkv_t, cos, sin)
    sent, g3.raw, d_f_got, (d_f0,) = tie(list(sent), g3.raw, d_f_got, [d_f0])
    step(g3)
    g3.finish_common()
    pieces = [sent[0]] + [net.attn_swap(sent[r], r) for r in range(1, na)]
    pieces, (d_f0,), g3.x = tie(pieces, [d_f0], g3.x)
    g3.send()
    d_f_got.append(net.trade(d_f0[cut:]))
    attn_p, lse = attn_fwd(net, idx, pieces, segr, segc, long)
    (lse,), d_f_got, attn_p, g3.raw = tie([lse], d_f_got, list(attn_p), g3.raw)
    attn_p = [attn_p[0]] + [net.attn_swap(attn_p[r], r) for r in range(1, na)]
    g3.join()
    attn_p, near = tie(attn_p, g3.x)
    g3.send()
    near_core = g3.core(near)
    attn, hidden2, normed_f, d_f = out_fwd(net, idx, attn_p, hidden, pick, mod_f, out_t, d_f0, d_f_got)

    view = lambda x: x.reshape(x.shape[0], 2, x.shape[1] // 2, x.shape[2])
    acc, dx, *got1 = ffn(normed_f, d_f, hidden2, [view(x) for x in near_core + near])
    (acc, dx, mixed, skip_in), far, got1 = tie([acc, dx, mixed, skip_in], g3.raw, got1)
    mixed_got, skip_got = net.trade(mixed), net.trade(skip_in)
    far_core = g3.core(far)
    count = len(far)
    swapped1 = [net.swap(x, core_bit) for x in got1[:count]]
    out_b, dx, *got2 = ffn(normed_f, d_f, acc, [view(x) for x in far_core + far], dx)
    (out_b, dx, mixed_got), got2, swapped1 = tie([out_b, dx, mixed_got], got2, swapped1)
    swapped2 = [net.swap(x, core_bit) for x in got2[:count]]

    d_h2, d_att, sums_f, d_attn_p = out_bwd(net, idx, dx, hidden2, d_f, pick, mod_f[:, d:], out_t)
    (d_h2, d_att, skip_got), d_attn_p, swapped2 = tie([d_h2, d_att, skip_got], list(d_attn_p), swapped2)
    d_attn_p = [d_attn_p[0]] + [net.attn_swap(d_attn_p[r], r) for r in range(1, na)]
    sum_far = [plus(a, b) for a, b in zip(got2[count:], swapped2)]
    d_attn_p, sum_far, (d_att,) = tie(d_attn_p, sum_far, [d_att])
    came = [net.swap(x, o[-2]) for x, o in zip(sum_far, g3.orders)]
    into = outer(net, me, d_att, [attn], n_out, n_qkv + n_out, n_qkv)
    d_attn_p, into, (out_b,) = tie(d_attn_p, list(into), [out_b])

    def send_half(xs, bits):
        n = xs[0].shape[0] // 2
        return [x[:n] for x in xs], [net.swap(x[n:], b) for x, b in zip(xs, bits)]

    all_pairs = d // na // LANES
    pairs = max(1, all_pairs // 2)
    d_sent = attn_bwd(net, idx, pieces, d_attn_p, lse, segr, segc, long, 0, pairs)
    d_sent, came, d_attn_p = tie(list(d_sent), came, d_attn_p)
    d_pieces = [d_sent[0]] + [net.attn_swap(d_sent[r], r) for r in range(1, na)]
    ff = [plus(a, b, c) for a, b, c in zip(got1[count:], swapped1, came)]
    d_attn_p, ff, (out_b,) = tie(d_attn_p, ff, [out_b])
    kept, raw = send_half(ff, [o[-3] for o in g3.orders])
    output_got = net.trade(out_b)
    if all_pairs > pairs:
        d_sent = attn_bwd(net, idx, pieces, d_attn_p, lse, segr, segc, long, pairs, all_pairs - pairs)
        d_sent, (output_got,), raw, d_pieces = tie(list(d_sent), [output_got], raw, d_pieces)
        d_pieces += [d_sent[0]] + [net.attn_swap(d_sent[r], r) for r in range(1, na)]
    ff = jnp.stack([plus(a, b) for a, b in zip(kept, raw)], axis=1)
    common = list(reversed(g3.orders[0][:-3]))
    d_pieces, (ff,) = tie(d_pieces, [ff])
    raw = []
    if common:
        kept, raw = send_half([ff], [common[0]])
    d_qkv = turn_back(net, idx, d_pieces, cos, sin, d)
    d_h, sums_a = qkv_bwd(d_qkv, hidden, d_h2, pick, mod_a[:, d:], qkv_t)
    (d_h, sums_a, d_qkv, output_got), raw = tie([d_h, sums_a, d_qkv, output_got], raw)
    if common:
        ff = plus(kept[0], raw[0])
    raw = []
    if len(common) > 1:
        kept, raw = send_half([ff], [common[1]])
    keep1, send1 = outer(net, me, d_h, [mixed, mixed_got, skip_in, skip_got], n_skip, n_skip, 0, choose=True)
    (keep1, send1, d_qkv, d_h), = tie([keep1, send1, d_qkv, d_h])
    got1 = net.swap(send1, core_bit)
    keep2, send2 = outer(net, me, d_qkv, [normed_a], n_qkv, n_qkv + n_out, 0, into)
    (keep2, send2, keep1, got1), = tie([keep2, send2, keep1, got1])
    got2 = net.swap(send2, core_bit)
    s1 = Sum(net, plus(keep1, got1))
    s1.send()
    (keep2, got2), = tie([keep2, got2])
    s2 = Sum(net, plus(keep2, got2))
    (s2.parts[0][0], s2.parts[1][0], sums_a, d_h, out_b), s1.raw = tie([s2.parts[0][0], s2.parts[1][0], sums_a, d_h, out_b], s1.raw)
    s2.send()
    s1.join()
    s1.send()
    d_h_got = net.trade(d_h)
    output = net.traded(out_b, output_got)

    d_mod = jnp.concatenate([sums_a, sums_f], axis=1).reshape(utt, nf, cols).transpose(1, 0, 2)
    d_mod = lax.all_to_all(d_mod, "fsdp", split_axis=0, concat_axis=0, tiled=True)
    s2.raw, s1.raw, raw, (d_h, d_mod, output) = tie(s2.raw, s1.raw, raw, [d_h, d_mod, output])
    if len(common) > 1:
        ff = plus(kept[0], raw[0])
    for bit in common[2:]:
        kept, raw = send_half([ff], [bit])
        ff = plus(kept[0], raw[0])
    ff = ff.reshape(-1, 2, half, d)
    s2.join()
    s2.send()
    s1.join()
    s1.send()
    grad_up, grad_down = from_units(net, ff[:, 0].reshape(units, d), ff[:, 1].reshape(units, d), y, f)
    s1.raw, s2.raw, (d_h, d_h_got, grad_up, grad_down) = tie(s1.raw, s2.raw, [d_h, d_h_got, grad_up, grad_down])
    s2.join()
    s2.send()
    s1.join()
    if s1.left:
        s1.send()
    d_frames, d_skip = skip_bwd(me, d_h, d_h_got, skip_t)
    s1.raw, s2.raw, (d_frames, d_skip, d_mod) = tie(s1.raw, s2.raw, [d_frames, d_skip, d_mod])
    if net.regroup:
        pair_sum = d_mod.reshape(nf // 2, 2, utt, cols).sum(axis=1)
        here = (jnp.arange(2) == y).astype(f32)
        d_mod = pair_sum[None] * here[:, None, None, None]
    d_mod = d_mod.reshape(nf * utt, cols)
    for b in range(net.db):
        d_mod = d_mod + net.swap(d_mod, ("dp", 1 << b))
    while s2.left:
        s2.join()
        if s1.left:
            s1.join()
        if s2.left:
            s2.send()
        if s1.left:
            s1.send()
        if s1.left and s2.left:
            s1.raw, s2.raw = tie(s1.raw, s2.raw)
    g_two = s2.finish()
    grad_qkv = g_two[:n_qkv].T.astype(f32)
    grad_out = g_two[n_qkv:].T.astype(f32)
    grad_skip = s1.finish().T.astype(f32)
    grad_mod = jnp.dot(smooth.astype(f32).T, d_mod, precision=highest)

    return (output[None], d_frames[None], d_skip[None], grad_skip, grad_qkv, grad_out, grad_up, grad_down, grad_mod)


def solution(mesh):
    rows = P("fsdp", "dp", None)
    ints = P("fsdp", None)
    weight = P("dp", "fsdp")
    return jax.shard_map(
        partial(local, Net(mesh)),
        mesh=mesh,
        in_specs=(rows, rows, rows, ints, ints, ints, *([weight] * 6), rows),
        out_specs=(rows, rows, rows, *([weight] * 6)),
        check_vma=False,
    )
```

profile of v0, /device:TPU:0, one launch (start us, length us, event | category | flops | bytes accessed | tf_op | source)
XLA Modules:
  0.0 657.7 jit_solution(7932577502371490043)
XLA Ops:
  10.7 6.3 collective-permute-done
  82.7 6.9 %all-to-all-start.1 = ((f32[16,8,256]{2,1,0:T(8,128)}), f32[16,8,256]{2,1,0:T(8,128)S(1)}, u32[]{:S(2)}, u32[]{:S(2)}) async-start(f32[16,8,256]{2,1,0:T(8,128)} %bitcast.14), calls=%async_computation.1 | async-start | bytes 262144 | tf_op jit(solution)/shard_map/all_to_all | solution.py:1200
  97.4 10.3 %skip_fwd.1 = (bf16[1024,1024]{1,0:T(8,128)(2,1)}, bf16[1024,1024]{1,0:T(8,128)(2,1)}) custom-call(s32[4]{0:T(128)} %copy-done.19, s32[2,8]{1,0:T(2,128)} %pad_add_fusion.4.lens, bf16[1024,1024]{1,0:T(8,128)(2,1)} %bitcast.146, bf16[1024,1024]{1,0:T(8,128)(2,1)} %bitcast.148, bf16[1024,1024]{1,0:T(8,128)(2,1)} %bitcast.147, bf16[1024,2048]{1,0:T(8,128)(2,1)} %copy-done.4), custom_call_target="tpu_custom_call" | custom-call | flops 4294967296 | bytes 14680064 | tf_op jit(solution)/shard_map/skip_fwd/pallas_call | solution.py:307
  124.9 18.9 %collective-permute-done.23 = bf16[1,256,1024]{2,1,0:T(8,128)(2,1)S(1)} collective-permute-done((bf16[1,256,1024]{2,1,0:T(8,128)(2,1)S(1)}, bf16[1,256,1024]{2,1,0:T(8,128)(2,1)S(1)}, u32[]{:S(2)}, u32[]{:S(2)}) %collective-permute-start.23) | collective-permute-done | bytes 524320 | tf_op jit(solution)/shard_map/ppermute | solution.py:58
  159.7 14.6 %qkv_fwd.1 = (bf16[1024,1024]{1,0:T(8,128)(2,1)}, bf16[1024,1024]{1,0:T(8,128)(2,1)}, bf16[3,1024,512]{2,1,0:T(8,128)(2,1)}, bf16[3,1024,512]{2,1,0:T(8,128)(2,1)}) custom-call(s32[3]{0:T(128)} %copy-done.18, bf16[1024,1024]{1,0:T(8,128)(2,1)} %get-tuple-element.280.hidden0, bf16[1024,1024]{1,0:T(8,128)(2,1)} %collective-permute-done.28.got, ...), custom_call_target="tpu_custom_call" | custom-call | flops 6442450944 | bytes 20971520 | tf_op jit(solution)/shard_map/qkv_fwd/pallas_call | solution.py:378
  174.3 7.1 %collective-permute-done.29 = bf16[2,256,1024]{2,1,0:T(8,128)(2,1)} collective-permute-done((bf16[2,256,1024]{2,1,0:T(8,128)(2,1)}, bf16[2,256,1024]{2,1,0:T(8,128)(2,1)}, u32[]{:S(2)}, u32[]{:S(2)}) %collective-permute-start.29) | collective-permute-done | bytes 1048608 | tf_op jit(solution)/shard_map/ppermute | solution.py:58
  196.2 34.6 %attn_fwd.1 = (bf16[1024,512]{1,0:T(8,128)(2,1)}, bf16[1024,512]{1,0:T(8,128)(2,1)}, f32[4,2,2048]{2,1,0:T(2,128)}) custom-call(s32[3]{0:T(128)} %copy-done.18, bf16[3,1024,512]{2,1,0:T(8,128)(2,1)} %get-tuple-element.296.refs_0_, bf16[3,1024,512]{2,1,0:T(8,128)(2,1)} %copy-done.64, s32[8,512]{1,0:T(8,128)} %copy-done.24, s32[512,128]{1,0:T(8,128)} %copy-done.23), custom_call_target="tpu_custom_call" | custom-call | flops 21474836480 | bytes 8388608 | tf_op jit(solution)/shard_map/attn_fwd/pallas_call | solution.py:825
  237.2 10.9 %out_fwd.1 = (bf16[1024,1024]{1,0:T(8,128)(2,1)}, f32[1024,1024]{1,0:T(8,128)}, bf16[1024,1024]{1,0:T(8,128)(2,1)}, bf16[1024,1024]{1,0:T(8,128)(2,1)}) custom-call(s32[3]{0:T(128)} %copy-done.18, bf16[1024,512]{1,0:T(8,128)(2,1)} %get-tuple-element.310.refs_0_, bf16[1024,512]{1,0:T(8,128)(2,1)} %copy-done.53, ...), custom_call_target="tpu_custom_call" | custom-call | flops 2147483648 | bytes 14680064 | tf_op jit(solution)/shard_map/out_fwd/pallas_call | solution.py:422
  248.1 34.7 %ffn.2 = (f32[1024,1024]{1,0:T(8,128)}, f32[1024,1024]{1,0:T(8,128)}, bf16[8,2,64,1024]{3,2,1,0:T(8,128)(2,1)}, bf16[8,2,64,1024]{3,2,1,0:T(8,128)(2,1)}, bf16[8...) custom-call(bf16[1024,1024]{1,0:T(8,128)(2,1)} %get-tuple-element.317.refs_0_, ...), custom_call_target="tpu_custom_call" | custom-call | flops 25769803776 | bytes 33554432 | tf_op jit(solution)/shard_map/ffn/pallas_call | solution.py:737
  296.5 36.5 %ffn.3 = (bf16[1024,1024]{1,0:T(8,128)(2,1)}, f32[1024,1024]{1,0:T(8,128)}, bf16[8,2,64,1024]{3,2,1,0:T(8,128)(2,1)}, bf16[8,2,64,1024]{3,2,1,0:T(8,128)(2,1)}, ...) custom-call(bf16[1024,1024]{1,0:T(8,128)(2,1)} %get-tuple-element.317.refs_0_, ...), custom_call_target="tpu_custom_call" | custom-call | flops 25769803776 | bytes 33554432 | tf_op jit(solution)/shard_map/ffn/pallas_call | solution.py:737
  335.1 13.0 %out_bwd.1 = (f32[1024,1024]{1,0:T(8,128)}, bf16[1024,1024]{1,0:T(8,128)(2,1)}, f32[8,2048]{1,0:T(8,128)}, bf16[1024,512]{1,0:T(8,128)(2,1)}, bf16[1024,512]{1,0:T(8,128)(2,1)}) custom-call(s32[3]{0:T(128)} %copy-done.18, f32[1024,1024]{1,0:T(8,128)} %get-tuple-element.342.grad, f32[1024,1024]{1,0:T(8,128)} %get-tuple-element.319.refs_2_.hidden2, ...), custom_call_target="tpu_custom_call" | custom-call | flops 2147483648 | bytes 23068672 | tf_op jit(solution)/shard_map/out_bwd/pallas_call | solution.py:487
  356.7 6.2 outer.3
  362.8 38.6 %attn_bwd.2 = (bf16[3,1024,256]{2,1,0:T(8,128)(2,1)}, bf16[3,1024,256]{2,1,0:T(8,128)(2,1)}) custom-call(s32[3]{0:T(128)} %copy-done.18, bf16[3,1024,512]{2,1,0:T(8,128)(2,1)} %get-tuple-element.296.refs_0_, bf16[3,1024,512]{2,1,0:T(8,128)(2,1)} %copy-done.64, bf16[1024,512]{1,0:T(8,128)(2,1)} %get-tuple-element.380.refs_2_, bf16[1024,512]{1,0:T(8,128)(2,1)} %copy-done.67, ...), custom_call_target="tpu_custom_call" | custom-call | flops 26843545600 | bytes 8388608 | tf_op jit(solution)/shard_map/attn_bwd/pallas_call | solution.py:913
  403.4 7.9 %add_convert_fusion.2 = (bf16[8,2,64,1024]{3,2,1,0:T(8,128)(2,1)S(1)}, bf16[8,2,64,1024]{3,2,1,0:T(8,128)(2,1)S(1)}) fusion(bf16[8,2,64,1024]{3,2,1,0:T(8,128)(2,1)} %collective-permute-done.50, bf16[8,2,64,1024]{3,2,1,0:T(8,128)(2,1)} %collective-permute-done.44, bf16[8,2,64,1024]{3,2,1,0:T(8,128)(2,1)} %get-tuple-element.376, ...), kind=kLoop, calls=%fused_computation.2 | loop fusion | flops 12582912 | bytes 16777216 | tf_op jit(solution)/shard_map/convert_element_type | solution.py:116
  419.1 38.3 %attn_bwd.3 = (bf16[3,1024,256]{2,1,0:T(8,128)(2,1)}, bf16[3,1024,256]{2,1,0:T(8,128)(2,1)}) custom-call(s32[3]{0:T(128)} %copy-done.18, bf16[3,1024,512]{2,1,0:T(8,128)(2,1)} %get-tuple-element.296.refs_0_, bf16[3,1024,512]{2,1,0:T(8,128)(2,1)} %copy-done.64, bf16[1024,512]{1,0:T(8,128)(2,1)} %get-tuple-element.380.refs_2_, bf16[1024,512]{1,0:T(8,128)(2,1)} %copy-done.67, ...), custom_call_target="tpu_custom_call" | custom-call | flops 26843545600 | bytes 8388608 | tf_op jit(solution)/shard_map/attn_bwd/pallas_call | solution.py:913
  467.7 8.8 %turn_back.1.d_qkv.g = bf16[1024,3072]{1,0:T(8,128)(2,1)} custom-call(s32[3]{0:T(128)} %copy-done.18, bf16[3,1024,256]{2,1,0:T(8,128)(2,1)} %get-tuple-element.395.refs_0_, bf16[3,1024,256]{2,1,0:T(8,128)(2,1)} %copy-done.44, bf16[3,1024,256]{2,1,0:T(8,128)(2,1)} %get-tuple-element.397.refs_2_, bf16[3,1024,256]{2,1,0:T(8,128)(2,1)} %collective-permute-done.55.refs_3_, ...), custom_call_target="tpu_custom_call" | custom-call | flops 12582912 | bytes 12582912 | tf_op jit(solution)/shard_map/turn_back/pallas_call | solution.py:527
  476.5 16.1 %qkv_bwd.1 = (bf16[1024,1024]{1,0:T(8,128)(2,1)}, f32[8,2048]{1,0:T(8,128)}) custom-call(bf16[1024,3072]{1,0:T(8,128)(2,1)} %turn_back.1.d_qkv.g, bf16[1024,1024]{1,0:T(8,128)(2,1)} %get-tuple-element.312.refs_2_.hidden, f32[1024,1024]{1,0:T(8,128)} %get-tuple-element.399.d_h2, bf16[1024,128]{1,0:T(8,128)(2,1)} %copy-done.6, bf16[128,1024]{1,0:T(8,128)(2,1)} %slice.99.scale, ...), custom_call_target="tpu_custom_call" | custom-call | flops 6442450944 | bytes 23068672 | tf_op jit(solution)/shard_map/qkv_bwd/pallas_call | solution.py:564
  492.6 10.6 %outer.4 = (bf16[8,64,2048]{2,1,0:T(8,128)(2,1)}, bf16[8,64,2048]{2,1,0:T(8,128)(2,1)}) custom-call(s32[4]{0:T(128)} %copy-done.19, bf16[1024,1024]{1,0:T(8,128)(2,1)} %get-tuple-element.446.g.d_h, bf16[1024,1024]{1,0:T(8,128)(2,1)} %get-tuple-element.335.refs_0_, bf16[1024,1024]{1,0:T(8,128)(2,1)} %collective-permute-done.42.refs_1_, ...), custom_call_target="tpu_custom_call" | custom-call | flops 4294967296 | bytes 10485760 | tf_op jit(solution)/shard_map/outer/pallas_call | solution.py:626
  503.2 13.0 %outer.5 = (bf16[8,256,1024]{2,1,0:T(8,128)(2,1)}, bf16[8,256,1024]{2,1,0:T(8,128)(2,1)}) custom-call(s32[4]{0:T(128)} %copy-done.19, bf16[1024,3072]{1,0:T(8,128)(2,1)} %turn_back.1.d_qkv.g, bf16[1024,1024]{1,0:T(8,128)(2,1)} %get-tuple-element.411.refs_0_, ...), custom_call_target="tpu_custom_call", output_to_operand_aliasing={{0}: (3, {}), {1}: (4, {})} | custom-call | flops 6442450944 | bytes 14680064 | tf_op jit(solution)/shard_map/outer/pallas_call | solution.py:626
  564.4 15.5 %collective-permute-done.63 = bf16[2,2,32,1024]{3,2,0,1:T(8,128)(2,1)} collective-permute-done((bf16[2,2,32,1024]{3,2,0,1:T(8,128)(2,1)S(1)}, bf16[2,2,32,1024]{3,2,0,1:T(8,128)(2,1)}, u32[]{:S(2)}, u32[]{:S(2)}) %collective-permute-start.63) | collective-permute-done | bytes 262176 | tf_op jit(solution)/shard_map/ppermute | solution.py:58
  592.0 5.9 all-to-all-start.3
  615.3 6.1 collective-permute-done.68
  630.5 9.6 %skip_bwd.1 = (f32[1024,1024]{1,0:T(8,128)}, f32[1024,1024]{1,0:T(8,128)}) custom-call(s32[4]{0:T(128)} %copy-done.19, bf16[1024,1024]{1,0:T(8,128)(2,1)} %get-tuple-element.446.g.d_h, bf16[1024,1024]{1,0:T(8,128)(2,1)} %collective-permute-done.69.d_h_got, bf16[1024,2048]{1,0:T(8,128)(2,1)} %copy-done.4), custom_call_target="tpu_custom_call" | custom-call | flops 4294967296 | bytes 16777216 | tf_op jit(solution)/shard_map/skip_bwd/pallas_call | solution.py:587
  647.6 8.1 %collective-permute-done.74 = bf16[256,512]{1,0:T(8,128)(2,1)S(1)} collective-permute-done((bf16[256,512]{1,0:T(8,128)(2,1)S(1)}, bf16[256,512]{1,0:T(8,128)(2,1)S(1)}, u32[]{:S(2)}, u32[]{:S(2)}) %collective-permute-start.74) | collective-permute-done | bytes 262176 | tf_op jit(solution)/shard_map/ppermute | solution.py:58
  (398 shorter events, 276.9 us)
Async XLA Ops:
  43.0 30.6 %all-to-all-start = ((bf16[16,128,64]{1,2,0:T(8,128)(2,1)}), bf16[16,128,64]{1,2,0:T(8,128)(2,1)S(1)}, u32[]{:S(2)}, u32[]{:S(2)}) async-start(bf16[16,128,64]{1,2,0:T(8,128)(2,1)} %copy_bitcast_fusion.3), calls=%async_computation | async-start | bytes 524288 | tf_op jit(solution)/shard_map/all_to_all | solution.py:1066
  109.8 34.0 %collective-permute-start.22 = (bf16[8,176,512]{2,1,0:T(8,128)(2,1)S(1)}, bf16[8,176,512]{2,1,0:T(8,128)(2,1)S(1)}, u32[]{:S(2)}, u32[]{:S(2)}) collective-permute-start(bf16[8,176,512]{2,1,0:T(8,128)(2,1)S(1)} %pad_maximum_fusion.4.refs_1_), channel_id=1, source_target_pairs={{0,2},{1,3},{2,0},{3,1},{4,6},{5,7},{6,4},{7,5},{8,10},{9,11},{10,... | collective-permute-start | bytes 4325384 | tf_op jit(solution)/shard_map/ppermute | solution.py:58
  111.0 32.8 %collective-permute-start.21 = (bf16[8,80,512]{2,1,0:T(8,128)(2,1)S(1)}, bf16[8,80,512]{2,1,0:T(8,128)(2,1)}, u32[]{:S(2)}, u32[]{:S(2)}) collective-permute-start(bf16[8,80,512]{2,1,0:T(8,128)(2,1)S(1)} %pad_maximum_fusion.6.refs_0_), channel_id=1, source_target_pairs={{0,16},{16,0},{1,17},{17,1},{2,18},{18,2},{3,19},{19,3},{4,20},{20... | collective-permute-start | bytes 1966088 | tf_op jit(solution)/shard_map/ppermute | solution.py:58
  111.2 44.5 %collective-permute-start.28 = (bf16[1024,1024]{1,0:T(8,128)(2,1)}, bf16[1024,1024]{1,0:T(8,128)(2,1)}, u32[]{:S(2)}, u32[]{:S(2)}) collective-permute-start(bf16[1024,1024]{1,0:T(8,128)(2,1)} %get-tuple-element.280.hidden0), channel_id=1, source_target_pairs={{1,16},{3,18},{5,20},{7,22},{9,24},{11,26},{13,28},{15,30},{16,1},... | collective-permute-start | bytes 6291464 | tf_op jit(solution)/shard_map/ppermute | solution.py:78
  121.0 28.7 %collective-permute-start.25 = (bf16[8,176,512]{2,1,0:T(8,128)(2,1)S(1)}, bf16[8,176,512]{2,1,0:T(8,128)(2,1)S(1)}, u32[]{:S(2)}, u32[]{:S(2)}) collective-permute-start(bf16[8,176,512]{2,1,0:T(8,128)(2,1)S(1)} %pad_maximum_fusion.4.refs_1_), channel_id=1, source_target_pairs={{0,1},{1,0},{2,3},{3,2},{4,5},{5,4},{6,7},{7,6},{8,9},{9,8},{10,11... | collective-permute-start | bytes 4325384 | tf_op jit(solution)/shard_map/ppermute | solution.py:58
  190.5 40.3 %collective-permute-start.32 = (bf16[512,1024]{1,0:T(8,128)(2,1)}, bf16[512,1024]{1,0:T(8,128)(2,1)}, u32[]{:S(2)}, u32[]{:S(2)}) collective-permute-start(bf16[512,1024]{1,0:T(8,128)(2,1)} %slice.91), channel_id=1, source_target_pairs={{1,16},{3,18},{5,20},{7,22},{9,24},{11,26},{13,28},{15,30},{16,1},... | collective-permute-start | bytes 3145736 | tf_op jit(solution)/shard_map/ppermute | solution.py:78
  192.1 38.7 %collective-permute-start.34 = (bf16[4,128,1024]{2,1,0:T(8,128)(2,1)S(1)}, bf16[4,128,1024]{2,1,0:T(8,128)(2,1)S(1)}, u32[]{:S(2)}, u32[]{:S(2)}) collective-permute-start(bf16[4,128,1024]{2,1,0:T(8,128)(2,1)S(1)} %get-tuple-element.490), channel_id=1, source_target_pairs={{0,16},{16,0},{1,17},{17,1},{2,18},{18,2},{3,19},{19,3},{4,20},{20... | collective-permute-start | bytes 3145736 | tf_op jit(solution)/shard_map/ppermute | solution.py:58
  194.3 36.6 %collective-permute-start.33 = (bf16[4,128,1024]{2,1,0:T(8,128)(2,1)}, bf16[4,128,1024]{2,1,0:T(8,128)(2,1)S(1)}, u32[]{:S(2)}, u32[]{:S(2)}) collective-permute-start(bf16[4,128,1024]{2,1,0:T(8,128)(2,1)} %get-tuple-element.491), channel_id=1, source_target_pairs={{0,2},{1,3},{2,0},{3,1},{4,6},{5,7},{6,4},{7,5},{8,10},{9,11},{10,... | collective-permute-start | bytes 3145736 | tf_op jit(solution)/shard_map/ppermute | solution.py:58
  236.3 48.3 %collective-permute-start.39 = (bf16[8,128,1024]{2,1,0:T(8,128)(2,1)}, bf16[8,128,1024]{2,1,0:T(8,128)(2,1)}, u32[]{:S(2)}, u32[]{:S(2)}) collective-permute-start(bf16[8,128,1024]{2,1,0:T(8,128)(2,1)} %pad_maximum_fusion.2), channel_id=1, source_target_pairs={{0,2},{1,3},{2,0},{3,1},{4,6},{5,7},{6,4},{7,5},{8,10},{9,11},{10,... | collective-permute-start | bytes 6291464 | tf_op jit(solution)/shard_map/ppermute | solution.py:58
  236.9 47.8 %collective-permute-start.38 = (bf16[8,128,1024]{2,1,0:T(8,128)(2,1)S(1)}, bf16[8,128,1024]{2,1,0:T(8,128)(2,1)}, u32[]{:S(2)}, u32[]{:S(2)}) collective-permute-start(bf16[8,128,1024]{2,1,0:T(8,128)(2,1)S(1)} %pad_maximum_fusion.1), channel_id=1, source_target_pairs={{0,16},{16,0},{1,17},{17,1},{2,18},{18,2},{3,19},{19,3},{4,20},{20... | collective-permute-start | bytes 6291464 | tf_op jit(solution)/shard_map/ppermute | solution.py:58
  285.3 47.7 %collective-permute-start.43 = (bf16[8,2,64,1024]{3,2,1,0:T(8,128)(2,1)}, bf16[8,2,64,1024]{3,2,1,0:T(8,128)(2,1)S(1)}, u32[]{:S(2)}, u32[]{:S(2)}) collective-permute-start(bf16[8,2,64,1024]{3,2,1,0:T(8,128)(2,1)} %get-tuple-element.340), channel_id=1, source_target_pairs={{0,1},{1,0},{2,3},{3,2},{4,5},{5,4},{6,7},{7,6},{8,9},{9,8},{10,11... | collective-permute-start | bytes 6291464 | tf_op jit(solution)/shard_map/ppermute | solution.py:58
  285.3 47.8 %collective-permute-start.44 = (bf16[8,2,64,1024]{3,2,1,0:T(8,128)(2,1)}, bf16[8,2,64,1024]{3,2,1,0:T(8,128)(2,1)}, u32[]{:S(2)}, u32[]{:S(2)}) collective-permute-start(bf16[8,2,64,1024]{3,2,1,0:T(8,128)(2,1)} %get-tuple-element.341), channel_id=1, source_target_pairs={{0,1},{1,0},{2,3},{3,2},{4,5},{5,4},{6,7},{7,6},{8,9},{9,8},{10,11... | collective-permute-start | bytes 6291464 | tf_op jit(solution)/shard_map/ppermute | solution.py:58
  285.8 47.3 %collective-permute-start.42 = (bf16[1024,1024]{1,0:T(8,128)(2,1)}, bf16[1024,1024]{1,0:T(8,128)(2,1)}, u32[]{:S(2)}, u32[]{:S(2)}) collective-permute-start(bf16[1024,1024]{1,0:T(8,128)(2,1)} %get-tuple-element.335.refs_0_), channel_id=1, source_target_pairs={{1,16},{3,18},{5,20},{7,22},{9,24},{11,26},{13,28},{15,30},{16,1},... | collective-permute-start | bytes 6291464 | tf_op jit(solution)/shard_map/ppermute | solution.py:78
  289.1 59.0 %collective-permute-start.45 = (bf16[1024,1024]{1,0:T(8,128)(2,1)}, bf16[1024,1024]{1,0:T(8,128)(2,1)}, u32[]{:S(2)}, u32[]{:S(2)}) collective-permute-start(bf16[1024,1024]{1,0:T(8,128)(2,1)} %bitcast.149), channel_id=1, source_target_pairs={{1,16},{3,18},{5,20},{7,22},{9,24},{11,26},{13,28},{15,30},{16,1},... | collective-permute-start | bytes 6291464 | tf_op jit(solution)/shard_map/ppermute | solution.py:78
  354.9 48.1 %collective-permute-start.49 = (bf16[8,2,64,1024]{3,2,1,0:T(8,128)(2,1)S(1)}, bf16[8,2,64,1024]{3,2,1,0:T(8,128)(2,1)}, u32[]{:S(2)}, u32[]{:S(2)}) collective-permute-start(bf16[8,2,64,1024]{3,2,1,0:T(8,128)(2,1)S(1)} %add_convert_fusion.5), channel_id=1, source_target_pairs={{0,16},{16,0},{1,17},{17,1},{2,18},{18,2},{3,19},{19,3},{4,20},{20... | collective-permute-start | bytes 6291464 | tf_op jit(solution)/shard_map/ppermute | solution.py:58
  355.3 48.1 %collective-permute-start.50 = (bf16[8,2,64,1024]{3,2,1,0:T(8,128)(2,1)}, bf16[8,2,64,1024]{3,2,1,0:T(8,128)(2,1)}, u32[]{:S(2)}, u32[]{:S(2)}) collective-permute-start(bf16[8,2,64,1024]{3,2,1,0:T(8,128)(2,1)} %add_convert_fusion.4), channel_id=1, source_target_pairs={{0,2},{1,3},{2,0},{3,1},{4,6},{5,7},{6,4},{7,5},{8,10},{9,11},{10,... | collective-permute-start | bytes 6291464 | tf_op jit(solution)/shard_map/ppermute | solution.py:58
  414.0 43.4 %collective-permute-start.53 = (bf16[4,2,64,1024]{3,2,1,0:T(8,128)(2,1)}, bf16[4,2,64,1024]{3,2,1,0:T(8,128)(2,1)}, u32[]{:S(2)}, u32[]{:S(2)}) collective-permute-start(bf16[4,2,64,1024]{3,2,1,0:T(8,128)(2,1)} %slice.96), channel_id=1, source_target_pairs={{0,16},{16,0},{1,17},{17,1},{2,18},{18,2},{3,19},{19,3},{4,20},{20... | collective-permute-start | bytes 3145736 | tf_op jit(solution)/shard_map/ppermute | solution.py:58
  415.7 41.8 %collective-permute-start.52 = (bf16[4,2,64,1024]{3,2,1,0:T(8,128)(2,1)}, bf16[4,2,64,1024]{3,2,1,0:T(8,128)(2,1)}, u32[]{:S(2)}, u32[]{:S(2)}) collective-permute-start(bf16[4,2,64,1024]{3,2,1,0:T(8,128)(2,1)} %slice.95), channel_id=1, source_target_pairs={{0,2},{1,3},{2,0},{3,1},{4,6},{5,7},{6,4},{7,5},{8,10},{9,11},{10,... | collective-permute-start | bytes 3145736 | tf_op jit(solution)/shard_map/ppermute | solution.py:58
  417.1 40.4 %collective-permute-start.54 = (bf16[3,1024,256]{2,1,0:T(8,128)(2,1)}, bf16[3,1024,256]{2,1,0:T(8,128)(2,1)S(1)}, u32[]{:S(2)}, u32[]{:S(2)}) collective-permute-start(bf16[3,1024,256]{2,1,0:T(8,128)(2,1)} %get-tuple-element.388), channel_id=1, source_target_pairs={{0,1},{1,0},{2,3},{3,2},{4,5},{5,4},{6,7},{7,6},{8,9},{9,8},{10,11... | collective-permute-start | bytes 4718600 | tf_op jit(solution)/shard_map/ppermute | solution.py:58
  417.1 40.4 %collective-permute-start.51 = (bf16[1024,1024]{1,0:T(8,128)(2,1)}, bf16[1024,1024]{1,0:T(8,128)(2,1)}, u32[]{:S(2)}, u32[]{:S(2)}) collective-permute-start(bf16[1024,1024]{1,0:T(8,128)(2,1)} %get-tuple-element.435), channel_id=1, source_target_pairs={{1,16},{3,18},{5,20},{7,22},{9,24},{11,26},{13,28},{15,30},{16,1},... | collective-permute-start | bytes 6291464 | tf_op jit(solution)/shard_map/ppermute | solution.py:78
  519.5 43.0 %collective-permute-start.65 = (bf16[1,2,2,64,1024]{4,3,2,0,1:T(8,128)(2,1)}, bf16[1,2,2,64,1024]{4,3,2,0,1:T(8,128)(2,1)}, u32[]{:S(2)}, u32[]{:S(2)}) collective-permute-start(bf16[1,2,2,64,1024]{4,3,2,0,1:T(8,128)(2,1)} %slice.123), channel_id=1, source_target_pairs={{0,8},{1,9},{2,10},{3,11},{4,12},{5,13},{6,14},{7,15},{8,0},{9,1},... | collective-permute-start | bytes 1572872 | tf_op jit(solution)/shard_map/ppermute | solution.py:58
  547.6 34.2 %collective-permute-start.62 = (bf16[2,2,128,1024]{3,2,0,1:T(8,128)(2,1)}, bf16[2,2,128,1024]{3,2,0,1:T(8,128)(2,1)}, u32[]{:S(2)}, u32[]{:S(2)}) collective-permute-start(bf16[2,2,128,1024]{3,2,0,1:T(8,128)(2,1)} %dynamic-slice_bitcast_fusion), channel_id=1, source_target_pairs={{0,2},{1,3},{2,0},{3,1},{4,6},{5,7},{6,4},{7,5},{8,10},{9,11},{10,... | collective-permute-start | bytes 3145736 | tf_op jit(solution)/shard_map/ppermute | solution.py:58
  550.6 31.2 %collective-permute-start.61 = (bf16[2,2,2,128,512]{4,3,0,1,2:T(8,128)(2,1)}, bf16[2,2,2,128,512]{4,3,0,1,2:T(8,128)(2,1)}, u32[]{:S(2)}, u32[]{:S(2)}) collective-permute-start(bf16[2,2,2,128,512]{4,3,0,1,2:T(8,128)(2,1)} %constant_dynamic-slice_fusion.6), channel_id=1, source_target_pairs={{0,16},{16,0},{1,17},{17,1},{2,18},{18,2},{3,19},{19,3},{4,20},{20... | collective-permute-start | bytes 3145736 | tf_op jit(solution)/shard_map/ppermute | solution.py:58
  562.4 61.4 %collective-permute-start.69 = (bf16[1024,1024]{1,0:T(8,128)(2,1)}, bf16[1024,1024]{1,0:T(8,128)(2,1)}, u32[]{:S(2)}, u32[]{:S(2)}) collective-permute-start(bf16[1024,1024]{1,0:T(8,128)(2,1)} %get-tuple-element.446.g.d_h), channel_id=1, source_target_pairs={{1,16},{3,18},{5,20},{7,22},{9,24},{11,26},{13,28},{15,30},{16,1},... | collective-permute-start | bytes 6291464 | tf_op jit(solution)/shard_map/ppermute | solution.py:78
  (124 other events, 1390.8 us)
where the time goes:
time: 668 us; the launch traced here: 658 us
  Pallas kernels  309 us (46%)
  starting transfers between devices  121 us (18%)
  waiting for transfers between devices  104 us (16%)
  other arithmetic  62.7 us (9%)
  local copies, waits for them, and re-layouts  57.7 us (9%)
    ppermute x65, waiting for transfers between devices, swap(): return lax.ppermute(x, axis, [(i, i ^ mask) for i in range(size)])  104 us
    ppermute x65, starting transfers between devices, swap(): return lax.ppermute(x, axis, [(i, i ^ mask) for i in range(size)])  79.5 us
    pallas_call x2, Pallas kernels, attn_bwd(): pl.pallas_call(partial(attn_bwd_kernel, na=na, long=long), grid_spec=pltp...  77 us
    pallas_call x2, Pallas kernels, ffn(): pl.pallas_call(partial(ffn_kernel, steps=steps, second=second), grid=(ste...  71.2 us
    pallas_call x1, Pallas kernels, attn_fwd(): pl.pallas_call(partial(attn_fwd_kernel, na=na, long=long), grid_spec=pltp...  34.6 us
    convert_element_type x17, other arithmetic, plus(): return total.astype(bf16)  34.1 us
    pallas_call x3, Pallas kernels, outer(): pl.pallas_call(partial(outer_kernel, n=n, own=len(xs), choose=choose), gr...  29.7 us
    unnamed x144, local copies, waits for them, and re-layouts  25.8 us
  transfers between devices with their start and end apart: 80, of which 25 were waited for; matrix products, arithmetic and copies ran while one was open for 12% of the time, Pallas kernels for 45%

commit v1 on v0

--- a/solution.py
+++ b/solution.py
@@ -49,7 +49,7 @@
         x, y, core = ("fsdp", 2), ("dp", 1), ("fsdp", 1)
         self.orders = (common + [x, y, core], common + [y, x, core])
         self.regroup = self.nd == 2
-        self.attn_axis = "core" if self.regroup else "dp"
+        self.int_bits = [*range(2, self.fb), 0, 1]
         self.na = 2 if self.regroup else self.nd
 
     def swap(self, x, bit):
@@ -330,10 +330,14 @@
     return x * cos + other * sin if sign > 0 else x * cos - other * sin
 
 
-def chosen(idx, own, got):
+def chosen(idx, own, got, part):
     half = pl.program_id(0) * 2 < pl.num_programs(0)
-    new = jnp.where(half, got[0][...], got[1][...]) if len(got) > 1 else got[0][...]
-    return jnp.where(idx[2] > 0, new, own[...])
+    new = jnp.where(half, got[0][part, :], got[1][part, :]) if len(got) > 1 else got[0][part, :]
+    return jnp.where(idx[2] > 0, new, own[part, :])
+
+
+def parts_of(rows):
+    return (slice(0, rows),)
 
 
 def chosen_specs(rb, d, steps, halves=2):
@@ -351,21 +355,25 @@
     d = hidden.shape[1]
     na = len(pieces)
     hw = d // na
-    h = chosen(idx, hidden0, (got,))
-    hidden[...] = h
-    xh, _ = norm_stats(h.astype(f32))
-    pk = pick[...]
-    y = (xh * (1.0 + dot(pk, mod[:, d:], 1, 0)) + dot(pk, mod[:, :d], 1, 0)).astype(bf16)
-    normed[...] = y
-    for part in range(3):
-        for r in range(na):
-            at = pl.multiple_of(part * d + (idx[0] ^ r) * hw, hw)
-            z = dot(y, w[pl.ds(at, hw), :], 1, 1)
-            if part < 2:
-                z = turn(z, cos[...], sin[...], 1)
-            if part == 0:
-                z = z * (1.0 / math.sqrt(HD))
-            pieces[r][part] = z.astype(bf16)
+    ys = []
+    for rows in parts_of(hidden.shape[0]):
+        h = chosen(idx, hidden0, (got,), rows)
+        hidden[rows, :] = h
+        xh, _ = norm_stats(h.astype(f32))
+        pk = pick[rows, :]
+        y = (xh * (1.0 + dot(pk, mod[:, d:], 1, 0)) + dot(pk, mod[:, :d], 1, 0)).astype(bf16)
+        normed[rows, :] = y
+        ys.append((rows, y))
+    for rows, y in ys:
+        for part in range(3):
+            for r in range(na):
+                at = pl.multiple_of(part * d + (idx[0] ^ r) * hw, hw)
+                z = dot(y, w[pl.ds(at, hw), :], 1, 1)
+                if part < 2:
+                    z = turn(z, cos[rows, :], sin[rows, :], 1)
+                if part == 0:
+                    z = z * (1.0 / math.sqrt(HD))
+                pieces[r][part, rows, :] = z.astype(bf16)
 
 
 def qkv_fwd(net, idx, hidden0, got, pick, mod, w, cos, sin):
@@ -402,15 +410,16 @@
     pieces = refs[:na]
     hidden, pick, mod, w, d_f0, got0, got1, attn, hidden2, normed, d_f = refs[na:]
     d = hidden.shape[1]
-    d_f[...] = chosen(idx, d_f0, (got0, got1))
     hw = d // na
-    for r in range(na):
-        attn[:, pl.ds(pl.multiple_of((idx[0] ^ r) * hw, hw), hw)] = pieces[r][...]
-    h2 = hidden[...].astype(f32) + dot(attn[...], w[...], 1, 1)
-    hidden2[...] = h2
-    xh, _ = norm_stats(h2)
-    pk = pick[...]
-    normed[...] = (xh * (1.0 + dot(pk, mod[:, d:], 1, 0)) + dot(pk, mod[:, :d], 1, 0)).astype(bf16)
+    for rows in parts_of(hidden.shape[0]):
+        d_f[rows, :] = chosen(idx, d_f0, (got0, got1), rows)
+        for r in range(na):
+            attn[rows, pl.ds(pl.multiple_of((idx[0] ^ r) * hw, hw), hw)] = pieces[r][rows, :]
+        h2 = hidden[rows, :].astype(f32) + dot(attn[rows, :], w[...], 1, 1)
+        hidden2[rows, :] = h2
+        xh, _ = norm_stats(h2)
+        pk = pick[rows, :]
+        normed[rows, :] = (xh * (1.0 + dot(pk, mod[:, d:], 1, 0)) + dot(pk, mod[:, :d], 1, 0)).astype(bf16)
 
 
 def out_fwd(net, idx, pieces, hidden, pick, mod, w, d_f0, d_f_got):
@@ -458,15 +467,17 @@
     na = len(refs)
     d = grad.shape[1]
     hw = d // na
-    dx, d_scale, d_shift = norm_back(hidden2[...], grad[...], pick[...], scale[...])
-    dh = d_f[...].astype(f32) + dx
-    d_h2[...] = dh
-    low = dh.astype(bf16)
-    d_att[...] = low
-    hold[...] = dot(low, w[...], 1, 0).astype(bf16)
-    for r in range(na):
-        refs[r][...] = hold[:, pl.ds(pl.multiple_of((idx[0] ^ r) * hw, hw), hw)]
-    both = jnp.concatenate([d_shift, d_scale], axis=1)
+    both = jnp.zeros(sums.shape, f32)
+    for rows in parts_of(grad.shape[0]):
+        dx, d_scale, d_shift = norm_back(hidden2[rows, :], grad[rows, :], pick[rows, :], scale[...])
+        dh = d_f[rows, :].astype(f32) + dx
+        d_h2[rows, :] = dh
+        low = dh.astype(bf16)
+        d_att[rows, :] = low
+        hold[rows, :] = dot(low, w[...], 1, 0).astype(bf16)
+        for r in range(na):
+            refs[r][rows, :] = hold[rows, pl.ds(pl.multiple_of((idx[0] ^ r) * hw, hw), hw)]
+        both = both + jnp.concatenate([d_shift, d_scale], axis=1)
 
     @pl.when(i == 0)
     def _():
@@ -541,10 +552,12 @@
 
 def qkv_bwd_kernel(d_qkv, hidden, d_h2, pick, scale, w, d_h, sums):
     i = pl.program_id(0)
-    grad = dot(d_qkv[...], w[...], 1, 0)
-    dx, d_scale, d_shift = norm_back(hidden[...].astype(f32), grad, pick[...], scale[...])
-    d_h[...] = (d_h2[...] + dx).astype(bf16)
-    both = jnp.concatenate([d_shift, d_scale], axis=1)
+    both = jnp.zeros(sums.shape, f32)
+    for rows in parts_of(hidden.shape[0]):
+        grad = dot(d_qkv[rows, :], w[...], 1, 0)
+        dx, d_scale, d_shift = norm_back(hidden[rows, :].astype(f32), grad, pick[rows, :], scale[...])
+        d_h[rows, :] = (d_h2[rows, :] + dx).astype(bf16)
+        both = both + jnp.concatenate([d_shift, d_scale], axis=1)
 
     @pl.when(i == 0)
     def _():
@@ -573,30 +586,30 @@
     )(d_qkv, hidden, d_h2, pick, scale, w)
 
 
-def skip_bwd_kernel(idx, d_h, d_h_got, w, d_frames, d_skip):
+def skip_bwd_kernel(idx, d_h, got0, got1, w, d_frames, d_skip):
     d = d_h.shape[1]
-    g = jnp.where(idx[2] > 0, d_h_got[...], d_h[...])
+    g = chosen(idx, d_h, (got0, got1), slice(None))
     d_frames[...] = dot(g, w[:, :d], 1, 0)
     d_skip[...] = dot(g, w[:, d:], 1, 0)
 
 
 def skip_bwd(idx, d_h, d_h_got, w):
     r, d = d_h.shape
-    rb = min(256, r)
+    rb = min(256, r // 2)
     row = pl.BlockSpec((rb, d), lambda i, s: (i, 0))
     return pl.pallas_call(
         skip_bwd_kernel,
         grid_spec=pltpu.PrefetchScalarGridSpec(
             num_scalar_prefetch=1,
             grid=(r // rb,),
-            in_specs=[row, row, pl.BlockSpec(w.shape, lambda i, s: (0, 0))],
+            in_specs=chosen_specs(rb, d, r // rb) + [pl.BlockSpec(w.shape, lambda i, s: (0, 0))],
             out_specs=[row, row],
         ),
         out_shape=[shape((r, d), f32)] * 2,
         compiler_params=params(),
         cost_estimate=cost(4 * r * d * d, 12 * r * d + 4 * d * d),
         name="skip_bwd",
-    )(idx, d_h, d_h_got, w)
+    )(idx, d_h, *d_h_got, w)
 
 
 def outer_kernel(idx, g, *refs, n, own, choose):
@@ -931,12 +944,17 @@
     )(idx, *pieces, *d_pieces, lse, segr, segc)
 
 
-def prep_kernel(ints, me, w_mod, cos, sin, pick, segr, segc, smooth, part, idx, gs, *, nd, utt, long, regroup):
+def prep_kernel(ints, me, w_mod, cos, sin, pick, segr, segc, smooth, part, idx, gs, *, nd, utt, long, regroup, bits):
     nf = ints.shape[0]
     rows, rest = cos.shape[0], segr.shape[1]
     total = rows * (2 if regroup else nd)
     y, f, block = me[0], me[1], me[3]
-    mine = ((f & ~1) | y) ^ f if regroup else 0
+
+    def slot(g):
+        r = g ^ f
+        return sum(((r >> b) & 1) << j for j, b in enumerate(bits))
+
+    mine = slot((f & ~1) | y if regroup else f)
     starts, ends, at, first = [], [], 0, 0
     for u in range(utt):
         size = ints[mine, u]
@@ -978,10 +996,11 @@
     d = wide * nd
     row = lax.broadcasted_iota(jnp.int32, (n, LANES), 0)
     when = jnp.zeros((n, LANES), jnp.int32)
+    slots = [slot(g) for g in range(nf)]
     for j in range(n):
         k, u = divmod(j, utt)
         g = 2 * (k % (nf // 2)) + k // (nf // 2) if regroup else k
-        when = jnp.where(row == j, ints[g ^ f, 2 * utt + u], when)
+        when = jnp.where(row == j, ints[slots[g], 2 * utt + u], when)
     flow = 1000.0 * (when[:, :1].astype(f32) / STEPS)
     col = y * wide + lax.broadcasted_iota(jnp.int32, (1, wide), 1)
     low = col < d // 2
@@ -999,7 +1018,7 @@
     smem = pl.BlockSpec(memory_space=pltpu.SMEM)
     vmem = pl.BlockSpec(memory_space=pltpu.VMEM)
     return pl.pallas_call(
-        partial(prep_kernel, nd=net.nd, utt=utt, long=long, regroup=net.regroup),
+        partial(prep_kernel, nd=net.nd, utt=utt, long=long, regroup=net.regroup, bits=tuple(net.int_bits)),
         in_specs=[smem, smem, vmem],
         out_specs=[vmem] * 7 + [smem, smem],
         out_shape=[
@@ -1048,7 +1067,7 @@
 
 def scaled(x, gs):
     r, d = x.shape
-    rb = min(512, r)
+    rb = min(256, r)
     row = pl.BlockSpec((rb, d), lambda i, s: (i, 0))
     return pl.pallas_call(
         scale_kernel,
@@ -1141,11 +1160,10 @@
     cols = w_mod.shape[1]
 
     skip_turned, qkv_turned, out_turned, up_turned = flip(w_skip, w_qkv, w_out, w_up)
-    g1 = Gather(net, skip_turned, part_of(n_skip, 0.5))
     g2 = Gather(net, jnp.concatenate([qkv_turned, out_turned], axis=0), part_of(n_qkv + n_out, 0.33))
     lens = jnp.concatenate([lengths, drop_mask], axis=0)
     ints = jnp.concatenate([lengths, drop_mask, time_index], axis=1)
-    bits = list(range(net.fb))
+    bits = net.int_bits[:]
 
     def more_ints():
         nonlocal ints
@@ -1162,10 +1180,11 @@
         else:
             g.raw = []
 
+    g1 = Gather(net, skip_turned, part_of(n_skip, 0.5))
     while g1.done < g1.common:
         g1.send()
         more_ints()
-        g1.raw, (ints, lens), g2.x = tie(g1.raw, [ints, lens], g2.x)
+        g1.raw, (ints, lens, up_turned, w_down), g2.x = tie(g1.raw, [ints, lens, up_turned, w_down], g2.x)
         g1.join()
     g1.send()
     start(g2)
@@ -1186,38 +1205,36 @@
         for b in range(net.db):
             part = part + net.swap(part, ("dp", 1 << b))
         mod_got = part
-    g1.raw, g2.raw, (ints, down, part, mod_got), up_parts = tie(
-        g1.raw, g2.raw, [ints, down, part, mod_got], up_parts
-    )
+    g1.raw, g2.raw, (ints, part, mod_got, down) = tie(g1.raw, g2.raw, [ints, part, mod_got, down])
     g1.join()
     theirs = g1.core(g1.x + g1.far)
     step(g2)
     g2.finish_common()
     g2.send()
+    skip_t, = place(net, me, g1, theirs, [n_skip])
+    (skip_t, lens, part, mod_got, down), up_parts = tie([skip_t, lens, part, mod_got, down], up_parts)
+    units = down.shape[0]
+    half = units // 2 if units // 2 % 16 == 0 else units
+    g3 = Gather(net, own_units(net, up_parts, down, half, y, f), units * 2 if half == units else units)
+    start(g3)
+    hidden0, mixed = skip_fwd(me, lens, frames, skip_in, cond_in, skip_t)
+    (hidden0, mixed, part, mod_got), g2.raw = tie([hidden0, mixed, part, mod_got], g2.raw)
+
+    hidden_got = [net.trade(hidden0)]
+    g2.join()
+    g2.send()
     if net.regroup:
         part = jnp.broadcast_to((part + mod_got)[:, None], (nf // 2, 2, utt, cols))
     part = part.reshape(nf, utt, cols)
     mod = lax.all_to_all(part, "fsdp", split_axis=0, concat_axis=2, tiled=True)
-    skip_t, = place(net, me, g1, theirs, [n_skip])
-    (skip_t, lens), = tie([skip_t, lens])
-    hidden0, mixed = skip_fwd(me, lens, frames, skip_in, cond_in, skip_t)
-    (hidden0, mixed, mod, down), g2.raw, up_parts = tie([hidden0, mixed, mod, down], g2.raw, up_parts)
-
-    hidden_got = [net.trade(hidden0)]
-    g2.join()
-    g2.send()
-    units = down.shape[0]
-    half = units // 2 if units // 2 % 16 == 0 else units
-    g3 = Gather(net, own_units(net, up_parts, down, half, y, f), units * 2 if half == units else units)
-    start(g3)
+    (hidden0, mod, d_out), g2.raw, g3.raw = tie([hidden0, mod, d_out], g2.raw, g3.raw)
     mods = three_terms(mod.reshape(utt, nf * cols))
     mod_a, mod_f = mods[:, : 2 * d], mods[:, 2 * d :]
-    (hidden0, mod_a, mod_f, d_out), g2.raw, g3.raw = tie([hidden0, mod_a, mod_f, d_out], g2.raw, g3.raw)
     g2.join()
     theirs = g2.core(g2.x + g2.far)
     qkv_t, out_t = place(net, me, g2, theirs, [n_qkv, n_out])
     step(g3)
-    (hidden0, qkv_t, out_t, d_out), hidden_got, g3.x = tie([hidden0, qkv_t, out_t, d_out], hidden_got, g3.x)
+    (hidden0, qkv_t, out_t, d_out, mod_a, mod_f), hidden_got, g3.x = tie([hidden0, qkv_t, out_t, d_out, mod_a, mod_f], hidden_got, g3.x)
 
     start(g3)
     d_f0 = scaled(d_out, gs)
@@ -1242,9 +1259,10 @@
     view = lambda x: x.reshape(x.shape[0], 2, x.shape[1] // 2, x.shape[2])
     acc, dx, *got1 = ffn(normed_f, d_f, hidden2, [view(x) for x in near_core + near])
     (acc, dx, mixed, skip_in), far, got1 = tie([acc, dx, mixed, skip_in], g3.raw, got1)
-    mixed_got, skip_got = net.trade(mixed), net.trade(skip_in)
     far_core = g3.core(far)
     count = len(far)
+    far_core, got1, (mixed, skip_in) = tie(far_core, got1, [mixed, skip_in])
+    mixed_got, skip_got = net.trade(mixed), net.trade(skip_in)
     swapped1 = [net.swap(x, core_bit) for x in got1[:count]]
     out_b, dx, *got2 = ffn(normed_f, d_f, acc, [view(x) for x in far_core + far], dx)
     (out_b, dx, mixed_got), got2, swapped1 = tie([out_b, dx, mixed_got], got2, swapped1)
@@ -1300,35 +1318,35 @@
     s1.send()
     (keep2, got2), = tie([keep2, got2])
     s2 = Sum(net, plus(keep2, got2))
-    (s2.parts[0][0], s2.parts[1][0], sums_a, d_h, out_b), s1.raw = tie([s2.parts[0][0], s2.parts[1][0], sums_a, d_h, out_b], s1.raw)
+    (s2.parts[0][0], s2.parts[1][0], sums_a, d_h, out_b), s1.raw = tie(
+        [s2.parts[0][0], s2.parts[1][0], sums_a, d_h, out_b], s1.raw
+    )
     s2.send()
     s1.join()
     s1.send()
-    d_h_got = net.trade(d_h)
-    output = net.traded(out_b, output_got)
-
-    d_mod = jnp.concatenate([sums_a, sums_f], axis=1).reshape(utt, nf, cols).transpose(1, 0, 2)
-    d_mod = lax.all_to_all(d_mod, "fsdp", split_axis=0, concat_axis=0, tiled=True)
-    s2.raw, s1.raw, raw, (d_h, d_mod, output) = tie(s2.raw, s1.raw, raw, [d_h, d_mod, output])
+    s1.raw, raw, (out_b, d_h) = tie(s1.raw, raw, [out_b, d_h])
     if len(common) > 1:
         ff = plus(kept[0], raw[0])
     for bit in common[2:]:
         kept, raw = send_half([ff], [bit])
         ff = plus(kept[0], raw[0])
     ff = ff.reshape(-1, 2, half, d)
-    s2.join()
-    s2.send()
     s1.join()
     s1.send()
+    output = net.traded(out_b, output_got)
     grad_up, grad_down = from_units(net, ff[:, 0].reshape(units, d), ff[:, 1].reshape(units, d), y, f)
-    s1.raw, s2.raw, (d_h, d_h_got, grad_up, grad_down) = tie(s1.raw, s2.raw, [d_h, d_h_got, grad_up, grad_down])
+    s1.raw, s2.raw, (sums_a, output, grad_up, grad_down, d_h) = tie(s1.raw, s2.raw, [sums_a, output, grad_up, grad_down, d_h])
+    d_h_got = [net.trade(d_h[:cut])]
     s2.join()
     s2.send()
     s1.join()
     if s1.left:
         s1.send()
-    d_frames, d_skip = skip_bwd(me, d_h, d_h_got, skip_t)
-    s1.raw, s2.raw, (d_frames, d_skip, d_mod) = tie(s1.raw, s2.raw, [d_frames, d_skip, d_mod])
+
+    d_mod = jnp.concatenate([sums_a, sums_f], axis=1).reshape(utt, nf, cols).transpose(1, 0, 2)
+    d_mod = lax.all_to_all(d_mod, "fsdp", split_axis=0, concat_axis=0, tiled=True)
+    s1.raw, s2.raw, (d_mod, d_h), d_h_got = tie(s1.raw, s2.raw, [d_mod, d_h], d_h_got)
+    d_h_got.append(net.trade(d_h[cut:]))
     if net.regroup:
         pair_sum = d_mod.reshape(nf // 2, 2, utt, cols).sum(axis=1)
         here = (jnp.arange(2) == y).astype(f32)
@@ -1345,7 +1363,10 @@
         if s1.left:
             s1.send()
         if s1.left and s2.left:
-            s1.raw, s2.raw = tie(s1.raw, s2.raw)
+            s1.raw, s2.raw, d_h_got = tie(s1.raw, s2.raw, d_h_got)
+        elif s2.left == 2:
+            s2.raw, d_h_got = tie(s2.raw, d_h_got)
+    d_frames, d_skip = skip_bwd(me, d_h, d_h_got, skip_t)
     g_two = s2.finish()
     grad_qkv = g_two[:n_qkv].T.astype(f32)
     grad_out = g_two[n_qkv:].T.astype(f32)

time: 668 us -> 648 us (0.970)
  starting transfers between devices: 121 us -> 105 us
  waiting for transfers between devices: 104 us -> 114 us
  local copies, waits for them, and re-layouts: 57.7 us -> 49.1 us
  other arithmetic: 62.7 us -> 55.9 us
    ppermute x65, waiting for transfers between devices: 104 us -> 80.8 us  [swap(): return lax.ppermute(x, axis, [(i, i ^ mask) for i in range(size)])]
    ppermute x65, starting transfers between devices: 79.5 us -> 62 us  [swap(): return lax.ppermute(x, axis, [(i, i ^ mask) for i in range(size)])]
    all_to_all x1, waiting for transfers between devices: 0.01 us -> 17.4 us  [local(): mod = lax.all_to_all(part, 'fsdp', split_axis=0, concat_axis=2, tiled=True)]
    ppermute x4, waiting for transfers between devices: 0.01 us -> 15.5 us  [move(): got = lax.ppermute(x, ('dp', 'fsdp'), [(a, b) for a, b in perm if a != b])]
    unnamed x144 -> x126, local copies, waits for them, and re-layouts: 25.8 us -> 23.6 us
    ppermute x7 -> x8, starting transfers between devices: 13.6 us -> 13.8 us  [trade(): return lax.ppermute(x, ('dp', 'fsdp'), perm)]
  transfers between devices with their start and end apart: 80 -> 81, of which waited for: 25 -> 29; matrix products, arithmetic and copies ran while one was open for 12% -> 10% of each run, Pallas kernels for 45% -> 47%
where the time goes in v1:
time: 648 us; the launch traced here: 638 us
  Pallas kernels  310 us (48%)
  waiting for transfers between devices  114 us (18%)
  starting transfers between devices  105 us (16%)
  other arithmetic  55.9 us (9%)
  local copies, waits for them, and re-layouts  49.1 us (8%)
    ppermute x65, waiting for transfers between devices, swap(): return lax.ppermute(x, axis, [(i, i ^ mask) for i in range(size)])  80.8 us
    pallas_call x2, Pallas kernels, attn_bwd(): pl.pallas_call(partial(attn_bwd_kernel, na=na, long=long), grid_spec=pltp...  77 us
    pallas_call x2, Pallas kernels, ffn(): pl.pallas_call(partial(ffn_kernel, steps=steps, second=second), grid=(ste...  71.4 us
    ppermute x65, starting transfers between devices, swap(): return lax.ppermute(x, axis, [(i, i ^ mask) for i in range(size)])  62 us
    pallas_call x1, Pallas kernels, attn_fwd(): pl.pallas_call(partial(attn_fwd_kernel, na=na, long=long), grid_spec=pltp...  34.6 us
    pallas_call x3, Pallas kernels, outer(): pl.pallas_call(partial(outer_kernel, n=n, own=len(xs), choose=choose), gr...  29.7 us
    convert_element_type x17, other arithmetic, plus(): return total.astype(bf16)  28.3 us
    unnamed x126, local copies, waits for them, and re-layouts  23.6 us
  transfers between devices with their start and end apart: 81, of which 29 were waited for; matrix products, arithmetic and copies ran while one was open for 10% of the time, Pallas kernels for 47%

profile of v1, /device:TPU:0, one launch (start us, length us, event | category | flops | bytes accessed | tf_op | source)
XLA Modules:
  0.0 638.0 jit_solution(3205836424626965445)
XLA Ops:
  35.1 7.3 %collective-permute-done.6 = bf16[1,256,512]{2,1,0:T(8,128)(2,1)S(1)} collective-permute-done((bf16[1,256,512]{2,1,0:T(8,128)(2,1)S(1)}, bf16[1,256,512]{2,1,0:T(8,128)(2,1)S(1)}, u32[]{:S(2)}, u32[]{:S(2)}) %collective-permute-start.6) | collective-permute-done | bytes 262176 | tf_op jit(solution)/shard_map/ppermute | solution.py:58
  86.6 6.6 %collective-permute-done.18.refs_1_ = bf16[128,512]{1,0:T(8,128)(2,1)S(1)} collective-permute-done((bf16[128,512]{1,0:T(8,128)(2,1)}, bf16[128,512]{1,0:T(8,128)(2,1)S(1)}, u32[]{:S(2)}, u32[]{:S(2)}) %collective-permute-start.18) | collective-permute-done | bytes 131104 | tf_op jit(solution)/shard_map/ppermute | solution.py:1136
  93.8 10.3 %skip_fwd.1 = (bf16[1024,1024]{1,0:T(8,128)(2,1)}, bf16[1024,1024]{1,0:T(8,128)(2,1)}) custom-call(s32[4]{0:T(128)} %copy-done.16, s32[2,8]{1,0:T(2,128)} %pad_add_fusion.4.lens, bf16[1024,1024]{1,0:T(8,128)(2,1)} %bitcast.146, bf16[1024,1024]{1,0:T(8,128)(2,1)} %bitcast.148, bf16[1024,1024]{1,0:T(8,128)(2,1)} %bitcast.147, bf16[1024,2048]{1,0:T(8,128)(2,1)} %copy-done.4), custom_call_target="tpu_custom_call" | custom-call | flops 4294967296 | bytes 14680064 | tf_op jit(solution)/shard_map/skip_fwd/pallas_call | solution.py:307
  112.4 7.3 %all-to-all-start.1 = ((f32[16,8,256]{2,1,0:T(8,128)}), f32[16,8,256]{2,1,0:T(8,128)S(1)}, u32[]{:S(2)}, u32[]{:S(2)}) async-start(f32[16,8,256]{2,1,0:T(8,128)} %bitcast.14), calls=%async_computation.1 | async-start | bytes 262144 | tf_op jit(solution)/shard_map/all_to_all | solution.py:1229
  120.3 17.4 %all-to-all-done.1 = f32[16,8,256]{2,1,0:T(8,128)S(1)} async-done(((f32[16,8,256]{2,1,0:T(8,128)}), f32[16,8,256]{2,1,0:T(8,128)S(1)}, u32[]{:S(2)}, u32[]{:S(2)}) %all-to-all-start.1) | async-done | bytes 131104 | tf_op jit(solution)/shard_map/all_to_all | solution.py:1229
  153.1 14.6 %qkv_fwd.1 = (bf16[1024,1024]{1,0:T(8,128)(2,1)}, bf16[1024,1024]{1,0:T(8,128)(2,1)}, bf16[3,1024,512]{2,1,0:T(8,128)(2,1)}, bf16[3,1024,512]{2,1,0:T(8,128)(2,1)}) custom-call(s32[3]{0:T(128)} %copy-done.15, bf16[1024,1024]{1,0:T(8,128)(2,1)} %get-tuple-element.302.hidden0, bf16[1024,1024]{1,0:T(8,128)(2,1)} %collective-permute-done.28.got, ...), custom_call_target="tpu_custom_call" | custom-call | flops 6442450944 | bytes 20971520 | tf_op jit(solution)/shard_map/qkv_fwd/pallas_call | solution.py:386
  167.7 7.2 %collective-permute-done.29 = bf16[2,256,1024]{2,1,0:T(8,128)(2,1)} collective-permute-done((bf16[2,256,1024]{2,1,0:T(8,128)(2,1)}, bf16[2,256,1024]{2,1,0:T(8,128)(2,1)}, u32[]{:S(2)}, u32[]{:S(2)}) %collective-permute-start.29) | collective-permute-done | bytes 1048608 | tf_op jit(solution)/shard_map/ppermute | solution.py:58
  188.4 34.6 %attn_fwd.1 = (bf16[1024,512]{1,0:T(8,128)(2,1)}, bf16[1024,512]{1,0:T(8,128)(2,1)}, f32[4,2,2048]{2,1,0:T(2,128)}) custom-call(s32[3]{0:T(128)} %copy-done.15, bf16[3,1024,512]{2,1,0:T(8,128)(2,1)} %get-tuple-element.318.refs_0_, bf16[3,1024,512]{2,1,0:T(8,128)(2,1)} %copy-done.54, s32[8,512]{1,0:T(8,128)} %copy-done.21, s32[512,128]{1,0:T(8,128)} %copy-done.20), custom_call_target="tpu_custom_call" | custom-call | flops 21474836480 | bytes 8388608 | tf_op jit(solution)/shard_map/attn_fwd/pallas_call | solution.py:838
  230.1 11.0 %out_fwd.1 = (bf16[1024,1024]{1,0:T(8,128)(2,1)}, f32[1024,1024]{1,0:T(8,128)}, bf16[1024,1024]{1,0:T(8,128)(2,1)}, bf16[1024,1024]{1,0:T(8,128)(2,1)}) custom-call(s32[3]{0:T(128)} %copy-done.15, bf16[1024,512]{1,0:T(8,128)(2,1)} %get-tuple-element.332.refs_0_, bf16[1024,512]{1,0:T(8,128)(2,1)} %copy-done.46, ...), custom_call_target="tpu_custom_call" | custom-call | flops 2147483648 | bytes 14680064 | tf_op jit(solution)/shard_map/out_fwd/pallas_call | solution.py:431
  241.0 34.7 %ffn.2 = (f32[1024,1024]{1,0:T(8,128)}, f32[1024,1024]{1,0:T(8,128)}, bf16[8,2,64,1024]{3,2,1,0:T(8,128)(2,1)}, bf16[8,2,64,1024]{3,2,1,0:T(8,128)(2,1)}, bf16[8...) custom-call(bf16[1024,1024]{1,0:T(8,128)(2,1)} %get-tuple-element.339.refs_0_, ...), custom_call_target="tpu_custom_call" | custom-call | flops 25769803776 | bytes 33554432 | tf_op jit(solution)/shard_map/ffn/pallas_call | solution.py:750
  289.8 36.7 %ffn.3 = (bf16[1024,1024]{1,0:T(8,128)(2,1)}, f32[1024,1024]{1,0:T(8,128)}, bf16[8,2,64,1024]{3,2,1,0:T(8,128)(2,1)}, bf16[8,2,64,1024]{3,2,1,0:T(8,128)(2,1)}, ...) custom-call(bf16[1024,1024]{1,0:T(8,128)(2,1)} %get-tuple-element.339.refs_0_, ...), custom_call_target="tpu_custom_call" | custom-call | flops 25769803776 | bytes 33554432 | tf_op jit(solution)/shard_map/ffn/pallas_call | solution.py:750
  329.1 13.0 %out_bwd.1 = (f32[1024,1024]{1,0:T(8,128)}, bf16[1024,1024]{1,0:T(8,128)(2,1)}, f32[8,2048]{1,0:T(8,128)}, bf16[1024,512]{1,0:T(8,128)(2,1)}, bf16[1024,512]{1,0:T(8,128)(2,1)}) custom-call(s32[3]{0:T(128)} %copy-done.15, f32[1024,1024]{1,0:T(8,128)} %get-tuple-element.372.grad, f32[1024,1024]{1,0:T(8,128)} %get-tuple-element.341.refs_2_.hidden2, ...), custom_call_target="tpu_custom_call" | custom-call | flops 2147483648 | bytes 23068672 | tf_op jit(solution)/shard_map/out_bwd/pallas_call | solution.py:498
  357.0 38.4 %attn_bwd.2 = (bf16[3,1024,256]{2,1,0:T(8,128)(2,1)}, bf16[3,1024,256]{2,1,0:T(8,128)(2,1)}) custom-call(s32[3]{0:T(128)} %copy-done.15, bf16[3,1024,512]{2,1,0:T(8,128)(2,1)} %get-tuple-element.318.refs_0_, bf16[3,1024,512]{2,1,0:T(8,128)(2,1)} %copy-done.54, bf16[1024,512]{1,0:T(8,128)(2,1)} %get-tuple-element.410.refs_2_, bf16[1024,512]{1,0:T(8,128)(2,1)} %copy-done.57, ...), custom_call_target="tpu_custom_call" | custom-call | flops 26843545600 | bytes 8388608 | tf_op jit(solution)/shard_map/attn_bwd/pallas_call | solution.py:926
  398.2 7.9 %add_convert_fusion.2 = (bf16[8,2,64,1024]{3,2,1,0:T(8,128)(2,1)S(1)}, bf16[8,2,64,1024]{3,2,1,0:T(8,128)(2,1)S(1)}) fusion(bf16[8,2,64,1024]{3,2,1,0:T(8,128)(2,1)} %collective-permute-done.50, bf16[8,2,64,1024]{3,2,1,0:T(8,128)(2,1)} %collective-permute-done.44, bf16[8,2,64,1024]{3,2,1,0:T(8,128)(2,1)} %get-tuple-element.406, ...), kind=kLoop, calls=%fused_computation.2 | loop fusion | flops 12582912 | bytes 16777216 | tf_op jit(solution)/shard_map/convert_element_type | solution.py:116
  412.9 38.5 %attn_bwd.3 = (bf16[3,1024,256]{2,1,0:T(8,128)(2,1)}, bf16[3,1024,256]{2,1,0:T(8,128)(2,1)}) custom-call(s32[3]{0:T(128)} %copy-done.15, bf16[3,1024,512]{2,1,0:T(8,128)(2,1)} %get-tuple-element.318.refs_0_, bf16[3,1024,512]{2,1,0:T(8,128)(2,1)} %copy-done.54, bf16[1024,512]{1,0:T(8,128)(2,1)} %get-tuple-element.410.refs_2_, bf16[1024,512]{1,0:T(8,128)(2,1)} %copy-done.57, ...), custom_call_target="tpu_custom_call" | custom-call | flops 26843545600 | bytes 8388608 | tf_op jit(solution)/shard_map/attn_bwd/pallas_call | solution.py:926
  462.2 8.7 %turn_back.1.d_qkv.g = bf16[1024,3072]{1,0:T(8,128)(2,1)} custom-call(s32[3]{0:T(128)} %copy-done.15, bf16[3,1024,256]{2,1,0:T(8,128)(2,1)} %get-tuple-element.425.refs_0_, bf16[3,1024,256]{2,1,0:T(8,128)(2,1)} %copy-done.36, bf16[3,1024,256]{2,1,0:T(8,128)(2,1)} %get-tuple-element.427.refs_2_, bf16[3,1024,256]{2,1,0:T(8,128)(2,1)} %collective-permute-done.55.refs_3_, ...), custom_call_target="tpu_custom_call" | custom-call | flops 12582912 | bytes 12582912 | tf_op jit(solution)/shard_map/turn_back/pallas_call | solution.py:538
  470.9 16.1 %qkv_bwd.1 = (bf16[1024,1024]{1,0:T(8,128)(2,1)}, f32[8,2048]{1,0:T(8,128)}) custom-call(bf16[1024,3072]{1,0:T(8,128)(2,1)} %turn_back.1.d_qkv.g, bf16[1024,1024]{1,0:T(8,128)(2,1)} %get-tuple-element.334.refs_2_.hidden, f32[1024,1024]{1,0:T(8,128)} %get-tuple-element.429.d_h2, bf16[1024,128]{1,0:T(8,128)(2,1)} %copy-done.6, ...), custom_call_target="tpu_custom_call" | custom-call | flops 6442450944 | bytes 23068672 | tf_op jit(solution)/shard_map/qkv_bwd/pallas_call | solution.py:577
  487.0 10.6 %outer.4 = (bf16[8,64,2048]{2,1,0:T(8,128)(2,1)}, bf16[8,64,2048]{2,1,0:T(8,128)(2,1)}) custom-call(s32[4]{0:T(128)} %copy-done.16, bf16[1024,1024]{1,0:T(8,128)(2,1)} %get-tuple-element.477.g.d_h, bf16[1024,1024]{1,0:T(8,128)(2,1)} %get-tuple-element.365.refs_0_, bf16[1024,1024]{1,0:T(8,128)(2,1)} %collective-permute-done.42.refs_1_, ...), custom_call_target="tpu_custom_call" | custom-call | flops 4294967296 | bytes 10485760 | tf_op jit(solution)/shard_map/outer/pallas_call | solution.py:639
  497.6 13.0 %outer.5 = (bf16[8,256,1024]{2,1,0:T(8,128)(2,1)}, bf16[8,256,1024]{2,1,0:T(8,128)(2,1)}) custom-call(s32[4]{0:T(128)} %copy-done.16, bf16[1024,3072]{1,0:T(8,128)(2,1)} %turn_back.1.d_qkv.g, bf16[1024,1024]{1,0:T(8,128)(2,1)} %get-tuple-element.441.refs_0_, ...), custom_call_target="tpu_custom_call", output_to_operand_aliasing={{0}: (3, {}), {1}: (4, {})} | custom-call | flops 6442450944 | bytes 14680064 | tf_op jit(solution)/shard_map/outer/pallas_call | solution.py:639
  557.2 8.9 %collective-permute-done.68 = bf16[128,512]{1,0:T(8,128)(2,1)} collective-permute-done((bf16[128,512]{1,0:T(8,128)(2,1)}, bf16[128,512]{1,0:T(8,128)(2,1)}, u32[]{:S(2)}, u32[]{:S(2)}) %collective-permute-start.68) | collective-permute-done | bytes 131104 | tf_op jit(solution)/shard_map/ppermute | solution.py:1136
  580.5 7.9 %all-to-all-start.3 = ((f32[16,8,256]{2,1,0:T(8,128)}), f32[16,8,256]{2,1,0:T(8,128)S(1)}, u32[]{:S(2)}, u32[]{:S(2)}) async-start(f32[16,8,256]{2,1,0:T(8,128)} %bitcast.54), calls=%async_computation.3 | async-start | bytes 262144 | tf_op jit(solution)/shard_map/all_to_all | solution.py:1347
  593.6 7.3 %collective-permute-done.69 = bf16[64,1024]{1,0:T(8,128)(2,1)S(1)} collective-permute-done((bf16[64,1024]{1,0:T(8,128)(2,1)S(1)}, bf16[64,1024]{1,0:T(8,128)(2,1)S(1)}, u32[]{:S(2)}, u32[]{:S(2)}) %collective-permute-start.69) | collective-permute-done | bytes 131104 | tf_op jit(solution)/shard_map/ppermute | solution.py:58
  608.7 13.1 %collective-permute-done.76 = f32[128,256]{1,0:T(8,128)S(1)} collective-permute-done((f32[128,256]{1,0:T(8,128)S(1)}, f32[128,256]{1,0:T(8,128)S(1)}, u32[]{:S(2)}, u32[]{:S(2)}) %collective-permute-start.76) | collective-permute-done | bytes 131104 | tf_op jit(solution)/shard_map/ppermute | solution.py:58
  624.2 10.1 %skip_bwd.1 = (f32[1024,1024]{1,0:T(8,128)}, f32[1024,1024]{1,0:T(8,128)}) custom-call(s32[4]{0:T(128)} %copy-done.16, bf16[1024,1024]{1,0:T(8,128)(2,1)} %get-tuple-element.477.g.d_h, bf16[512,1024]{1,0:T(8,128)(2,1)} %collective-permute-done.72.got0, bf16[512,1024]{1,0:T(8,128)(2,1)} %copy-done.58, bf16[1024,2048]{1,0:T(8,128)(2,1)} %copy-done.4), custom_call_target="tpu_custom_call" | custom-call | flops 4294967296 | bytes 16777216 | tf_op jit(solution)/shard_map/skip_bwd/pallas_call | solution.py:600
  (384 shorter events, 254.9 us)
Async XLA Ops:
  73.0 31.0 %collective-permute-start.20 = (bf16[4,176,512]{2,1,0:T(8,128)(2,1)}, bf16[4,176,512]{2,1,0:T(8,128)(2,1)}, u32[]{:S(2)}, u32[]{:S(2)}) collective-permute-start(bf16[4,176,512]{2,1,0:T(8,128)(2,1)} %slice.123), channel_id=1, source_target_pairs={{0,16},{16,0},{1,17},{17,1},{2,18},{18,2},{3,19},{19,3},{4,20},{20... | collective-permute-start | bytes 2162696 | tf_op jit(solution)/shard_map/ppermute | solution.py:58
  76.4 27.6 %collective-permute-start.19 = (bf16[4,80,512]{2,1,0:T(8,128)(2,1)S(1)}, bf16[4,80,512]{2,1,0:T(8,128)(2,1)}, u32[]{:S(2)}, u32[]{:S(2)}) collective-permute-start(bf16[4,80,512]{2,1,0:T(8,128)(2,1)S(1)} %slice.122), channel_id=1, source_target_pairs={{0,2},{1,3},{2,0},{3,1},{4,6},{5,7},{6,4},{7,5},{8,10},{9,11},{10,... | collective-permute-start | bytes 983048 | tf_op jit(solution)/shard_map/ppermute | solution.py:58
  105.6 32.1 %collective-permute-start.22 = (bf16[8,176,512]{2,1,0:T(8,128)(2,1)S(1)}, bf16[8,176,512]{2,1,0:T(8,128)(2,1)}, u32[]{:S(2)}, u32[]{:S(2)}) collective-permute-start(bf16[8,176,512]{2,1,0:T(8,128)(2,1)S(1)} %pad_maximum_fusion.4.refs_1_), channel_id=1, source_target_pairs={{0,2},{1,3},{2,0},{3,1},{4,6},{5,7},{6,4},{7,5},{8,10},{9,11},{10,... | collective-permute-start | bytes 4325384 | tf_op jit(solution)/shard_map/ppermute | solution.py:58
  106.7 31.0 %collective-permute-start.21 = (bf16[8,80,512]{2,1,0:T(8,128)(2,1)S(1)}, bf16[8,80,512]{2,1,0:T(8,128)(2,1)S(1)}, u32[]{:S(2)}, u32[]{:S(2)}) collective-permute-start(bf16[8,80,512]{2,1,0:T(8,128)(2,1)S(1)} %pad_maximum_fusion.6.refs_0_), channel_id=1, source_target_pairs={{0,16},{16,0},{1,17},{17,1},{2,18},{18,2},{3,19},{19,3},{4,20},{20... | collective-permute-start | bytes 1966088 | tf_op jit(solution)/shard_map/ppermute | solution.py:58
  106.8 42.6 %collective-permute-start.28 = (bf16[1024,1024]{1,0:T(8,128)(2,1)}, bf16[1024,1024]{1,0:T(8,128)(2,1)}, u32[]{:S(2)}, u32[]{:S(2)}) collective-permute-start(bf16[1024,1024]{1,0:T(8,128)(2,1)} %get-tuple-element.302.hidden0), channel_id=1, source_target_pairs={{1,16},{3,18},{5,20},{7,22},{9,24},{11,26},{13,28},{15,30},{16,1},... | collective-permute-start | bytes 6291464 | tf_op jit(solution)/shard_map/ppermute | solution.py:78
  110.8 26.9 %collective-permute-start.23 = (bf16[1,256,1024]{2,1,0:T(8,128)(2,1)S(1)}, bf16[1,256,1024]{2,1,0:T(8,128)(2,1)}, u32[]{:S(2)}, u32[]{:S(2)}) collective-permute-start(bf16[1,256,1024]{2,1,0:T(8,128)(2,1)S(1)} %bitcast.132), channel_id=1, source_target_pairs={{0,8},{1,9},{2,10},{3,11},{4,12},{5,13},{6,14},{7,15},{8,0},{9,1},... | collective-permute-start | bytes 1572872 | tf_op jit(solution)/shard_map/ppermute | solution.py:58
  183.9 39.1 %collective-permute-start.32 = (bf16[512,1024]{1,0:T(8,128)(2,1)}, bf16[512,1024]{1,0:T(8,128)(2,1)}, u32[]{:S(2)}, u32[]{:S(2)}) collective-permute-start(bf16[512,1024]{1,0:T(8,128)(2,1)} %slice.97), channel_id=1, source_target_pairs={{1,16},{3,18},{5,20},{7,22},{9,24},{11,26},{13,28},{15,30},{16,1},... | collective-permute-start | bytes 3145736 | tf_op jit(solution)/shard_map/ppermute | solution.py:78
  185.5 37.5 %collective-permute-start.34 = (bf16[4,128,1024]{2,1,0:T(8,128)(2,1)S(1)}, bf16[4,128,1024]{2,1,0:T(8,128)(2,1)S(1)}, u32[]{:S(2)}, u32[]{:S(2)}) collective-permute-start(bf16[4,128,1024]{2,1,0:T(8,128)(2,1)S(1)} %get-tuple-element.522), channel_id=1, source_target_pairs={{0,16},{16,0},{1,17},{17,1},{2,18},{18,2},{3,19},{19,3},{4,20},{20... | collective-permute-start | bytes 3145736 | tf_op jit(solution)/shard_map/ppermute | solution.py:58
  187.7 35.4 %collective-permute-start.33 = (bf16[4,128,1024]{2,1,0:T(8,128)(2,1)}, bf16[4,128,1024]{2,1,0:T(8,128)(2,1)S(1)}, u32[]{:S(2)}, u32[]{:S(2)}) collective-permute-start(bf16[4,128,1024]{2,1,0:T(8,128)(2,1)} %get-tuple-element.523), channel_id=1, source_target_pairs={{0,2},{1,3},{2,0},{3,1},{4,6},{5,7},{6,4},{7,5},{8,10},{9,11},{10,... | collective-permute-start | bytes 3145736 | tf_op jit(solution)/shard_map/ppermute | solution.py:58
  228.5 48.3 %collective-permute-start.39 = (bf16[8,128,1024]{2,1,0:T(8,128)(2,1)}, bf16[8,128,1024]{2,1,0:T(8,128)(2,1)}, u32[]{:S(2)}, u32[]{:S(2)}) collective-permute-start(bf16[8,128,1024]{2,1,0:T(8,128)(2,1)} %pad_maximum_fusion.2), channel_id=1, source_target_pairs={{0,2},{1,3},{2,0},{3,1},{4,6},{5,7},{6,4},{7,5},{8,10},{9,11},{10,... | collective-permute-start | bytes 6291464 | tf_op jit(solution)/shard_map/ppermute | solution.py:58
  230.1 47.8 %collective-permute-start.38 = (bf16[8,128,1024]{2,1,0:T(8,128)(2,1)S(1)}, bf16[8,128,1024]{2,1,0:T(8,128)(2,1)}, u32[]{:S(2)}, u32[]{:S(2)}) collective-permute-start(bf16[8,128,1024]{2,1,0:T(8,128)(2,1)S(1)} %pad_maximum_fusion.1), channel_id=1, source_target_pairs={{0,16},{16,0},{1,17},{17,1},{2,18},{18,2},{3,19},{19,3},{4,20},{20... | collective-permute-start | bytes 6291464 | tf_op jit(solution)/shard_map/ppermute | solution.py:58
  285.2 41.2 %collective-permute-start.43 = (bf16[8,2,64,1024]{3,2,1,0:T(8,128)(2,1)}, bf16[8,2,64,1024]{3,2,1,0:T(8,128)(2,1)S(1)}, u32[]{:S(2)}, u32[]{:S(2)}) collective-permute-start(bf16[8,2,64,1024]{3,2,1,0:T(8,128)(2,1)} %get-tuple-element.370), channel_id=1, source_target_pairs={{0,1},{1,0},{2,3},{3,2},{4,5},{5,4},{6,7},{7,6},{8,9},{9,8},{10,11... | collective-permute-start | bytes 6291464 | tf_op jit(solution)/shard_map/ppermute | solution.py:58
  285.4 41.1 %collective-permute-start.44 = (bf16[8,2,64,1024]{3,2,1,0:T(8,128)(2,1)}, bf16[8,2,64,1024]{3,2,1,0:T(8,128)(2,1)}, u32[]{:S(2)}, u32[]{:S(2)}) collective-permute-start(bf16[8,2,64,1024]{3,2,1,0:T(8,128)(2,1)} %get-tuple-element.371), channel_id=1, source_target_pairs={{0,1},{1,0},{2,3},{3,2},{4,5},{5,4},{6,7},{7,6},{8,9},{9,8},{10,11... | collective-permute-start | bytes 6291464 | tf_op jit(solution)/shard_map/ppermute | solution.py:58
  285.7 40.7 %collective-permute-start.42 = (bf16[1024,1024]{1,0:T(8,128)(2,1)}, bf16[1024,1024]{1,0:T(8,128)(2,1)}, u32[]{:S(2)}, u32[]{:S(2)}) collective-permute-start(bf16[1024,1024]{1,0:T(8,128)(2,1)} %get-tuple-element.365.refs_0_), channel_id=1, source_target_pairs={{1,16},{3,18},{5,20},{7,22},{9,24},{11,26},{13,28},{15,30},{16,1},... | collective-permute-start | bytes 6291464 | tf_op jit(solution)/shard_map/ppermute | solution.py:78
  287.7 54.4 %collective-permute-start.45 = (bf16[1024,1024]{1,0:T(8,128)(2,1)}, bf16[1024,1024]{1,0:T(8,128)(2,1)}, u32[]{:S(2)}, u32[]{:S(2)}) collective-permute-start(bf16[1024,1024]{1,0:T(8,128)(2,1)} %bitcast.149), channel_id=1, source_target_pairs={{1,16},{3,18},{5,20},{7,22},{9,24},{11,26},{13,28},{15,30},{16,1},... | collective-permute-start | bytes 6291464 | tf_op jit(solution)/shard_map/ppermute | solution.py:78
  349.9 47.9 %collective-permute-start.49 = (bf16[8,2,64,1024]{3,2,1,0:T(8,128)(2,1)S(1)}, bf16[8,2,64,1024]{3,2,1,0:T(8,128)(2,1)}, u32[]{:S(2)}, u32[]{:S(2)}) collective-permute-start(bf16[8,2,64,1024]{3,2,1,0:T(8,128)(2,1)S(1)} %add_convert_fusion.5), channel_id=1, source_target_pairs={{0,16},{16,0},{1,17},{17,1},{2,18},{18,2},{3,19},{19,3},{4,20},{20... | collective-permute-start | bytes 6291464 | tf_op jit(solution)/shard_map/ppermute | solution.py:58
  350.3 47.9 %collective-permute-start.50 = (bf16[8,2,64,1024]{3,2,1,0:T(8,128)(2,1)}, bf16[8,2,64,1024]{3,2,1,0:T(8,128)(2,1)}, u32[]{:S(2)}, u32[]{:S(2)}) collective-permute-start(bf16[8,2,64,1024]{3,2,1,0:T(8,128)(2,1)} %add_convert_fusion.4), channel_id=1, source_target_pairs={{0,2},{1,3},{2,0},{3,1},{4,6},{5,7},{6,4},{7,5},{8,10},{9,11},{10,... | collective-permute-start | bytes 6291464 | tf_op jit(solution)/shard_map/ppermute | solution.py:58
  408.9 42.6 %collective-permute-start.53 = (bf16[4,2,64,1024]{3,2,1,0:T(8,128)(2,1)}, bf16[4,2,64,1024]{3,2,1,0:T(8,128)(2,1)}, u32[]{:S(2)}, u32[]{:S(2)}) collective-permute-start(bf16[4,2,64,1024]{3,2,1,0:T(8,128)(2,1)} %slice.102), channel_id=1, source_target_pairs={{0,16},{16,0},{1,17},{17,1},{2,18},{18,2},{3,19},{19,3},{4,20},{20... | collective-permute-start | bytes 3145736 | tf_op jit(solution)/shard_map/ppermute | solution.py:58
  410.4 41.1 %collective-permute-start.52 = (bf16[4,2,64,1024]{3,2,1,0:T(8,128)(2,1)}, bf16[4,2,64,1024]{3,2,1,0:T(8,128)(2,1)}, u32[]{:S(2)}, u32[]{:S(2)}) collective-permute-start(bf16[4,2,64,1024]{3,2,1,0:T(8,128)(2,1)} %slice.101), channel_id=1, source_target_pairs={{0,2},{1,3},{2,0},{3,1},{4,6},{5,7},{6,4},{7,5},{8,10},{9,11},{10,... | collective-permute-start | bytes 3145736 | tf_op jit(solution)/shard_map/ppermute | solution.py:58
  410.9 40.6 %collective-permute-start.54 = (bf16[3,1024,256]{2,1,0:T(8,128)(2,1)}, bf16[3,1024,256]{2,1,0:T(8,128)(2,1)S(1)}, u32[]{:S(2)}, u32[]{:S(2)}) collective-permute-start(bf16[3,1024,256]{2,1,0:T(8,128)(2,1)} %get-tuple-element.418), channel_id=1, source_target_pairs={{0,1},{1,0},{2,3},{3,2},{4,5},{5,4},{6,7},{7,6},{8,9},{9,8},{10,11... | collective-permute-start | bytes 4718600 | tf_op jit(solution)/shard_map/ppermute | solution.py:58
  410.9 40.6 %collective-permute-start.51 = (bf16[1024,1024]{1,0:T(8,128)(2,1)}, bf16[1024,1024]{1,0:T(8,128)(2,1)}, u32[]{:S(2)}, u32[]{:S(2)}) collective-permute-start(bf16[1024,1024]{1,0:T(8,128)(2,1)} %get-tuple-element.467), channel_id=1, source_target_pairs={{1,16},{3,18},{5,20},{7,22},{9,24},{11,26},{13,28},{15,30},{16,1},... | collective-permute-start | bytes 6291464 | tf_op jit(solution)/shard_map/ppermute | solution.py:78
  534.5 34.5 %collective-permute-start.66 = (bf16[2,2,128,1024]{3,2,0,1:T(8,128)(2,1)}, bf16[2,2,128,1024]{3,2,0,1:T(8,128)(2,1)}, u32[]{:S(2)}, u32[]{:S(2)}) collective-permute-start(bf16[2,2,128,1024]{3,2,0,1:T(8,128)(2,1)} %dynamic-slice_bitcast_fusion), channel_id=1, source_target_pairs={{0,2},{1,3},{2,0},{3,1},{4,6},{5,7},{6,4},{7,5},{8,10},{9,11},{10,... | collective-permute-start | bytes 3145736 | tf_op jit(solution)/shard_map/ppermute | solution.py:58
  536.2 32.8 %collective-permute-start.65 = (bf16[2,2,2,128,512]{4,3,0,1,2:T(8,128)(2,1)}, bf16[2,2,2,128,512]{4,3,0,1,2:T(8,128)(2,1)}, u32[]{:S(2)}, u32[]{:S(2)}) collective-permute-start(bf16[2,2,2,128,512]{4,3,0,1,2:T(8,128)(2,1)} %constant_dynamic-slice_fusion.3), channel_id=1, source_target_pairs={{0,16},{16,0},{1,17},{17,1},{2,18},{18,2},{3,19},{19,3},{4,20},{20... | collective-permute-start | bytes 3145736 | tf_op jit(solution)/shard_map/ppermute | solution.py:58
  572.0 28.9 %collective-permute-start.71 = (bf16[2,2,128,512]{3,2,0,1:T(8,128)(2,1)}, bf16[2,2,128,512]{3,2,0,1:T(8,128)(2,1)}, u32[]{:S(2)}, u32[]{:S(2)}) collective-permute-start(bf16[2,2,128,512]{3,2,0,1:T(8,128)(2,1)} %constant_dynamic-slice_fusion), channel_id=1, source_target_pairs={{0,16},{16,0},{1,17},{17,1},{2,18},{18,2},{3,19},{19,3},{4,20},{20... | collective-permute-start | bytes 1572872 | tf_op jit(solution)/shard_map/ppermute | solution.py:58
  (116 other events, 1233.8 us)

commit v2 on v1

--- a/solution.py
+++ b/solution.py
@@ -1159,7 +1159,8 @@
     cut = rows // 2
     cols = w_mod.shape[1]
 
-    skip_turned, qkv_turned, out_turned, up_turned = flip(w_skip, w_qkv, w_out, w_up)
+    (skip_turned,) = flip(w_skip)
+    qkv_turned, out_turned, up_turned = flip(w_qkv, w_out, w_up)
     g2 = Gather(net, jnp.concatenate([qkv_turned, out_turned], axis=0), part_of(n_qkv + n_out, 0.33))
     lens = jnp.concatenate([lengths, drop_mask], axis=0)
     ints = jnp.concatenate([lengths, drop_mask, time_index], axis=1)
@@ -1292,7 +1293,7 @@
     output_got = net.trade(out_b)
     if all_pairs > pairs:
         d_sent = attn_bwd(net, idx, pieces, d_attn_p, lse, segr, segc, long, pairs, all_pairs - pairs)
-        d_sent, (output_got,), raw, d_pieces = tie(list(d_sent), [output_got], raw, d_pieces)
+        d_sent, raw, d_pieces = tie(list(d_sent), raw, d_pieces)
         d_pieces += [d_sent[0]] + [net.attn_swap(d_sent[r], r) for r in range(1, na)]
     ff = jnp.stack([plus(a, b) for a, b in zip(kept, raw)], axis=1)
     common = list(reversed(g3.orders[0][:-3]))

time: 648 us -> 641 us (0.989)
  transfers between devices with their start and end apart: 81 -> 81, of which waited for: 29 -> 27; matrix products, arithmetic and copies ran while one was open for 10% -> 11% of each run, Pallas kernels for 47% -> 48%
where the time goes in v2:
time: 641 us; the launch traced here: 631 us
  Pallas kernels  311 us (49%)
  waiting for transfers between devices  109 us (17%)
  starting transfers between devices  104 us (16%)
  other arithmetic  55.9 us (9%)
  local copies, waits for them, and re-layouts  48.3 us (8%)
    pallas_call x2, Pallas kernels, attn_bwd(): pl.pallas_call(partial(attn_bwd_kernel, na=na, long=long), grid_spec=pltp...  77.2 us
    ppermute x65, waiting for transfers between devices, swap(): return lax.ppermute(x, axis, [(i, i ^ mask) for i in range(size)])  76.4 us
    pallas_call x2, Pallas kernels, ffn(): pl.pallas_call(partial(ffn_kernel, steps=steps, second=second), grid=(ste...  71.4 us
    ppermute x65, starting transfers between devices, swap(): return lax.ppermute(x, axis, [(i, i ^ mask) for i in range(size)])  59.6 us
    pallas_call x1, Pallas kernels, attn_fwd(): pl.pallas_call(partial(attn_fwd_kernel, na=na, long=long), grid_spec=pltp...  34.9 us
    pallas_call x3, Pallas kernels, outer(): pl.pallas_call(partial(outer_kernel, n=n, own=len(xs), choose=choose), gr...  29.7 us
    convert_element_type x17, other arithmetic, plus(): return total.astype(bf16)  28.3 us
    unnamed x126, local copies, waits for them, and re-layouts  22.9 us
  transfers between devices with their start and end apart: 81, of which 27 were waited for; matrix products, arithmetic and copies ran while one was open for 11% of the time, Pallas kernels for 48%

profile of v2, /device:TPU:0, one launch (start us, length us, event | category | flops | bytes accessed | tf_op | source)
XLA Modules:
  0.0 631.3 jit_solution(9696335225000731932)
XLA Ops:
  31.9 7.3 %collective-permute-done.6 = bf16[1,256,512]{2,1,0:T(8,128)(2,1)S(1)} collective-permute-done((bf16[1,256,512]{2,1,0:T(8,128)(2,1)S(1)}, bf16[1,256,512]{2,1,0:T(8,128)(2,1)S(1)}, u32[]{:S(2)}, u32[]{:S(2)}) %collective-permute-start.6) | collective-permute-done | bytes 262176 | tf_op jit(solution)/shard_map/ppermute | solution.py:58
  83.4 6.6 %collective-permute-done.18.refs_1_ = bf16[128,512]{1,0:T(8,128)(2,1)S(1)} collective-permute-done((bf16[128,512]{1,0:T(8,128)(2,1)}, bf16[128,512]{1,0:T(8,128)(2,1)S(1)}, u32[]{:S(2)}, u32[]{:S(2)}) %collective-permute-start.18) | collective-permute-done | bytes 131104 | tf_op jit(solution)/shard_map/ppermute | solution.py:1136
  90.6 10.3 %skip_fwd.1 = (bf16[1024,1024]{1,0:T(8,128)(2,1)}, bf16[1024,1024]{1,0:T(8,128)(2,1)}) custom-call(s32[4]{0:T(128)} %copy-done.16, s32[2,8]{1,0:T(2,128)} %pad_add_fusion.4.lens, bf16[1024,1024]{1,0:T(8,128)(2,1)} %bitcast.146, bf16[1024,1024]{1,0:T(8,128)(2,1)} %bitcast.148, bf16[1024,1024]{1,0:T(8,128)(2,1)} %bitcast.147, bf16[1024,2048]{1,0:T(8,128)(2,1)} %copy-done.4), custom_call_target="tpu_custom_call" | custom-call | flops 4294967296 | bytes 14680064 | tf_op jit(solution)/shard_map/skip_fwd/pallas_call | solution.py:307
  109.2 7.3 %all-to-all-start.1 = ((f32[16,8,256]{2,1,0:T(8,128)}), f32[16,8,256]{2,1,0:T(8,128)S(1)}, u32[]{:S(2)}, u32[]{:S(2)}) async-start(f32[16,8,256]{2,1,0:T(8,128)} %bitcast.14), calls=%async_computation.1 | async-start | bytes 262144 | tf_op jit(solution)/shard_map/all_to_all | solution.py:1230
  117.1 17.4 %all-to-all-done.1 = f32[16,8,256]{2,1,0:T(8,128)S(1)} async-done(((f32[16,8,256]{2,1,0:T(8,128)}), f32[16,8,256]{2,1,0:T(8,128)S(1)}, u32[]{:S(2)}, u32[]{:S(2)}) %all-to-all-start.1) | async-done | bytes 131104 | tf_op jit(solution)/shard_map/all_to_all | solution.py:1230
  150.0 14.6 %qkv_fwd.1 = (bf16[1024,1024]{1,0:T(8,128)(2,1)}, bf16[1024,1024]{1,0:T(8,128)(2,1)}, bf16[3,1024,512]{2,1,0:T(8,128)(2,1)}, bf16[3,1024,512]{2,1,0:T(8,128)(2,1)}) custom-call(s32[3]{0:T(128)} %copy-done.15, bf16[1024,1024]{1,0:T(8,128)(2,1)} %get-tuple-element.299.hidden0, bf16[1024,1024]{1,0:T(8,128)(2,1)} %collective-permute-done.28.got, ...), custom_call_target="tpu_custom_call" | custom-call | flops 6442450944 | bytes 20971520 | tf_op jit(solution)/shard_map/qkv_fwd/pallas_call | solution.py:386
  164.5 7.2 %collective-permute-done.29 = bf16[2,256,1024]{2,1,0:T(8,128)(2,1)} collective-permute-done((bf16[2,256,1024]{2,1,0:T(8,128)(2,1)}, bf16[2,256,1024]{2,1,0:T(8,128)(2,1)}, u32[]{:S(2)}, u32[]{:S(2)}) %collective-permute-start.29) | collective-permute-done | bytes 1048608 | tf_op jit(solution)/shard_map/ppermute | solution.py:58
  185.2 34.9 %attn_fwd.1 = (bf16[1024,512]{1,0:T(8,128)(2,1)}, bf16[1024,512]{1,0:T(8,128)(2,1)}, f32[4,2,2048]{2,1,0:T(2,128)}) custom-call(s32[3]{0:T(128)} %copy-done.15, bf16[3,1024,512]{2,1,0:T(8,128)(2,1)} %get-tuple-element.315.refs_0_, bf16[3,1024,512]{2,1,0:T(8,128)(2,1)} %copy-done.54, s32[8,512]{1,0:T(8,128)} %copy-done.21, s32[512,128]{1,0:T(8,128)} %copy-done.20), custom_call_target="tpu_custom_call" | custom-call | flops 21474836480 | bytes 8388608 | tf_op jit(solution)/shard_map/attn_fwd/pallas_call | solution.py:838
  226.8 10.9 %out_fwd.1 = (bf16[1024,1024]{1,0:T(8,128)(2,1)}, f32[1024,1024]{1,0:T(8,128)}, bf16[1024,1024]{1,0:T(8,128)(2,1)}, bf16[1024,1024]{1,0:T(8,128)(2,1)}) custom-call(s32[3]{0:T(128)} %copy-done.15, bf16[1024,512]{1,0:T(8,128)(2,1)} %get-tuple-element.329.refs_0_, bf16[1024,512]{1,0:T(8,128)(2,1)} %copy-done.46, ...), custom_call_target="tpu_custom_call" | custom-call | flops 2147483648 | bytes 14680064 | tf_op jit(solution)/shard_map/out_fwd/pallas_call | solution.py:431
  237.7 34.7 %ffn.2 = (f32[1024,1024]{1,0:T(8,128)}, f32[1024,1024]{1,0:T(8,128)}, bf16[8,2,64,1024]{3,2,1,0:T(8,128)(2,1)}, bf16[8,2,64,1024]{3,2,1,0:T(8,128)(2,1)}, bf16[8...) custom-call(bf16[1024,1024]{1,0:T(8,128)(2,1)} %get-tuple-element.336.refs_0_, ...), custom_call_target="tpu_custom_call" | custom-call | flops 25769803776 | bytes 33554432 | tf_op jit(solution)/shard_map/ffn/pallas_call | solution.py:750
  286.5 36.7 %ffn.3 = (bf16[1024,1024]{1,0:T(8,128)(2,1)}, f32[1024,1024]{1,0:T(8,128)}, bf16[8,2,64,1024]{3,2,1,0:T(8,128)(2,1)}, bf16[8,2,64,1024]{3,2,1,0:T(8,128)(2,1)}, ...) custom-call(bf16[1024,1024]{1,0:T(8,128)(2,1)} %get-tuple-element.336.refs_0_, ...), custom_call_target="tpu_custom_call" | custom-call | flops 25769803776 | bytes 33554432 | tf_op jit(solution)/shard_map/ffn/pallas_call | solution.py:750
  325.8 13.0 %out_bwd.1 = (f32[1024,1024]{1,0:T(8,128)}, bf16[1024,1024]{1,0:T(8,128)(2,1)}, f32[8,2048]{1,0:T(8,128)}, bf16[1024,512]{1,0:T(8,128)(2,1)}, bf16[1024,512]{1,0:T(8,128)(2,1)}) custom-call(s32[3]{0:T(128)} %copy-done.15, f32[1024,1024]{1,0:T(8,128)} %get-tuple-element.369.grad, f32[1024,1024]{1,0:T(8,128)} %get-tuple-element.338.refs_2_.hidden2, ...), custom_call_target="tpu_custom_call" | custom-call | flops 2147483648 | bytes 23068672 | tf_op jit(solution)/shard_map/out_bwd/pallas_call | solution.py:498
  354.1 38.5 %attn_bwd.2 = (bf16[3,1024,256]{2,1,0:T(8,128)(2,1)}, bf16[3,1024,256]{2,1,0:T(8,128)(2,1)}) custom-call(s32[3]{0:T(128)} %copy-done.15, bf16[3,1024,512]{2,1,0:T(8,128)(2,1)} %get-tuple-element.315.refs_0_, bf16[3,1024,512]{2,1,0:T(8,128)(2,1)} %copy-done.54, bf16[1024,512]{1,0:T(8,128)(2,1)} %get-tuple-element.407.refs_2_, bf16[1024,512]{1,0:T(8,128)(2,1)} %copy-done.57, ...), custom_call_target="tpu_custom_call" | custom-call | flops 26843545600 | bytes 8388608 | tf_op jit(solution)/shard_map/attn_bwd/pallas_call | solution.py:926
  394.9 7.9 %add_convert_fusion.2 = (bf16[8,2,64,1024]{3,2,1,0:T(8,128)(2,1)S(1)}, bf16[8,2,64,1024]{3,2,1,0:T(8,128)(2,1)S(1)}) fusion(bf16[8,2,64,1024]{3,2,1,0:T(8,128)(2,1)} %collective-permute-done.50, bf16[8,2,64,1024]{3,2,1,0:T(8,128)(2,1)} %collective-permute-done.44, bf16[8,2,64,1024]{3,2,1,0:T(8,128)(2,1)} %get-tuple-element.403, ...), kind=kLoop, calls=%fused_computation.2 | loop fusion | flops 12582912 | bytes 16777216 | tf_op jit(solution)/shard_map/convert_element_type | solution.py:116
  407.9 38.7 %attn_bwd.3 = (bf16[3,1024,256]{2,1,0:T(8,128)(2,1)}, bf16[3,1024,256]{2,1,0:T(8,128)(2,1)}) custom-call(s32[3]{0:T(128)} %copy-done.15, bf16[3,1024,512]{2,1,0:T(8,128)(2,1)} %get-tuple-element.315.refs_0_, bf16[3,1024,512]{2,1,0:T(8,128)(2,1)} %copy-done.54, bf16[1024,512]{1,0:T(8,128)(2,1)} %get-tuple-element.407.refs_2_, bf16[1024,512]{1,0:T(8,128)(2,1)} %copy-done.57, ...), custom_call_target="tpu_custom_call" | custom-call | flops 26843545600 | bytes 8388608 | tf_op jit(solution)/shard_map/attn_bwd/pallas_call | solution.py:926
  455.3 8.7 %turn_back.1.d_qkv.g = bf16[1024,3072]{1,0:T(8,128)(2,1)} custom-call(s32[3]{0:T(128)} %copy-done.15, bf16[3,1024,256]{2,1,0:T(8,128)(2,1)} %get-tuple-element.421.refs_0_, bf16[3,1024,256]{2,1,0:T(8,128)(2,1)} %copy-done.36, bf16[3,1024,256]{2,1,0:T(8,128)(2,1)} %get-tuple-element.423.refs_2_, bf16[3,1024,256]{2,1,0:T(8,128)(2,1)} %collective-permute-done.54.refs_3_, ...), custom_call_target="tpu_custom_call" | custom-call | flops 12582912 | bytes 12582912 | tf_op jit(solution)/shard_map/turn_back/pallas_call | solution.py:538
  464.0 16.1 %qkv_bwd.1 = (bf16[1024,1024]{1,0:T(8,128)(2,1)}, f32[8,2048]{1,0:T(8,128)}) custom-call(bf16[1024,3072]{1,0:T(8,128)(2,1)} %turn_back.1.d_qkv.g, bf16[1024,1024]{1,0:T(8,128)(2,1)} %get-tuple-element.331.refs_2_.hidden, f32[1024,1024]{1,0:T(8,128)} %get-tuple-element.425.d_h2, bf16[1024,128]{1,0:T(8,128)(2,1)} %copy-done.6, ...), custom_call_target="tpu_custom_call" | custom-call | flops 6442450944 | bytes 23068672 | tf_op jit(solution)/shard_map/qkv_bwd/pallas_call | solution.py:577
  480.1 10.6 %outer.4 = (bf16[8,64,2048]{2,1,0:T(8,128)(2,1)}, bf16[8,64,2048]{2,1,0:T(8,128)(2,1)}) custom-call(s32[4]{0:T(128)} %copy-done.16, bf16[1024,1024]{1,0:T(8,128)(2,1)} %get-tuple-element.473.g.d_h, bf16[1024,1024]{1,0:T(8,128)(2,1)} %get-tuple-element.362.refs_0_, bf16[1024,1024]{1,0:T(8,128)(2,1)} %collective-permute-done.42.refs_1_, ...), custom_call_target="tpu_custom_call" | custom-call | flops 4294967296 | bytes 10485760 | tf_op jit(solution)/shard_map/outer/pallas_call | solution.py:639
  490.9 13.0 %outer.5 = (bf16[8,256,1024]{2,1,0:T(8,128)(2,1)}, bf16[8,256,1024]{2,1,0:T(8,128)(2,1)}) custom-call(s32[4]{0:T(128)} %copy-done.16, bf16[1024,3072]{1,0:T(8,128)(2,1)} %turn_back.1.d_qkv.g, bf16[1024,1024]{1,0:T(8,128)(2,1)} %get-tuple-element.437.refs_0_, ...), custom_call_target="tpu_custom_call", output_to_operand_aliasing={{0}: (3, {}), {1}: (4, {})} | custom-call | flops 6442450944 | bytes 14680064 | tf_op jit(solution)/shard_map/outer/pallas_call | solution.py:639
  539.0 6.5 %all-to-all-start.2 = ((bf16[128,16,64]{0,2,1:T(8,128)(2,1)}), bf16[128,16,64]{0,2,1:T(8,128)(2,1)S(1)}, u32[]{:S(2)}, u32[]{:S(2)}) async-start(bf16[128,16,64]{0,2,1:T(8,128)(2,1)} %copy.62), calls=%async_computation.2 | async-start | bytes 524288 | tf_op jit(solution)/shard_map/all_to_all | solution.py:1121
  574.3 7.4 %all-to-all-start.3 = ((f32[16,8,256]{2,1,0:T(8,128)}), f32[16,8,256]{2,1,0:T(8,128)S(1)}, u32[]{:S(2)}, u32[]{:S(2)}) async-start(f32[16,8,256]{2,1,0:T(8,128)} %bitcast.54), calls=%async_computation.3 | async-start | bytes 262144 | tf_op jit(solution)/shard_map/all_to_all | solution.py:1348
  586.9 7.3 %collective-permute-done.69 = bf16[64,1024]{1,0:T(8,128)(2,1)S(1)} collective-permute-done((bf16[64,1024]{1,0:T(8,128)(2,1)S(1)}, bf16[64,1024]{1,0:T(8,128)(2,1)S(1)}, u32[]{:S(2)}, u32[]{:S(2)}) %collective-permute-start.69) | collective-permute-done | bytes 131104 | tf_op jit(solution)/shard_map/ppermute | solution.py:58
  602.1 13.1 %collective-permute-done.76 = f32[128,256]{1,0:T(8,128)S(1)} collective-permute-done((f32[128,256]{1,0:T(8,128)S(1)}, f32[128,256]{1,0:T(8,128)S(1)}, u32[]{:S(2)}, u32[]{:S(2)}) %collective-permute-start.76) | collective-permute-done | bytes 131104 | tf_op jit(solution)/shard_map/ppermute | solution.py:58
  617.5 10.1 %skip_bwd.1 = (f32[1024,1024]{1,0:T(8,128)}, f32[1024,1024]{1,0:T(8,128)}) custom-call(s32[4]{0:T(128)} %copy-done.16, bf16[1024,1024]{1,0:T(8,128)(2,1)} %get-tuple-element.473.g.d_h, bf16[512,1024]{1,0:T(8,128)(2,1)} %collective-permute-done.72.got0, bf16[512,1024]{1,0:T(8,128)(2,1)} %copy-done.58, bf16[1024,2048]{1,0:T(8,128)(2,1)} %copy-done.4), custom_call_target="tpu_custom_call" | custom-call | flops 4294967296 | bytes 16777216 | tf_op jit(solution)/shard_map/skip_bwd/pallas_call | solution.py:600
  (385 shorter events, 250.5 us)
Async XLA Ops:
  69.8 31.0 %collective-permute-start.20 = (bf16[4,176,512]{2,1,0:T(8,128)(2,1)}, bf16[4,176,512]{2,1,0:T(8,128)(2,1)}, u32[]{:S(2)}, u32[]{:S(2)}) collective-permute-start(bf16[4,176,512]{2,1,0:T(8,128)(2,1)} %slice.123), channel_id=1, source_target_pairs={{0,16},{16,0},{1,17},{17,1},{2,18},{18,2},{3,19},{19,3},{4,20},{20... | collective-permute-start | bytes 2162696 | tf_op jit(solution)/shard_map/ppermute | solution.py:58
  73.3 27.6 %collective-permute-start.19 = (bf16[4,80,512]{2,1,0:T(8,128)(2,1)S(1)}, bf16[4,80,512]{2,1,0:T(8,128)(2,1)}, u32[]{:S(2)}, u32[]{:S(2)}) collective-permute-start(bf16[4,80,512]{2,1,0:T(8,128)(2,1)S(1)} %slice.122), channel_id=1, source_target_pairs={{0,2},{1,3},{2,0},{3,1},{4,6},{5,7},{6,4},{7,5},{8,10},{9,11},{10,... | collective-permute-start | bytes 983048 | tf_op jit(solution)/shard_map/ppermute | solution.py:58
  102.4 32.1 %collective-permute-start.22 = (bf16[8,176,512]{2,1,0:T(8,128)(2,1)S(1)}, bf16[8,176,512]{2,1,0:T(8,128)(2,1)}, u32[]{:S(2)}, u32[]{:S(2)}) collective-permute-start(bf16[8,176,512]{2,1,0:T(8,128)(2,1)S(1)} %pad_maximum_fusion.4.refs_1_), channel_id=1, source_target_pairs={{0,2},{1,3},{2,0},{3,1},{4,6},{5,7},{6,4},{7,5},{8,10},{9,11},{10,... | collective-permute-start | bytes 4325384 | tf_op jit(solution)/shard_map/ppermute | solution.py:58
  103.5 31.0 %collective-permute-start.21 = (bf16[8,80,512]{2,1,0:T(8,128)(2,1)S(1)}, bf16[8,80,512]{2,1,0:T(8,128)(2,1)S(1)}, u32[]{:S(2)}, u32[]{:S(2)}) collective-permute-start(bf16[8,80,512]{2,1,0:T(8,128)(2,1)S(1)} %pad_maximum_fusion.6.refs_0_), channel_id=1, source_target_pairs={{0,16},{16,0},{1,17},{17,1},{2,18},{18,2},{3,19},{19,3},{4,20},{20... | collective-permute-start | bytes 1966088 | tf_op jit(solution)/shard_map/ppermute | solution.py:58
  103.6 42.6 %collective-permute-start.28 = (bf16[1024,1024]{1,0:T(8,128)(2,1)}, bf16[1024,1024]{1,0:T(8,128)(2,1)}, u32[]{:S(2)}, u32[]{:S(2)}) collective-permute-start(bf16[1024,1024]{1,0:T(8,128)(2,1)} %get-tuple-element.299.hidden0), channel_id=1, source_target_pairs={{1,16},{3,18},{5,20},{7,22},{9,24},{11,26},{13,28},{15,30},{16,1},... | collective-permute-start | bytes 6291464 | tf_op jit(solution)/shard_map/ppermute | solution.py:78
  180.7 39.4 %collective-permute-start.32 = (bf16[512,1024]{1,0:T(8,128)(2,1)}, bf16[512,1024]{1,0:T(8,128)(2,1)}, u32[]{:S(2)}, u32[]{:S(2)}) collective-permute-start(bf16[512,1024]{1,0:T(8,128)(2,1)} %slice.97), channel_id=1, source_target_pairs={{1,16},{3,18},{5,20},{7,22},{9,24},{11,26},{13,28},{15,30},{16,1},... | collective-permute-start | bytes 3145736 | tf_op jit(solution)/shard_map/ppermute | solution.py:78
  182.4 37.8 %collective-permute-start.34 = (bf16[4,128,1024]{2,1,0:T(8,128)(2,1)S(1)}, bf16[4,128,1024]{2,1,0:T(8,128)(2,1)S(1)}, u32[]{:S(2)}, u32[]{:S(2)}) collective-permute-start(bf16[4,128,1024]{2,1,0:T(8,128)(2,1)S(1)} %get-tuple-element.518), channel_id=1, source_target_pairs={{0,16},{16,0},{1,17},{17,1},{2,18},{18,2},{3,19},{19,3},{4,20},{20... | collective-permute-start | bytes 3145736 | tf_op jit(solution)/shard_map/ppermute | solution.py:58
  184.5 35.7 %collective-permute-start.33 = (bf16[4,128,1024]{2,1,0:T(8,128)(2,1)}, bf16[4,128,1024]{2,1,0:T(8,128)(2,1)S(1)}, u32[]{:S(2)}, u32[]{:S(2)}) collective-permute-start(bf16[4,128,1024]{2,1,0:T(8,128)(2,1)} %get-tuple-element.519), channel_id=1, source_target_pairs={{0,2},{1,3},{2,0},{3,1},{4,6},{5,7},{6,4},{7,5},{8,10},{9,11},{10,... | collective-permute-start | bytes 3145736 | tf_op jit(solution)/shard_map/ppermute | solution.py:58
  225.6 48.3 %collective-permute-start.39 = (bf16[8,128,1024]{2,1,0:T(8,128)(2,1)}, bf16[8,128,1024]{2,1,0:T(8,128)(2,1)}, u32[]{:S(2)}, u32[]{:S(2)}) collective-permute-start(bf16[8,128,1024]{2,1,0:T(8,128)(2,1)} %pad_maximum_fusion.2), channel_id=1, source_target_pairs={{0,2},{1,3},{2,0},{3,1},{4,6},{5,7},{6,4},{7,5},{8,10},{9,11},{10,... | collective-permute-start | bytes 6291464 | tf_op jit(solution)/shard_map/ppermute | solution.py:58
  226.8 47.8 %collective-permute-start.38 = (bf16[8,128,1024]{2,1,0:T(8,128)(2,1)S(1)}, bf16[8,128,1024]{2,1,0:T(8,128)(2,1)}, u32[]{:S(2)}, u32[]{:S(2)}) collective-permute-start(bf16[8,128,1024]{2,1,0:T(8,128)(2,1)S(1)} %pad_maximum_fusion.1), channel_id=1, source_target_pairs={{0,16},{16,0},{1,17},{17,1},{2,18},{18,2},{3,19},{19,3},{4,20},{20... | collective-permute-start | bytes 6291464 | tf_op jit(solution)/shard_map/ppermute | solution.py:58
  281.9 41.2 %collective-permute-start.43 = (bf16[8,2,64,1024]{3,2,1,0:T(8,128)(2,1)}, bf16[8,2,64,1024]{3,2,1,0:T(8,128)(2,1)S(1)}, u32[]{:S(2)}, u32[]{:S(2)}) collective-permute-start(bf16[8,2,64,1024]{3,2,1,0:T(8,128)(2,1)} %get-tuple-element.367), channel_id=1, source_target_pairs={{0,1},{1,0},{2,3},{3,2},{4,5},{5,4},{6,7},{7,6},{8,9},{9,8},{10,11... | collective-permute-start | bytes 6291464 | tf_op jit(solution)/shard_map/ppermute | solution.py:58
  282.1 41.1 %collective-permute-start.44 = (bf16[8,2,64,1024]{3,2,1,0:T(8,128)(2,1)}, bf16[8,2,64,1024]{3,2,1,0:T(8,128)(2,1)}, u32[]{:S(2)}, u32[]{:S(2)}) collective-permute-start(bf16[8,2,64,1024]{3,2,1,0:T(8,128)(2,1)} %get-tuple-element.368), channel_id=1, source_target_pairs={{0,1},{1,0},{2,3},{3,2},{4,5},{5,4},{6,7},{7,6},{8,9},{9,8},{10,11... | collective-permute-start | bytes 6291464 | tf_op jit(solution)/shard_map/ppermute | solution.py:58
  282.4 40.8 %collective-permute-start.42 = (bf16[1024,1024]{1,0:T(8,128)(2,1)}, bf16[1024,1024]{1,0:T(8,128)(2,1)}, u32[]{:S(2)}, u32[]{:S(2)}) collective-permute-start(bf16[1024,1024]{1,0:T(8,128)(2,1)} %get-tuple-element.362.refs_0_), channel_id=1, source_target_pairs={{1,16},{3,18},{5,20},{7,22},{9,24},{11,26},{13,28},{15,30},{16,1},... | collective-permute-start | bytes 6291464 | tf_op jit(solution)/shard_map/ppermute | solution.py:78
  284.4 54.5 %collective-permute-start.45 = (bf16[1024,1024]{1,0:T(8,128)(2,1)}, bf16[1024,1024]{1,0:T(8,128)(2,1)}, u32[]{:S(2)}, u32[]{:S(2)}) collective-permute-start(bf16[1024,1024]{1,0:T(8,128)(2,1)} %bitcast.149), channel_id=1, source_target_pairs={{1,16},{3,18},{5,20},{7,22},{9,24},{11,26},{13,28},{15,30},{16,1},... | collective-permute-start | bytes 6291464 | tf_op jit(solution)/shard_map/ppermute | solution.py:78
  346.6 47.9 %collective-permute-start.49 = (bf16[8,2,64,1024]{3,2,1,0:T(8,128)(2,1)S(1)}, bf16[8,2,64,1024]{3,2,1,0:T(8,128)(2,1)}, u32[]{:S(2)}, u32[]{:S(2)}) collective-permute-start(bf16[8,2,64,1024]{3,2,1,0:T(8,128)(2,1)S(1)} %add_convert_fusion.5), channel_id=1, source_target_pairs={{0,16},{16,0},{1,17},{17,1},{2,18},{18,2},{3,19},{19,3},{4,20},{20... | collective-permute-start | bytes 6291464 | tf_op jit(solution)/shard_map/ppermute | solution.py:58
  347.0 47.9 %collective-permute-start.50 = (bf16[8,2,64,1024]{3,2,1,0:T(8,128)(2,1)}, bf16[8,2,64,1024]{3,2,1,0:T(8,128)(2,1)}, u32[]{:S(2)}, u32[]{:S(2)}) collective-permute-start(bf16[8,2,64,1024]{3,2,1,0:T(8,128)(2,1)} %add_convert_fusion.4), channel_id=1, source_target_pairs={{0,2},{1,3},{2,0},{3,1},{4,6},{5,7},{6,4},{7,5},{8,10},{9,11},{10,... | collective-permute-start | bytes 6291464 | tf_op jit(solution)/shard_map/ppermute | solution.py:58
  405.5 41.1 %collective-permute-start.52 = (bf16[4,2,64,1024]{3,2,1,0:T(8,128)(2,1)}, bf16[4,2,64,1024]{3,2,1,0:T(8,128)(2,1)}, u32[]{:S(2)}, u32[]{:S(2)}) collective-permute-start(bf16[4,2,64,1024]{3,2,1,0:T(8,128)(2,1)} %slice.102), channel_id=1, source_target_pairs={{0,16},{16,0},{1,17},{17,1},{2,18},{18,2},{3,19},{19,3},{4,20},{20... | collective-permute-start | bytes 3145736 | tf_op jit(solution)/shard_map/ppermute | solution.py:58
  407.0 39.5 %collective-permute-start.51 = (bf16[4,2,64,1024]{3,2,1,0:T(8,128)(2,1)}, bf16[4,2,64,1024]{3,2,1,0:T(8,128)(2,1)}, u32[]{:S(2)}, u32[]{:S(2)}) collective-permute-start(bf16[4,2,64,1024]{3,2,1,0:T(8,128)(2,1)} %slice.101), channel_id=1, source_target_pairs={{0,2},{1,3},{2,0},{3,1},{4,6},{5,7},{6,4},{7,5},{8,10},{9,11},{10,... | collective-permute-start | bytes 3145736 | tf_op jit(solution)/shard_map/ppermute | solution.py:58
  407.9 38.7 %collective-permute-start.53 = (bf16[3,1024,256]{2,1,0:T(8,128)(2,1)}, bf16[3,1024,256]{2,1,0:T(8,128)(2,1)S(1)}, u32[]{:S(2)}, u32[]{:S(2)}) collective-permute-start(bf16[3,1024,256]{2,1,0:T(8,128)(2,1)} %get-tuple-element.414), channel_id=1, source_target_pairs={{0,1},{1,0},{2,3},{3,2},{4,5},{5,4},{6,7},{7,6},{8,9},{9,8},{10,11... | collective-permute-start | bytes 4718600 | tf_op jit(solution)/shard_map/ppermute | solution.py:58
  447.2 32.9 %collective-permute-start.55 = (bf16[1024,1024]{1,0:T(8,128)(2,1)}, bf16[1024,1024]{1,0:T(8,128)(2,1)}, u32[]{:S(2)}, u32[]{:S(2)}) collective-permute-start(bf16[1024,1024]{1,0:T(8,128)(2,1)} %get-tuple-element.463), channel_id=1, source_target_pairs={{1,16},{3,18},{5,20},{7,22},{9,24},{11,26},{13,28},{15,30},{16,1},... | collective-permute-start | bytes 6291464 | tf_op jit(solution)/shard_map/ppermute | solution.py:78
  527.5 35.4 %collective-permute-start.66 = (bf16[2,2,128,1024]{3,2,0,1:T(8,128)(2,1)}, bf16[2,2,128,1024]{3,2,0,1:T(8,128)(2,1)}, u32[]{:S(2)}, u32[]{:S(2)}) collective-permute-start(bf16[2,2,128,1024]{3,2,0,1:T(8,128)(2,1)} %dynamic-slice_bitcast_fusion), channel_id=1, source_target_pairs={{0,2},{1,3},{2,0},{3,1},{4,6},{5,7},{6,4},{7,5},{8,10},{9,11},{10,... | collective-permute-start | bytes 3145736 | tf_op jit(solution)/shard_map/ppermute | solution.py:58
  530.0 32.9 %collective-permute-start.65 = (bf16[2,2,2,128,512]{4,3,0,1,2:T(8,128)(2,1)}, bf16[2,2,2,128,512]{4,3,0,1,2:T(8,128)(2,1)}, u32[]{:S(2)}, u32[]{:S(2)}) collective-permute-start(bf16[2,2,2,128,512]{4,3,0,1,2:T(8,128)(2,1)} %constant_dynamic-slice_fusion.3), channel_id=1, source_target_pairs={{0,16},{16,0},{1,17},{17,1},{2,18},{18,2},{3,19},{19,3},{4,20},{20... | collective-permute-start | bytes 3145736 | tf_op jit(solution)/shard_map/ppermute | solution.py:58
  565.9 28.3 %collective-permute-start.71 = (bf16[2,2,128,512]{3,2,0,1:T(8,128)(2,1)}, bf16[2,2,128,512]{3,2,0,1:T(8,128)(2,1)}, u32[]{:S(2)}, u32[]{:S(2)}) collective-permute-start(bf16[2,2,128,512]{3,2,0,1:T(8,128)(2,1)} %constant_dynamic-slice_fusion), channel_id=1, source_target_pairs={{0,16},{16,0},{1,17},{17,1},{2,18},{18,2},{3,19},{19,3},{4,20},{20... | collective-permute-start | bytes 1572872 | tf_op jit(solution)/shard_map/ppermute | solution.py:58
  567.0 28.0 %collective-permute-start.72 = (bf16[512,1024]{1,0:T(8,128)(2,1)}, bf16[512,1024]{1,0:T(8,128)(2,1)}, u32[]{:S(2)}, u32[]{:S(2)}) collective-permute-start(bf16[512,1024]{1,0:T(8,128)(2,1)} %slice.116), channel_id=1, source_target_pairs={{1,16},{3,18},{5,20},{7,22},{9,24},{11,26},{13,28},{15,30},{16,1},... | collective-permute-start | bytes 3145736 | tf_op jit(solution)/shard_map/ppermute | solution.py:78
  (116 other events, 1233.9 us)

commit v3 on v2

--- a/solution.py
+++ b/solution.py
@@ -629,7 +629,7 @@
 
 def outer(net, idx, g, xs, n, rows, first, into=None, choose=False):
     r, wide = g.shape
-    per = max(1, 512 // (2 * n))
+    per = max(1, 768 // (2 * n))
     while net.nf // 2 % per:
         per -= 1
     k = sum(x.shape[1] for x in xs) // (2 if choose else 1)

time: 641 us -> 640 us (level)
  waiting for transfers between devices: 109 us -> 99.9 us
  starting transfers between devices: 104 us -> 113 us
    all_to_all x1, starting transfers between devices: 7.28 us -> 17.2 us  [local(): mod = lax.all_to_all(part, 'fsdp', split_axis=0, concat_axis=2, tiled=True)]
    all_to_all x1, waiting for transfers between devices: 17.4 us -> 7.51 us  [local(): mod = lax.all_to_all(part, 'fsdp', split_axis=0, concat_axis=2, tiled=True)]
  transfers between devices with their start and end apart: 81 -> 81, of which waited for: 27 -> 29; matrix products, arithmetic and copies ran while one was open for 11% -> 11% of each run, Pallas kernels for 48% -> 47%
where the time goes in v3:
time: 640 us; the launch traced here: 630 us
  Pallas kernels  309 us (48%)
  starting transfers between devices  113 us (18%)
  waiting for transfers between devices  99.9 us (16%)
  other arithmetic  55.9 us (9%)
  local copies, waits for them, and re-layouts  48.9 us (8%)
    pallas_call x2, Pallas kernels, attn_bwd(): pl.pallas_call(partial(attn_bwd_kernel, na=na, long=long), grid_spec=pltp...  76.8 us
    ppermute x65, waiting for transfers between devices, swap(): return lax.ppermute(x, axis, [(i, i ^ mask) for i in range(size)])  76.7 us
    pallas_call x2, Pallas kernels, ffn(): pl.pallas_call(partial(ffn_kernel, steps=steps, second=second), grid=(ste...  71.4 us
    ppermute x65, starting transfers between devices, swap(): return lax.ppermute(x, axis, [(i, i ^ mask) for i in range(size)])  59.7 us
    pallas_call x1, Pallas kernels, attn_fwd(): pl.pallas_call(partial(attn_fwd_kernel, na=na, long=long), grid_spec=pltp...  34.6 us
    pallas_call x3, Pallas kernels, outer(): pl.pallas_call(partial(outer_kernel, n=n, own=len(xs), choose=choose), gr...  28.3 us
    convert_element_type x17, other arithmetic, plus(): return total.astype(bf16)  28.3 us
    unnamed x126, local copies, waits for them, and re-layouts  23.5 us
  transfers between devices with their start and end apart: 81, of which 29 were waited for; matrix products, arithmetic and copies ran while one was open for 11% of the time, Pallas kernels for 47%

profile of v3, /device:TPU:0, one launch (start us, length us, event | category | flops | bytes accessed | tf_op | source)
XLA Modules:
  0.0 629.7 jit_solution(5908973001936722932)
XLA Ops:
  31.9 7.3 %collective-permute-done.6 = bf16[1,256,512]{2,1,0:T(8,128)(2,1)S(1)} collective-permute-done((bf16[1,256,512]{2,1,0:T(8,128)(2,1)S(1)}, bf16[1,256,512]{2,1,0:T(8,128)(2,1)S(1)}, u32[]{:S(2)}, u32[]{:S(2)}) %collective-permute-start.6) | collective-permute-done | bytes 262176 | tf_op jit(solution)/shard_map/ppermute | solution.py:58
  83.4 6.6 %collective-permute-done.18.refs_1_ = bf16[128,512]{1,0:T(8,128)(2,1)S(1)} collective-permute-done((bf16[128,512]{1,0:T(8,128)(2,1)}, bf16[128,512]{1,0:T(8,128)(2,1)S(1)}, u32[]{:S(2)}, u32[]{:S(2)}) %collective-permute-start.18) | collective-permute-done | bytes 131104 | tf_op jit(solution)/shard_map/ppermute | solution.py:1136
  90.6 10.3 %skip_fwd.1 = (bf16[1024,1024]{1,0:T(8,128)(2,1)}, bf16[1024,1024]{1,0:T(8,128)(2,1)}) custom-call(s32[4]{0:T(128)} %copy-done.16, s32[2,8]{1,0:T(2,128)} %pad_add_fusion.4.lens, bf16[1024,1024]{1,0:T(8,128)(2,1)} %bitcast.146, bf16[1024,1024]{1,0:T(8,128)(2,1)} %bitcast.148, bf16[1024,1024]{1,0:T(8,128)(2,1)} %bitcast.147, bf16[1024,2048]{1,0:T(8,128)(2,1)} %copy-done.4), custom_call_target="tpu_custom_call" | custom-call | flops 4294967296 | bytes 14680064 | tf_op jit(solution)/shard_map/skip_fwd/pallas_call | solution.py:307
  109.2 17.2 %all-to-all-start.1 = ((f32[16,8,256]{2,1,0:T(8,128)}), f32[16,8,256]{2,1,0:T(8,128)S(1)}, u32[]{:S(2)}, u32[]{:S(2)}) async-start(f32[16,8,256]{2,1,0:T(8,128)} %bitcast.14), calls=%async_computation.1 | async-start | bytes 262144 | tf_op jit(solution)/shard_map/all_to_all | solution.py:1230
  127.0 7.5 %all-to-all-done.1 = f32[16,8,256]{2,1,0:T(8,128)S(1)} async-done(((f32[16,8,256]{2,1,0:T(8,128)}), f32[16,8,256]{2,1,0:T(8,128)S(1)}, u32[]{:S(2)}, u32[]{:S(2)}) %all-to-all-start.1) | async-done | bytes 131104 | tf_op jit(solution)/shard_map/all_to_all | solution.py:1230
  150.0 14.6 %qkv_fwd.1 = (bf16[1024,1024]{1,0:T(8,128)(2,1)}, bf16[1024,1024]{1,0:T(8,128)(2,1)}, bf16[3,1024,512]{2,1,0:T(8,128)(2,1)}, bf16[3,1024,512]{2,1,0:T(8,128)(2,1)}) custom-call(s32[3]{0:T(128)} %copy-done.15, bf16[1024,1024]{1,0:T(8,128)(2,1)} %get-tuple-element.299.hidden0, bf16[1024,1024]{1,0:T(8,128)(2,1)} %collective-permute-done.28.got, ...), custom_call_target="tpu_custom_call" | custom-call | flops 6442450944 | bytes 20971520 | tf_op jit(solution)/shard_map/qkv_fwd/pallas_call | solution.py:386
  164.6 7.2 %collective-permute-done.29 = bf16[2,256,1024]{2,1,0:T(8,128)(2,1)} collective-permute-done((bf16[2,256,1024]{2,1,0:T(8,128)(2,1)}, bf16[2,256,1024]{2,1,0:T(8,128)(2,1)}, u32[]{:S(2)}, u32[]{:S(2)}) %collective-permute-start.29) | collective-permute-done | bytes 1048608 | tf_op jit(solution)/shard_map/ppermute | solution.py:58
  185.3 34.6 %attn_fwd.1 = (bf16[1024,512]{1,0:T(8,128)(2,1)}, bf16[1024,512]{1,0:T(8,128)(2,1)}, f32[4,2,2048]{2,1,0:T(2,128)}) custom-call(s32[3]{0:T(128)} %copy-done.15, bf16[3,1024,512]{2,1,0:T(8,128)(2,1)} %get-tuple-element.315.refs_0_, bf16[3,1024,512]{2,1,0:T(8,128)(2,1)} %copy-done.54, s32[8,512]{1,0:T(8,128)} %copy-done.21, s32[512,128]{1,0:T(8,128)} %copy-done.20), custom_call_target="tpu_custom_call" | custom-call | flops 21474836480 | bytes 8388608 | tf_op jit(solution)/shard_map/attn_fwd/pallas_call | solution.py:838
  227.2 10.9 %out_fwd.1 = (bf16[1024,1024]{1,0:T(8,128)(2,1)}, f32[1024,1024]{1,0:T(8,128)}, bf16[1024,1024]{1,0:T(8,128)(2,1)}, bf16[1024,1024]{1,0:T(8,128)(2,1)}) custom-call(s32[3]{0:T(128)} %copy-done.15, bf16[1024,512]{1,0:T(8,128)(2,1)} %get-tuple-element.329.refs_0_, bf16[1024,512]{1,0:T(8,128)(2,1)} %copy-done.46, ...), custom_call_target="tpu_custom_call" | custom-call | flops 2147483648 | bytes 14680064 | tf_op jit(solution)/shard_map/out_fwd/pallas_call | solution.py:431
  238.2 34.7 %ffn.2 = (f32[1024,1024]{1,0:T(8,128)}, f32[1024,1024]{1,0:T(8,128)}, bf16[8,2,64,1024]{3,2,1,0:T(8,128)(2,1)}, bf16[8,2,64,1024]{3,2,1,0:T(8,128)(2,1)}, bf16[8...) custom-call(bf16[1024,1024]{1,0:T(8,128)(2,1)} %get-tuple-element.336.refs_0_, ...), custom_call_target="tpu_custom_call" | custom-call | flops 25769803776 | bytes 33554432 | tf_op jit(solution)/shard_map/ffn/pallas_call | solution.py:750
  286.5 36.7 %ffn.3 = (bf16[1024,1024]{1,0:T(8,128)(2,1)}, f32[1024,1024]{1,0:T(8,128)}, bf16[8,2,64,1024]{3,2,1,0:T(8,128)(2,1)}, bf16[8,2,64,1024]{3,2,1,0:T(8,128)(2,1)}, ...) custom-call(bf16[1024,1024]{1,0:T(8,128)(2,1)} %get-tuple-element.336.refs_0_, ...), custom_call_target="tpu_custom_call" | custom-call | flops 25769803776 | bytes 33554432 | tf_op jit(solution)/shard_map/ffn/pallas_call | solution.py:750
  325.9 13.0 %out_bwd.1 = (f32[1024,1024]{1,0:T(8,128)}, bf16[1024,1024]{1,0:T(8,128)(2,1)}, f32[8,2048]{1,0:T(8,128)}, bf16[1024,512]{1,0:T(8,128)(2,1)}, bf16[1024,512]{1,0:T(8,128)(2,1)}) custom-call(s32[3]{0:T(128)} %copy-done.15, f32[1024,1024]{1,0:T(8,128)} %get-tuple-element.369.grad, f32[1024,1024]{1,0:T(8,128)} %get-tuple-element.338.refs_2_.hidden2, ...), custom_call_target="tpu_custom_call" | custom-call | flops 2147483648 | bytes 23068672 | tf_op jit(solution)/shard_map/out_bwd/pallas_call | solution.py:498
  347.6 6.2 outer.3
  353.8 38.4 %attn_bwd.2 = (bf16[3,1024,256]{2,1,0:T(8,128)(2,1)}, bf16[3,1024,256]{2,1,0:T(8,128)(2,1)}) custom-call(s32[3]{0:T(128)} %copy-done.15, bf16[3,1024,512]{2,1,0:T(8,128)(2,1)} %get-tuple-element.315.refs_0_, bf16[3,1024,512]{2,1,0:T(8,128)(2,1)} %copy-done.54, bf16[1024,512]{1,0:T(8,128)(2,1)} %get-tuple-element.407.refs_2_, bf16[1024,512]{1,0:T(8,128)(2,1)} %copy-done.57, ...), custom_call_target="tpu_custom_call" | custom-call | flops 26843545600 | bytes 8388608 | tf_op jit(solution)/shard_map/attn_bwd/pallas_call | solution.py:926
  394.9 7.9 %add_convert_fusion.2 = (bf16[8,2,64,1024]{3,2,1,0:T(8,128)(2,1)S(1)}, bf16[8,2,64,1024]{3,2,1,0:T(8,128)(2,1)S(1)}) fusion(bf16[8,2,64,1024]{3,2,1,0:T(8,128)(2,1)} %collective-permute-done.50, bf16[8,2,64,1024]{3,2,1,0:T(8,128)(2,1)} %collective-permute-done.44, bf16[8,2,64,1024]{3,2,1,0:T(8,128)(2,1)} %get-tuple-element.403, ...), kind=kLoop, calls=%fused_computation.2 | loop fusion | flops 12582912 | bytes 16777216 | tf_op jit(solution)/shard_map/convert_element_type | solution.py:116
  407.7 38.3 %attn_bwd.3 = (bf16[3,1024,256]{2,1,0:T(8,128)(2,1)}, bf16[3,1024,256]{2,1,0:T(8,128)(2,1)}) custom-call(s32[3]{0:T(128)} %copy-done.15, bf16[3,1024,512]{2,1,0:T(8,128)(2,1)} %get-tuple-element.315.refs_0_, bf16[3,1024,512]{2,1,0:T(8,128)(2,1)} %copy-done.54, bf16[1024,512]{1,0:T(8,128)(2,1)} %get-tuple-element.407.refs_2_, bf16[1024,512]{1,0:T(8,128)(2,1)} %copy-done.57, ...), custom_call_target="tpu_custom_call" | custom-call | flops 26843545600 | bytes 8388608 | tf_op jit(solution)/shard_map/attn_bwd/pallas_call | solution.py:926
  455.5 9.0 %turn_back.1.d_qkv.g = bf16[1024,3072]{1,0:T(8,128)(2,1)} custom-call(s32[3]{0:T(128)} %copy-done.15, bf16[3,1024,256]{2,1,0:T(8,128)(2,1)} %get-tuple-element.421.refs_0_, bf16[3,1024,256]{2,1,0:T(8,128)(2,1)} %copy-done.36, bf16[3,1024,256]{2,1,0:T(8,128)(2,1)} %get-tuple-element.423.refs_2_, bf16[3,1024,256]{2,1,0:T(8,128)(2,1)} %collective-permute-done.54.refs_3_, ...), custom_call_target="tpu_custom_call" | custom-call | flops 12582912 | bytes 12582912 | tf_op jit(solution)/shard_map/turn_back/pallas_call | solution.py:538
  464.4 16.1 %qkv_bwd.1 = (bf16[1024,1024]{1,0:T(8,128)(2,1)}, f32[8,2048]{1,0:T(8,128)}) custom-call(bf16[1024,3072]{1,0:T(8,128)(2,1)} %turn_back.1.d_qkv.g, bf16[1024,1024]{1,0:T(8,128)(2,1)} %get-tuple-element.331.refs_2_.hidden, f32[1024,1024]{1,0:T(8,128)} %get-tuple-element.425.d_h2, bf16[1024,128]{1,0:T(8,128)(2,1)} %copy-done.6, ...), custom_call_target="tpu_custom_call" | custom-call | flops 6442450944 | bytes 23068672 | tf_op jit(solution)/shard_map/qkv_bwd/pallas_call | solution.py:577
  480.6 10.6 %outer.4 = (bf16[8,64,2048]{2,1,0:T(8,128)(2,1)}, bf16[8,64,2048]{2,1,0:T(8,128)(2,1)}) custom-call(s32[4]{0:T(128)} %copy-done.16, bf16[1024,1024]{1,0:T(8,128)(2,1)} %get-tuple-element.473.g.d_h, bf16[1024,1024]{1,0:T(8,128)(2,1)} %get-tuple-element.362.refs_0_, bf16[1024,1024]{1,0:T(8,128)(2,1)} %collective-permute-done.42.refs_1_, ...), custom_call_target="tpu_custom_call" | custom-call | flops 4294967296 | bytes 10485760 | tf_op jit(solution)/shard_map/outer/pallas_call | solution.py:639
  491.3 11.6 %outer.5 = (bf16[8,256,1024]{2,1,0:T(8,128)(2,1)}, bf16[8,256,1024]{2,1,0:T(8,128)(2,1)}) custom-call(s32[4]{0:T(128)} %copy-done.16, bf16[1024,3072]{1,0:T(8,128)(2,1)} %turn_back.1.d_qkv.g, bf16[1024,1024]{1,0:T(8,128)(2,1)} %get-tuple-element.437.refs_0_, ...), custom_call_target="tpu_custom_call", output_to_operand_aliasing={{0}: (3, {}), {1}: (4, {})} | custom-call | flops 6442450944 | bytes 14680064 | tf_op jit(solution)/shard_map/outer/pallas_call | solution.py:639
  573.3 6.8 %all-to-all-start.3 = ((f32[16,8,256]{2,1,0:T(8,128)}), f32[16,8,256]{2,1,0:T(8,128)S(1)}, u32[]{:S(2)}, u32[]{:S(2)}) async-start(f32[16,8,256]{2,1,0:T(8,128)} %bitcast.54), calls=%async_computation.3 | async-start | bytes 262144 | tf_op jit(solution)/shard_map/all_to_all | solution.py:1348
  585.3 7.3 %collective-permute-done.69 = bf16[64,1024]{1,0:T(8,128)(2,1)S(1)} collective-permute-done((bf16[64,1024]{1,0:T(8,128)(2,1)S(1)}, bf16[64,1024]{1,0:T(8,128)(2,1)S(1)}, u32[]{:S(2)}, u32[]{:S(2)}) %collective-permute-start.69) | collective-permute-done | bytes 131104 | tf_op jit(solution)/shard_map/ppermute | solution.py:58
  600.4 13.1 %collective-permute-done.76 = f32[128,256]{1,0:T(8,128)S(1)} collective-permute-done((f32[128,256]{1,0:T(8,128)S(1)}, f32[128,256]{1,0:T(8,128)S(1)}, u32[]{:S(2)}, u32[]{:S(2)}) %collective-permute-start.76) | collective-permute-done | bytes 131104 | tf_op jit(solution)/shard_map/ppermute | solution.py:58
  615.9 10.1 %skip_bwd.1 = (f32[1024,1024]{1,0:T(8,128)}, f32[1024,1024]{1,0:T(8,128)}) custom-call(s32[4]{0:T(128)} %copy-done.16, bf16[1024,1024]{1,0:T(8,128)(2,1)} %get-tuple-element.473.g.d_h, bf16[512,1024]{1,0:T(8,128)(2,1)} %collective-permute-done.72.got0, bf16[512,1024]{1,0:T(8,128)(2,1)} %copy-done.58, bf16[1024,2048]{1,0:T(8,128)(2,1)} %copy-done.4), custom_call_target="tpu_custom_call" | custom-call | flops 4294967296 | bytes 16777216 | tf_op jit(solution)/shard_map/skip_bwd/pallas_call | solution.py:600
  (385 shorter events, 251.6 us)
Async XLA Ops:
  69.8 31.0 %collective-permute-start.20 = (bf16[4,176,512]{2,1,0:T(8,128)(2,1)}, bf16[4,176,512]{2,1,0:T(8,128)(2,1)}, u32[]{:S(2)}, u32[]{:S(2)}) collective-permute-start(bf16[4,176,512]{2,1,0:T(8,128)(2,1)} %slice.123), channel_id=1, source_target_pairs={{0,16},{16,0},{1,17},{17,1},{2,18},{18,2},{3,19},{19,3},{4,20},{20... | collective-permute-start | bytes 2162696 | tf_op jit(solution)/shard_map/ppermute | solution.py:58
  73.3 27.6 %collective-permute-start.19 = (bf16[4,80,512]{2,1,0:T(8,128)(2,1)S(1)}, bf16[4,80,512]{2,1,0:T(8,128)(2,1)}, u32[]{:S(2)}, u32[]{:S(2)}) collective-permute-start(bf16[4,80,512]{2,1,0:T(8,128)(2,1)S(1)} %slice.122), channel_id=1, source_target_pairs={{0,2},{1,3},{2,0},{3,1},{4,6},{5,7},{6,4},{7,5},{8,10},{9,11},{10,... | collective-permute-start | bytes 983048 | tf_op jit(solution)/shard_map/ppermute | solution.py:58
  102.4 32.2 %collective-permute-start.22 = (bf16[8,176,512]{2,1,0:T(8,128)(2,1)S(1)}, bf16[8,176,512]{2,1,0:T(8,128)(2,1)}, u32[]{:S(2)}, u32[]{:S(2)}) collective-permute-start(bf16[8,176,512]{2,1,0:T(8,128)(2,1)S(1)} %pad_maximum_fusion.4.refs_1_), channel_id=1, source_target_pairs={{0,2},{1,3},{2,0},{3,1},{4,6},{5,7},{6,4},{7,5},{8,10},{9,11},{10,... | collective-permute-start | bytes 4325384 | tf_op jit(solution)/shard_map/ppermute | solution.py:58
  103.5 31.0 %collective-permute-start.21 = (bf16[8,80,512]{2,1,0:T(8,128)(2,1)S(1)}, bf16[8,80,512]{2,1,0:T(8,128)(2,1)S(1)}, u32[]{:S(2)}, u32[]{:S(2)}) collective-permute-start(bf16[8,80,512]{2,1,0:T(8,128)(2,1)S(1)} %pad_maximum_fusion.6.refs_0_), channel_id=1, source_target_pairs={{0,16},{16,0},{1,17},{17,1},{2,18},{18,2},{3,19},{19,3},{4,20},{20... | collective-permute-start | bytes 1966088 | tf_op jit(solution)/shard_map/ppermute | solution.py:58
  103.6 42.6 %collective-permute-start.28 = (bf16[1024,1024]{1,0:T(8,128)(2,1)}, bf16[1024,1024]{1,0:T(8,128)(2,1)}, u32[]{:S(2)}, u32[]{:S(2)}) collective-permute-start(bf16[1024,1024]{1,0:T(8,128)(2,1)} %get-tuple-element.299.hidden0), channel_id=1, source_target_pairs={{1,16},{3,18},{5,20},{7,22},{9,24},{11,26},{13,28},{15,30},{16,1},... | collective-permute-start | bytes 6291464 | tf_op jit(solution)/shard_map/ppermute | solution.py:78
  180.8 39.1 %collective-permute-start.32 = (bf16[512,1024]{1,0:T(8,128)(2,1)}, bf16[512,1024]{1,0:T(8,128)(2,1)}, u32[]{:S(2)}, u32[]{:S(2)}) collective-permute-start(bf16[512,1024]{1,0:T(8,128)(2,1)} %slice.97), channel_id=1, source_target_pairs={{1,16},{3,18},{5,20},{7,22},{9,24},{11,26},{13,28},{15,30},{16,1},... | collective-permute-start | bytes 3145736 | tf_op jit(solution)/shard_map/ppermute | solution.py:78
  182.4 37.5 %collective-permute-start.34 = (bf16[4,128,1024]{2,1,0:T(8,128)(2,1)S(1)}, bf16[4,128,1024]{2,1,0:T(8,128)(2,1)S(1)}, u32[]{:S(2)}, u32[]{:S(2)}) collective-permute-start(bf16[4,128,1024]{2,1,0:T(8,128)(2,1)S(1)} %get-tuple-element.518), channel_id=1, source_target_pairs={{0,16},{16,0},{1,17},{17,1},{2,18},{18,2},{3,19},{19,3},{4,20},{20... | collective-permute-start | bytes 3145736 | tf_op jit(solution)/shard_map/ppermute | solution.py:58
  184.5 35.4 %collective-permute-start.33 = (bf16[4,128,1024]{2,1,0:T(8,128)(2,1)}, bf16[4,128,1024]{2,1,0:T(8,128)(2,1)S(1)}, u32[]{:S(2)}, u32[]{:S(2)}) collective-permute-start(bf16[4,128,1024]{2,1,0:T(8,128)(2,1)} %get-tuple-element.519), channel_id=1, source_target_pairs={{0,2},{1,3},{2,0},{3,1},{4,6},{5,7},{6,4},{7,5},{8,10},{9,11},{10,... | collective-permute-start | bytes 3145736 | tf_op jit(solution)/shard_map/ppermute | solution.py:58
  225.4 48.3 %collective-permute-start.39 = (bf16[8,128,1024]{2,1,0:T(8,128)(2,1)}, bf16[8,128,1024]{2,1,0:T(8,128)(2,1)}, u32[]{:S(2)}, u32[]{:S(2)}) collective-permute-start(bf16[8,128,1024]{2,1,0:T(8,128)(2,1)} %pad_maximum_fusion.2), channel_id=1, source_target_pairs={{0,2},{1,3},{2,0},{3,1},{4,6},{5,7},{6,4},{7,5},{8,10},{9,11},{10,... | collective-permute-start | bytes 6291464 | tf_op jit(solution)/shard_map/ppermute | solution.py:58
  226.8 47.8 %collective-permute-start.38 = (bf16[8,128,1024]{2,1,0:T(8,128)(2,1)S(1)}, bf16[8,128,1024]{2,1,0:T(8,128)(2,1)}, u32[]{:S(2)}, u32[]{:S(2)}) collective-permute-start(bf16[8,128,1024]{2,1,0:T(8,128)(2,1)S(1)} %pad_maximum_fusion.1), channel_id=1, source_target_pairs={{0,16},{16,0},{1,17},{17,1},{2,18},{18,2},{3,19},{19,3},{4,20},{20... | collective-permute-start | bytes 6291464 | tf_op jit(solution)/shard_map/ppermute | solution.py:58
  282.0 41.2 %collective-permute-start.43 = (bf16[8,2,64,1024]{3,2,1,0:T(8,128)(2,1)}, bf16[8,2,64,1024]{3,2,1,0:T(8,128)(2,1)S(1)}, u32[]{:S(2)}, u32[]{:S(2)}) collective-permute-start(bf16[8,2,64,1024]{3,2,1,0:T(8,128)(2,1)} %get-tuple-element.367), channel_id=1, source_target_pairs={{0,1},{1,0},{2,3},{3,2},{4,5},{5,4},{6,7},{7,6},{8,9},{9,8},{10,11... | collective-permute-start | bytes 6291464 | tf_op jit(solution)/shard_map/ppermute | solution.py:58
  282.1 41.1 %collective-permute-start.44 = (bf16[8,2,64,1024]{3,2,1,0:T(8,128)(2,1)}, bf16[8,2,64,1024]{3,2,1,0:T(8,128)(2,1)}, u32[]{:S(2)}, u32[]{:S(2)}) collective-permute-start(bf16[8,2,64,1024]{3,2,1,0:T(8,128)(2,1)} %get-tuple-element.368), channel_id=1, source_target_pairs={{0,1},{1,0},{2,3},{3,2},{4,5},{5,4},{6,7},{7,6},{8,9},{9,8},{10,11... | collective-permute-start | bytes 6291464 | tf_op jit(solution)/shard_map/ppermute | solution.py:58
  282.5 40.8 %collective-permute-start.42 = (bf16[1024,1024]{1,0:T(8,128)(2,1)}, bf16[1024,1024]{1,0:T(8,128)(2,1)}, u32[]{:S(2)}, u32[]{:S(2)}) collective-permute-start(bf16[1024,1024]{1,0:T(8,128)(2,1)} %get-tuple-element.362.refs_0_), channel_id=1, source_target_pairs={{1,16},{3,18},{5,20},{7,22},{9,24},{11,26},{13,28},{15,30},{16,1},... | collective-permute-start | bytes 6291464 | tf_op jit(solution)/shard_map/ppermute | solution.py:78
  284.4 54.5 %collective-permute-start.45 = (bf16[1024,1024]{1,0:T(8,128)(2,1)}, bf16[1024,1024]{1,0:T(8,128)(2,1)}, u32[]{:S(2)}, u32[]{:S(2)}) collective-permute-start(bf16[1024,1024]{1,0:T(8,128)(2,1)} %bitcast.149), channel_id=1, source_target_pairs={{1,16},{3,18},{5,20},{7,22},{9,24},{11,26},{13,28},{15,30},{16,1},... | collective-permute-start | bytes 6291464 | tf_op jit(solution)/shard_map/ppermute | solution.py:78
  346.7 47.9 %collective-permute-start.49 = (bf16[8,2,64,1024]{3,2,1,0:T(8,128)(2,1)S(1)}, bf16[8,2,64,1024]{3,2,1,0:T(8,128)(2,1)}, u32[]{:S(2)}, u32[]{:S(2)}) collective-permute-start(bf16[8,2,64,1024]{3,2,1,0:T(8,128)(2,1)S(1)} %add_convert_fusion.5), channel_id=1, source_target_pairs={{0,16},{16,0},{1,17},{17,1},{2,18},{18,2},{3,19},{19,3},{4,20},{20... | collective-permute-start | bytes 6291464 | tf_op jit(solution)/shard_map/ppermute | solution.py:58
  347.0 47.9 %collective-permute-start.50 = (bf16[8,2,64,1024]{3,2,1,0:T(8,128)(2,1)}, bf16[8,2,64,1024]{3,2,1,0:T(8,128)(2,1)}, u32[]{:S(2)}, u32[]{:S(2)}) collective-permute-start(bf16[8,2,64,1024]{3,2,1,0:T(8,128)(2,1)} %add_convert_fusion.4), channel_id=1, source_target_pairs={{0,2},{1,3},{2,0},{3,1},{4,6},{5,7},{6,4},{7,5},{8,10},{9,11},{10,... | collective-permute-start | bytes 6291464 | tf_op jit(solution)/shard_map/ppermute | solution.py:58
  405.6 40.5 %collective-permute-start.52 = (bf16[4,2,64,1024]{3,2,1,0:T(8,128)(2,1)}, bf16[4,2,64,1024]{3,2,1,0:T(8,128)(2,1)}, u32[]{:S(2)}, u32[]{:S(2)}) collective-permute-start(bf16[4,2,64,1024]{3,2,1,0:T(8,128)(2,1)} %slice.102), channel_id=1, source_target_pairs={{0,16},{16,0},{1,17},{17,1},{2,18},{18,2},{3,19},{19,3},{4,20},{20... | collective-permute-start | bytes 3145736 | tf_op jit(solution)/shard_map/ppermute | solution.py:58
  407.1 38.9 %collective-permute-start.51 = (bf16[4,2,64,1024]{3,2,1,0:T(8,128)(2,1)}, bf16[4,2,64,1024]{3,2,1,0:T(8,128)(2,1)}, u32[]{:S(2)}, u32[]{:S(2)}) collective-permute-start(bf16[4,2,64,1024]{3,2,1,0:T(8,128)(2,1)} %slice.101), channel_id=1, source_target_pairs={{0,2},{1,3},{2,0},{3,1},{4,6},{5,7},{6,4},{7,5},{8,10},{9,11},{10,... | collective-permute-start | bytes 3145736 | tf_op jit(solution)/shard_map/ppermute | solution.py:58
  407.7 38.4 %collective-permute-start.53 = (bf16[3,1024,256]{2,1,0:T(8,128)(2,1)}, bf16[3,1024,256]{2,1,0:T(8,128)(2,1)S(1)}, u32[]{:S(2)}, u32[]{:S(2)}) collective-permute-start(bf16[3,1024,256]{2,1,0:T(8,128)(2,1)} %get-tuple-element.414), channel_id=1, source_target_pairs={{0,1},{1,0},{2,3},{3,2},{4,5},{5,4},{6,7},{7,6},{8,9},{9,8},{10,11... | collective-permute-start | bytes 4718600 | tf_op jit(solution)/shard_map/ppermute | solution.py:58
  446.6 33.9 %collective-permute-start.55 = (bf16[1024,1024]{1,0:T(8,128)(2,1)}, bf16[1024,1024]{1,0:T(8,128)(2,1)}, u32[]{:S(2)}, u32[]{:S(2)}) collective-permute-start(bf16[1024,1024]{1,0:T(8,128)(2,1)} %get-tuple-element.463), channel_id=1, source_target_pairs={{1,16},{3,18},{5,20},{7,22},{9,24},{11,26},{13,28},{15,30},{16,1},... | collective-permute-start | bytes 6291464 | tf_op jit(solution)/shard_map/ppermute | solution.py:78
  526.7 35.2 %collective-permute-start.66 = (bf16[2,2,128,1024]{3,2,0,1:T(8,128)(2,1)}, bf16[2,2,128,1024]{3,2,0,1:T(8,128)(2,1)}, u32[]{:S(2)}, u32[]{:S(2)}) collective-permute-start(bf16[2,2,128,1024]{3,2,0,1:T(8,128)(2,1)} %dynamic-slice_bitcast_fusion), channel_id=1, source_target_pairs={{0,2},{1,3},{2,0},{3,1},{4,6},{5,7},{6,4},{7,5},{8,10},{9,11},{10,... | collective-permute-start | bytes 3145736 | tf_op jit(solution)/shard_map/ppermute | solution.py:58
  528.8 33.1 %collective-permute-start.65 = (bf16[2,2,2,128,512]{4,3,0,1,2:T(8,128)(2,1)}, bf16[2,2,2,128,512]{4,3,0,1,2:T(8,128)(2,1)}, u32[]{:S(2)}, u32[]{:S(2)}) collective-permute-start(bf16[2,2,2,128,512]{4,3,0,1,2:T(8,128)(2,1)} %constant_dynamic-slice_fusion.3), channel_id=1, source_target_pairs={{0,16},{16,0},{1,17},{17,1},{2,18},{18,2},{3,19},{19,3},{4,20},{20... | collective-permute-start | bytes 3145736 | tf_op jit(solution)/shard_map/ppermute | solution.py:58
  564.9 27.7 %collective-permute-start.71 = (bf16[2,2,128,512]{3,2,0,1:T(8,128)(2,1)}, bf16[2,2,128,512]{3,2,0,1:T(8,128)(2,1)}, u32[]{:S(2)}, u32[]{:S(2)}) collective-permute-start(bf16[2,2,128,512]{3,2,0,1:T(8,128)(2,1)} %constant_dynamic-slice_fusion), channel_id=1, source_target_pairs={{0,16},{16,0},{1,17},{17,1},{2,18},{18,2},{3,19},{19,3},{4,20},{20... | collective-permute-start | bytes 1572872 | tf_op jit(solution)/shard_map/ppermute | solution.py:58
  565.9 27.4 %collective-permute-start.72 = (bf16[512,1024]{1,0:T(8,128)(2,1)}, bf16[512,1024]{1,0:T(8,128)(2,1)}, u32[]{:S(2)}, u32[]{:S(2)}) collective-permute-start(bf16[512,1024]{1,0:T(8,128)(2,1)} %slice.116), channel_id=1, source_target_pairs={{1,16},{3,18},{5,20},{7,22},{9,24},{11,26},{13,28},{15,30},{16,1},... | collective-permute-start | bytes 3145736 | tf_op jit(solution)/shard_map/ppermute | solution.py:78
  (116 other events, 1223.5 us)
